TPU v7x, 128 devices: a whole 4x4x4 slice. The times are simulated.
128 devices in a mesh: section: 8 (over z, x_lo), ctx: 16 (over y, x_hi, core).
Axes of the slice: x: 4 (x_hi: 2, x_lo: 2; x = x_hi * 2 + x_lo), y: 4, z: 4, core: 2. Of those that a mesh axis runs over, the one named last changes fastest.
Arguments:
- queries: bfloat16 [2, 8, 2048, 4096], P(None, 'section', 'ctx'), may hold values from -12 to 12
- keys: bfloat16 [2, 8, 2048, 512], P(None, 'section', 'ctx'), may hold values from -16 to 16
- values: bfloat16 [2, 8, 2048, 512], P(None, 'section', 'ctx'), may hold values from -4 to 4
- output_gradient: bfloat16 [2, 8, 2048, 4096], P(None, 'section', 'ctx'), may hold values from -12 to 12
- doc_tiles: int32 [2, 8, 4], P(None, 'section'), may hold values from 1 to 9, 16 in all within a row
- sink_logits: float32 [8, 32], replicated, may hold values from -1 to 3
Outputs:
- attention: bfloat16 [2, 8, 2048, 4096], P(None, 'section', 'ctx')
- query_grad: bfloat16 [2, 8, 2048, 4096], P(None, 'section', 'ctx')
- key_gradient: bfloat16 [2, 8, 2048, 512], P(None, 'section', 'ctx')
- value_gradient: bfloat16 [2, 8, 2048, 512], P(None, 'section', 'ctx')
- sink_grad: float32 [8, 32], P('section')
Inputs may be any that keep to these rules, and one draw needn't show every extreme that they name: `doc_tiles`: the 4 lengths of each micro-batch sum to 16.
All inputs are finite; a program needn't handle non-finite values.
Results may differ from a plain program's by a relative error of at most 0.015.
Values may be sent and summed in bfloat16 or wider, within the bound.
No kernel may reach another device: no remote copies, remote signals or barrier semaphores. Data moves between devices by JAX's collectives and lax.ppermute only.
A program may use at most 128 MiB of HBM per device.

v0:
```python
import math

import jax
import jax.numpy as jnp
from jax import lax
from jax.sharding import PartitionSpec as P

HEAD_WIDTH = 128
HQ = 32
KEY_HEADS = 4
QUERY_PER_KV = 8
TILE = 128
RELAY_COUNT = 2


def swapped(block, axis, distance):
    count = lax.axis_size(axis)
    route = []
    for low in range(count):
        high = low | 1 << distance
        if high != low and high < count:
            route += [(low, high), (high, low)]
    return lax.ppermute(block, axis, route)


def document_of(positions, ends):
    tiles = positions // TILE
    return jnp.sum((tiles[:, None] >= ends[None, :]).astype(jnp.int32), axis=1)


def attend(
    query_block, key_row_view, value_row_view, grad_block, sink_logit, query_pos, ends, key_root=0
):
    query_count, heads_kv, group_size, head_size = query_block.shape
    key_count = key_row_view.shape[0]
    block_size = math.gcd(key_count, 512)
    block_count = key_count // block_size
    scale = 1.0 / math.sqrt(head_size)
    query_doc = document_of(query_pos, ends)

    def pieces(index):
        start = index * block_size
        key_pos = key_root + start + jnp.arange(block_size, dtype=jnp.int32)
        key_doc = document_of(key_pos, ends)
        visible = (key_doc[None, :] == query_doc[:, None]) & (
            key_pos[None, :] <= query_pos[:, None]
        )
        visible = visible & (key_pos[None, :] >= 0)
        key_block = lax.dynamic_slice_in_dim(key_row_view, start, block_size, 0)
        value_block = lax.dynamic_slice_in_dim(value_row_view, start, block_size, 0)
        return (start, visible, key_block, value_block)

    def scores_of(key_block):
        return (
            jnp.einsum("qhgd,khd->hgqk", query_block, key_block, preferred_element_type=jnp.float32)
            * scale
        )

    def first_pass(index, carry):
        start, visible, key_block, value_block = pieces(index)

        def first_update(state):
            highest, exp_total = state
            masked = jnp.where(visible, scores_of(key_block), -jnp.inf)
            new_highest = jnp.maximum(highest, jnp.max(masked, axis=-1))
            exp_total = exp_total * jnp.exp(highest - new_highest) + jnp.sum(
                jnp.exp(masked - new_highest[..., None]), axis=-1
            )
            return (new_highest, exp_total)

        return lax.cond(jnp.any(visible), first_update, lambda state: state, carry)

    start_high = jnp.broadcast_to(sink_logit[:, :, None], (heads_kv, group_size, query_count))
    highest, exp_total = lax.fori_loop(
        0, block_count, first_pass, (start_high, jnp.ones_like(start_high))
    )
    log_total = highest + jnp.log(exp_total)

    def shares_of(visible, key_block):
        return jnp.where(visible, jnp.exp(scores_of(key_block) - log_total[..., None]), 0.0)

    def second_pass(index, carry):
        start, visible, key_block, value_block = pieces(index)

        def second_update(output_acc):
            shares_low = shares_of(visible, key_block).astype(jnp.bfloat16)
            return output_acc + jnp.einsum(
                "hgqk,khd->hgqd", shares_low, value_block, preferred_element_type=jnp.float32
            )

        return lax.cond(jnp.any(visible), second_update, lambda output_acc: output_acc, carry)

    output_zero = jnp.zeros((heads_kv, group_size, query_count, head_size), jnp.float32)
    heads = lax.fori_loop(0, block_count, second_pass, output_zero).astype(jnp.bfloat16)
    heads_kept = lax.optimization_barrier(heads)
    gradient_heads = jnp.transpose(grad_block, (1, 2, 0, 3))
    row_delta = jnp.sum(
        gradient_heads.astype(jnp.float32) * heads_kept.astype(jnp.float32), axis=-1
    )

    def third_pass(index, carry):
        start, visible, key_block, value_block = pieces(index)

        def third_update(state):
            query_acc, key_running_sum, value_running_sum = state
            shares = shares_of(visible, key_block)
            shares_low = shares.astype(jnp.bfloat16)
            share_grads = jnp.einsum(
                "qhgd,khd->hgqk", grad_block, value_block, preferred_element_type=jnp.float32
            )
            score_grads = (shares * (share_grads - row_delta[..., None])).astype(jnp.bfloat16)
            query_acc = query_acc + jnp.einsum(
                "hgqk,khd->hgqd", score_grads, key_block, preferred_element_type=jnp.float32
            )
            key_part = (
                jnp.einsum(
                    "hgqk,qhgd->khd", score_grads, query_block, preferred_element_type=jnp.float32
                )
                * scale
            )
            value_part = jnp.einsum(
                "hgqk,qhgd->khd", shares_low, grad_block, preferred_element_type=jnp.float32
            )
            key_running_sum = lax.dynamic_update_slice_in_dim(
                key_running_sum,
                lax.dynamic_slice_in_dim(key_running_sum, start, block_size, 0) + key_part,
                start,
                0,
            )
            value_running_sum = lax.dynamic_update_slice_in_dim(
                value_running_sum,
                lax.dynamic_slice_in_dim(value_running_sum, start, block_size, 0) + value_part,
                start,
                0,
            )
            return (query_acc, key_running_sum, value_running_sum)

        return lax.cond(jnp.any(visible), third_update, lambda state: state, carry)

    key_zero = jnp.zeros((key_count, heads_kv, head_size), jnp.float32)
    query_acc, key_running_sum, value_running_sum = lax.fori_loop(
        0, block_count, third_pass, (output_zero, key_zero, key_zero)
    )
    sink_part = -jnp.sum(jnp.exp(sink_logit[:, :, None] - log_total) * row_delta, axis=-1)
    return (heads, query_acc * scale, key_running_sum, value_running_sum, sink_part)


def shards(queries, keys, values, output_gradient, doc_tiles, sink_logits):
    row_entries = queries.shape[2]
    ctx_count = lax.axis_size("ctx")
    ctx_pos = lax.axis_index("ctx")
    sequence_tokens = row_entries * ctx_count
    section_pos = lax.axis_index("section")
    section_count = lax.axis_size("section")
    down_sink = lax.dynamic_index_in_dim(sink_logits, section_pos, 0, keepdims=False)
    up_sink = lax.dynamic_index_in_dim(
        sink_logits, section_count - 1 - section_pos, 0, keepdims=False
    )
    sink_couple = jnp.stack([down_sink, up_sink])
    ends_pair = jnp.cumsum(doc_tiles[:, 0], axis=-1)
    every_key, every_value = (
        lax.all_gather(keys, "ctx", axis=2, tiled=True),
        lax.all_gather(values, "ctx", axis=2, tiled=True),
    )
    query_pos = ctx_pos * row_entries + jnp.arange(row_entries, dtype=jnp.int32)
    outputs, query_grads, key_partial_terms, value_partial_terms, sink_parts = ([], [], [], [], [])
    for relay_index in range(RELAY_COUNT):
        heads, query_acc, key_running_sum, value_running_sum, sink_part = attend(
            queries[relay_index, 0].reshape(row_entries, KEY_HEADS, QUERY_PER_KV, HEAD_WIDTH),
            every_key[relay_index, 0].reshape(sequence_tokens, KEY_HEADS, HEAD_WIDTH),
            every_value[relay_index, 0].reshape(sequence_tokens, KEY_HEADS, HEAD_WIDTH),
            output_gradient[relay_index, 0].reshape(
                row_entries, KEY_HEADS, QUERY_PER_KV, HEAD_WIDTH
            ),
            sink_couple[relay_index].reshape(KEY_HEADS, QUERY_PER_KV),
            query_pos,
            ends_pair[relay_index],
        )
        outputs.append(jnp.transpose(heads, (2, 0, 1, 3)).reshape(row_entries, HQ * HEAD_WIDTH))
        query_grads.append(
            jnp.transpose(query_acc, (2, 0, 1, 3))
            .reshape(row_entries, HQ * HEAD_WIDTH)
            .astype(jnp.bfloat16)
        )
        key_partial_terms.append(key_running_sum.reshape(sequence_tokens, KEY_HEADS * HEAD_WIDTH))
        value_partial_terms.append(
            value_running_sum.reshape(sequence_tokens, KEY_HEADS * HEAD_WIDTH)
        )
        sink_parts.append(sink_part.reshape(HQ))
    key_sums, value_sums = (
        lax.psum_scatter(
            jnp.stack(key_partial_terms).astype(jnp.bfloat16),
            "ctx",
            scatter_dimension=1,
            tiled=True,
        ).astype(jnp.float32),
        lax.psum_scatter(
            jnp.stack(value_partial_terms).astype(jnp.bfloat16),
            "ctx",
            scatter_dimension=1,
            tiled=True,
        ).astype(jnp.float32),
    )
    attention = jnp.stack(outputs)[:, None]
    query_grad = jnp.stack(query_grads)[:, None]
    key_gradient = key_sums.astype(jnp.bfloat16)[:, None]
    value_gradient = value_sums.astype(jnp.bfloat16)[:, None]
    sink_local = jnp.stack(sink_parts)
    sink_total = lax.psum(sink_local, "ctx")
    mirrored = sink_total[1]
    for bit in range(section_count.bit_length() - 1):
        mirrored = swapped(mirrored, "section", bit)
    sink_grad = (sink_total[0] + mirrored)[None]
    return (attention, query_grad, key_gradient, value_gradient, sink_grad)


def solution(mesh):
    placed = (
        P(None, "section", "ctx", None),
        P(None, "section", "ctx", None),
        P(None, "section", "ctx", None),
        P(None, "section", "ctx", None),
        P(None, "section", None),
        P(),
    )
    return jax.shard_map(
        shards,
        mesh=mesh,
        in_specs=placed,
        out_specs=(
            P(None, "section", "ctx", None),
            P(None, "section", "ctx", None),
            P(None, "section", "ctx", None),
            P(None, "section", "ctx", None),
            P("section", None),
        ),
        check_vma=False,
    )
```

profile of v0, /device:TPU:1, one launch (start us, length us, event | category | flops | bytes accessed | tf_op | source)
XLA Modules:
  0.0 560.7 jit_solution(18069623506363828621)
XLA Ops:
  12.7 2.7 fusion.174
  16.7 2.8 fusion.173
  23.9 2.7 copy.87
  28.0 43.2 %all-gather.3.cloned.1.call-done = bf16[2,1,2048,512]{2,3,1,0:T(8,128)(2,1)} async-done(((bf16[2,1,128,512]{2,3,1,0:T(8,128)(2,1)}), bf16[2,1,2048,512]{2,3,1,0:T(8,128)(2,1)}) %all-gather.3.cloned.1.call-update) | async-done | bytes 4194320 | tf_op jit(solution)/shard_map/all_gather | solution.py:162
  71.2 4.8 fusion.172
  76.0 4.0 copy.70
  80.0 11.0 %while.114 = (s32[]{:T(128)}, f32[4,8,128]{2,1,0:T(8,128)S(1)}, f32[4,8,128]{2,1,0:T(8,128)S(1)}, s32[1,4]{1,0:T(1,128)S(1)}, s32[128]{0:T(128)S(1)}, /*index=5*...) while((s32[]{:T(128)}, f32[4,8,128]{2,1,0:T(8,128)S(1)}, ...), condition=%wide.region_9.10_spmd.clone, body=%wide.region_2.9_spmd.clone.sunk | while | flops 551901824 | bytes 18774800 | solution.py:74
  81.7 4.2 conditional.18
  81.7 2.3 fusion.12
  91.0 37.5 %all-gather.5.cloned.1.call-done = bf16[2,1,2048,512]{2,3,1,0:T(8,128)(2,1)} async-done(((bf16[2,1,128,512]{2,3,1,0:T(8,128)(2,1)}), bf16[2,1,2048,512]{2,3,1,0:T(8,128)(2,1)}) %all-gather.5.cloned.1.call-update) | async-done | bytes 4194320 | tf_op jit(solution)/shard_map/all_gather | solution.py:163
  128.6 4.9 fusion.171
  133.4 4.0 copy.72
  139.0 13.0 %while.115 = (s32[]{:T(128)}, f32[4,8,128,128]{3,2,1,0:T(8,128)}, s32[1,4]{1,0:T(1,128)S(1)}, s32[128]{0:T(128)S(1)}, bf16[2048,4,128]{2,0,1:T(8,128)(2,1)}, /*i...) while((s32[]{:T(128)}, f32[4,8,128,128]{3,2,1,0:T(8,128)}, ...), condition=%wide.region_15.16_spmd.clone, body=%wide.region_10.15_spmd.clone.sunk | while | flops 1082997376 | bytes 6455037 | solution.py:94
  140.6 6.3 %conditional.19 = (f32[4,8,128,128]{3,2,1,0:T(8,128)}) conditional(s32[]{:T(128)} %convert_element_type.313, f32[4,8,128,128]{3,2,1,0:T(8,128)} %get-tuple-element.3110, (pred[128,512]{0,1:T(8,128)(4,1)S(1)}, s32[]{:T(128)}, bf16[2048,4,128]{2,0,1:T(8,128)(2,1)}, bf16[128,4,8,128]{3,0,2,1:T(8,128)(2,1)S(1)}, f32[4,8,128]{2,1,0:T(8,128)S(1)}, ...), branch_computations={%region_13.13_spmd, %region_14.14_spmd} | conditional | flops 1082654720 | bytes 6374442 | solution.py:91
  140.7 6.2 %fusion.28 = f32[4,8,128,128]{3,2,1,0:T(8,128)} fusion(f32[4,8,128,128]{3,2,1,0:T(8,128)} %get-tuple-element.1963, f32[4,8,128]{2,1,0:T(8,128)S(1)} %get-tuple-element.1968, pred[128,512]{0,1:T(8,128)(4,1)S(1)} %get-tuple-element.1964, bf16[128,4,8,128]{3,0,2,1:T(8,128)(2,1)S(1)} %get-tuple-element.1967, bf16[2048,4,128]{2,0,1:T(8,128)(2,1)} %get-tuple-element.1969, ...), kind=kOutput, calls=%fused_computation.24 | convolution fusion | flops 1082654720 | bytes 6374400 | tf_op jit(solution)/shard_map/while/body/eval_jaxpr/cond/branch_1_fun/hgqk,khd->hgqd/dot_general | solution.py:87
  153.9 2.0 fusion.161
  155.9 4.0 copy.77
  159.9 11.2 %while.116 = (s32[]{:T(128)}, f32[4,8,128]{2,1,0:T(8,128)S(1)}, f32[4,8,128]{2,1,0:T(8,128)S(1)}, s32[1,4]{1,0:T(1,128)S(1)}, s32[128]{0:T(128)S(1)}, /*index=5*...) while((s32[]{:T(128)}, f32[4,8,128]{2,1,0:T(8,128)S(1)}, ...), condition=%wide.region_24.25_spmd.clone, body=%wide.region_17.24_spmd.clone.sunk | while | flops 551901824 | bytes 18774800 | solution.py:74
  161.8 4.1 conditional.20
  161.8 2.3 fusion.41
  171.1 3.9 copy.79
  176.6 13.0 %while.117 = (s32[]{:T(128)}, f32[4,8,128,128]{3,2,1,0:T(8,128)}, s32[1,4]{1,0:T(1,128)S(1)}, s32[128]{0:T(128)S(1)}, bf16[2048,4,128]{2,0,1:T(8,128)(2,1)}, /*i...) while((s32[]{:T(128)}, f32[4,8,128,128]{3,2,1,0:T(8,128)}, ...), condition=%wide.region_30.31_spmd.clone, body=%wide.region_25.30_spmd.clone.sunk | while | flops 1082997376 | bytes 6455037 | solution.py:94
  178.3 6.3 %conditional.21 = (f32[4,8,128,128]{3,2,1,0:T(8,128)}) conditional(s32[]{:T(128)} %convert_element_type.317, f32[4,8,128,128]{3,2,1,0:T(8,128)} %get-tuple-element.3047, (pred[128,512]{0,1:T(8,128)(4,1)S(1)}, s32[]{:T(128)}, bf16[2048,4,128]{2,0,1:T(8,128)(2,1)}, bf16[128,4,8,128]{3,0,2,1:T(8,128)(2,1)S(1)}, f32[4,8,128]{2,1,0:T(8,128)S(1)}, ...), branch_computations={%region_28.28_spmd, %region_29.29_spmd} | conditional | flops 1082654720 | bytes 6374442 | solution.py:91
  178.3 6.2 %fusion.57 = f32[4,8,128,128]{3,2,1,0:T(8,128)} fusion(f32[4,8,128,128]{3,2,1,0:T(8,128)} %get-tuple-element.1997, f32[4,8,128]{2,1,0:T(8,128)S(1)} %get-tuple-element.2002, pred[128,512]{0,1:T(8,128)(4,1)S(1)} %get-tuple-element.1998, bf16[128,4,8,128]{3,0,2,1:T(8,128)(2,1)S(1)} %get-tuple-element.2001, bf16[2048,4,128]{2,0,1:T(8,128)(2,1)} %get-tuple-element.2003, ...), kind=kOutput, calls=%fused_computation.50 | convolution fusion | flops 1082654720 | bytes 6374400 | tf_op jit(solution)/shard_map/while/body/eval_jaxpr/cond/branch_1_fun/hgqk,khd->hgqd/dot_general | solution.py:87
  191.5 2.0 fusion.160
  193.5 2.2 broadcast.773.clone.2
  195.7 2.2 broadcast.773.clone.3
  199.5 25.4 %while.118 = (s32[]{:T(128)}, f32[4,8,128,128]{3,2,1,0:T(8,128)}, f32[2048,4,128]{2,0,1:T(8,128)}, f32[2048,4,128]{2,0,1:T(8,128)}, s32[1,4]{1,0:T(1,128)S(1)}, ...) while((s32[]{:T(128)}, f32[4,8,128,128]{3,2,1,0:T(8,128)}, ...), condition=%wide.region_37.38_spmd.clone, body=%wide.region_32.37_spmd.clone.sunk | while | flops 2706979584 | bytes 106691584 | solution.py:141
  201.4 18.3 %conditional.22 = ((f32[4,8,128,128]{3,2,1,0:T(8,128)}, f32[2048,4,128]{2,0,1:T(8,128)}, f32[2048,4,128]{2,0,1:T(8,128)})) conditional(s32[]{:T(128)} %convert_element_type.319, (f32[4,8,128,128]{3,2,1,0:T(8,128)}, f32[2048,4,128]{2,0,1:T(8,128)}, f32[2048,4,128]{2,0,1:T(8,128)}) %tuple.398, (pred[128,512]{0,1:T(8,128)(4,1)S(1)}, s32[]{:T(128)}, ...), branch_computations={%region_35.35_spmd, %region_36.36_spmd} | conditional | flops 2706636800 | bytes 106610904 | solution.py:138
  201.5 2.4 fusion.93
  203.9 3.8 fusion.71
  207.7 3.6 fusion.84
  211.3 3.6 convolution_add_fusion
  217.8 1.9 copy-done.5
  224.9 2.5 convert.20
  227.4 10.2 %copy.97 = bf16[2048,4,128]{2,1,0:T(4,128)(2,1)S(1)} copy(bf16[2048,4,128]{2,0,1:T(8,128)(2,1)S(1)} %convert.20) | data formatting | bytes 4194304 | tf_op jit(solution)/shard_map/convert.5
  237.6 2.2 stack_reshape.28
  239.8 2.2 broadcast.773.clone
  242.1 2.2 broadcast.773.clone.1
  244.5 23.9 %while.119 = (s32[]{:T(128)}, f32[4,8,128,128]{3,2,1,0:T(8,128)S(1)}, f32[2048,4,128]{2,0,1:T(8,128)}, f32[2048,4,128]{2,0,1:T(8,128)}, s32[1,4]{1,0:T(1,128)S(1...) while((s32[]{:T(128)}, ...), condition=%wide.region_44.45_spmd.clone, body=%wide.region_39.44_spmd.clone.sunk | while | flops 2706979584 | bytes 89914320 | solution.py:141
  246.3 16.9 %conditional.23 = ((f32[4,8,128,128]{3,2,1,0:T(8,128)S(1)}, f32[2048,4,128]{2,0,1:T(8,128)}, f32[2048,4,128]{2,0,1:T(8,128)})) conditional(s32[]{:T(128)} %convert_element_type.321, (f32[4,8,128,128]{3,2,1,0:T(8,128)S(1)}, f32[2048,4,128]{2,0,1:T(8,128)}, f32[2048,4,128]{2,0,1:T(8,128)}) %tuple.403, (pred[128,512]{0,1:T(8,128)(4,1)S(1)}, ...), branch_computations={%region_42.42_spmd, %region_43.43_spmd} | conditional | flops 2706636800 | bytes 89833640 | solution.py:138
  246.4 2.4 fusion.126
  248.8 3.8 fusion.104
  252.6 3.5 fusion.117
  256.1 3.6 convolution_add_fusion.1
  261.4 1.9 copy-done.3
  268.4 2.5 convert.21
  270.9 10.9 %copy.98 = bf16[2048,4,128]{2,1,0:T(4,128)(2,1)} copy(bf16[2048,4,128]{2,0,1:T(8,128)(2,1)S(1)} %convert.21) | data formatting | bytes 4194304 | tf_op jit(solution)/shard_map/convert.4
  281.8 4.1 stack_reshape.29
  285.9 4.5 pad_maximum_fusion.1
  290.5 2.5 convert.18
  293.0 11.0 %copy.95 = bf16[2048,4,128]{2,1,0:T(4,128)(2,1)} copy(bf16[2048,4,128]{2,0,1:T(8,128)(2,1)S(1)} %convert.18) | data formatting | bytes 4194304 | tf_op jit(solution)/shard_map/convert.9
  304.0 4.1 stack_reshape.26
  308.1 2.5 convert.19
  310.6 10.7 %copy.96 = bf16[2048,4,128]{2,1,0:T(4,128)(2,1)} copy(bf16[2048,4,128]{2,0,1:T(8,128)(2,1)S(1)} %convert.19) | data formatting | bytes 4194304 | tf_op jit(solution)/shard_map/convert.8
  321.3 4.1 stack_reshape.27
  325.4 4.6 pad_maximum_fusion
  331.2 104.8 %psum.7 = f32[2,32]{1,0:T(2,128)S(1)} all-reduce(f32[2,32]{1,0:T(2,128)S(1)} %pad_maximum_fusion.2), channel_id=1, replica_groups=mesh['section'=8,'ctx'=16] {'ctx'}, use_global_device_ids=true, to_apply=%region_49.50 | all-reduce | flops 64 | bytes 512 | tf_op jit(solution)/shard_map/psum | solution.py:209
  436.0 17.6 %collective-permute-start = (f32[32]{0:T(128)S(1)}, f32[32]{0:T(128)S(1)}, u32[]{:S(2)}, u32[]{:S(2)}) collective-permute-start(f32[32]{0:T(128)S(1)} %slice_bitcast_fusion), channel_id=1, source_target_pairs={{0,16},{16,0},{32,48},{48,32},{64,80},{80,64},{96,112},{112,96},{1... | collective-permute-start | bytes 392 | tf_op jit(solution)/shard_map/ppermute | solution.py:23
  457.1 2.3 convert_element_type.233
  463.6 2.2 collective-permute-done.1
  465.8 10.0 %collective-permute-start.2 = (f32[32]{0:T(128)S(1)}, f32[32]{0:T(128)S(1)}, u32[]{:S(2)}, u32[]{:S(2)}) collective-permute-start(f32[32]{0:T(128)S(1)} %collective-permute-done.1), channel_id=1, source_target_pairs={{0,64},{64,0},{16,80},{80,16},{32,96},{96,32},{48,112},{112,48},{1... | collective-permute-start | bytes 392 | tf_op jit(solution)/shard_map/ppermute | solution.py:23
  475.8 3.9 maximum_bitcast_fusion
  480.3 73.5 %reduce-scatter.3.cloned.1.call-done = bf16[2,128,512]{2,1,0:T(8,128)(2,1)} async-done(((bf16[2,2048,512]{2,1,0:T(8,128)(2,1)}), bf16[2,128,512]{2,1,0:T(8,128)(2,1)}) %reduce-scatter.3.cloned.1.call-update) | async-done | bytes 262160 | tf_op jit(solution)/shard_map/reduce_scatter | solution.py:191
  (240 shorter events, 63.5 us)
Async XLA Ops:
  7.2 64.0 %all-gather.3.cloned.1.call-start = ((), (), s32[]{:S(2)}) async-start(), calls=%async_computation.2 | async-start | bytes 4456448 | tf_op jit(solution)/shard_map/all_gather | solution.py:162
  9.0 119.5 %all-gather.5.cloned.1.call-start = ((), (), s32[]{:S(2)}) async-start(), calls=%async_computation.3 | async-start | bytes 4456448 | tf_op jit(solution)/shard_map/all_gather | solution.py:163
  10.9 469.4 %reduce-scatter.5.cloned.1.call-start = ((), (), s32[]{:S(2)}) async-start(), calls=%async_computation.5 | async-start | bytes 4456448 | tf_op jit(solution)/shard_map/reduce_scatter | solution.py:197
  11.8 68.1 %copy-start.15 = (f32[4,8]{1,0:T(4,128)}, f32[4,8]{1,0:T(4,128)S(1)}, u32[]{:S(2)}) copy-start(f32[4,8]{1,0:T(4,128)S(1)} %broadcast_in_dim.201) | copy-start | bytes 388
  16.7 4.2 copy-start.11
  20.9 139.0 %copy-start.17 = (f32[4,8]{1,0:T(4,128)}, f32[4,8]{1,0:T(4,128)S(1)}, u32[]{:S(2)}) copy-start(f32[4,8]{1,0:T(4,128)S(1)} %broadcast_in_dim.203) | copy-start | bytes 388
  23.9 52.1 %copy-start.10 = (bf16[1,1,128,4096]{2,3,1,0:T(8,128)(2,1)}, bf16[1,1,128,4096]{2,3,1,0:T(8,128)(2,1)S(1)}, u32[]{:S(2)}) copy-start(bf16[1,1,128,4096]{2,3,1,0:T(8,128)(2,1)S(1)} %copy.120) | copy-start | bytes 3145732
  153.9 6.1 %copy-start.6 = (bf16[4,8,128,128]{2,3,1,0:T(8,128)(2,1)}, bf16[4,8,128,128]{2,3,1,0:T(8,128)(2,1)S(1)}, u32[]{:S(2)}) copy-start(bf16[4,8,128,128]{2,3,1,0:T(8,128)(2,1)S(1)} %copy.73) | copy-start | bytes 3145732
  191.5 6.5 %copy-start.8 = (bf16[4,8,128,128]{2,3,1,0:T(8,128)(2,1)}, bf16[4,8,128,128]{2,3,1,0:T(8,128)(2,1)S(1)}, u32[]{:S(2)}) copy-start(bf16[4,8,128,128]{2,3,1,0:T(8,128)(2,1)S(1)} %copy.80) | copy-start | bytes 3145732
  201.4 2.4 copy-start.14
  207.6 3.6 copy-start
  211.3 4.9 copy-start.4
  214.9 1.3 copy-start.1
  217.8 1.9 copy-start.5
  246.4 2.4 copy-start.13
  256.1 3.6 copy-start.2
  261.3 1.9 copy-start.3
  290.5 263.2 %reduce-scatter.3.cloned.1.call-start = ((), (), s32[]{:S(2)}) async-start(), calls=%async_computation.4 | async-start | bytes 4456448 | tf_op jit(solution)/shard_map/reduce_scatter | solution.py:191
  330.0 0.7 copy-start.16
  330.0 0.9 copy-start.18
  436.0 27.1 %collective-permute-start = (f32[32]{0:T(128)S(1)}, f32[32]{0:T(128)S(1)}, u32[]{:S(2)}, u32[]{:S(2)}) collective-permute-start(f32[32]{0:T(128)S(1)} %slice_bitcast_fusion), channel_id=1, source_target_pairs={{0,16},{16,0},{32,48},{48,32},{64,80},{80,64},{96,112},{112,96},{1... | collective-permute-start | bytes 392 | tf_op jit(solution)/shard_map/ppermute | solution.py:23
  459.4 2.4 copy-start.7
  459.7 3.4 copy-start.9
  461.7 14.1 %copy-start.12 = (bf16[1,128,4096]{2,1,0:T(8,128)(2,1)S(1)}, bf16[1,128,4096]{2,1,0:T(8,128)(2,1)}, u32[]{:S(2)}) copy-start(bf16[1,128,4096]{2,1,0:T(8,128)(2,1)} %convert_element_type.233) | copy-start | bytes 3145732
  463.1 2.8 collective-permute-start.1
  465.8 13.9 %collective-permute-start.2 = (f32[32]{0:T(128)S(1)}, f32[32]{0:T(128)S(1)}, u32[]{:S(2)}, u32[]{:S(2)}) collective-permute-start(f32[32]{0:T(128)S(1)} %collective-permute-done.1), channel_id=1, source_target_pairs={{0,64},{64,0},{16,80},{80,16},{32,96},{96,32},{48,112},{112,48},{1... | collective-permute-start | bytes 392 | tf_op jit(solution)/shard_map/ppermute | solution.py:23
Sparse Core Ops, SparseCore 0:
  10.9 60.2 all-gather.2
  74.1 54.4 all-gather.4
  290.6 178.7 reduce-scatter.4
  474.3 79.3 reduce-scatter.2
where the time goes:
time: 572 us; the launch traced here: 561 us
  waiting for transfers between devices  157 us (27%)
  local copies, waits for them, and re-layouts  134 us (23%)
  blocking collectives  105 us (18%)
  other arithmetic  58.6 us (10%)
  matrix products  47.1 us (8%)
  starting transfers between devices  27.7 us (5%)
  loops' own time  17.5 us (3%)
  between operations  14.5 us (3%)
    psum x1, blocking collectives, shards(): sink_total = lax.psum(sink_local, 'ctx')  105 us
    reduce_scatter x1, waiting for transfers between devices, shards(): lax.psum_scatter(jnp.stack(key_partial_terms).astype(jnp.bfloat16), 'ctx'...  73.5 us
    another operation x14, local copies, waits for them, and re-layouts  56.6 us
    all_gather x1, waiting for transfers between devices, shards(): lax.all_gather(keys, 'ctx', axis=2, tiled=True)  43.2 us
    all_gather x1, waiting for transfers between devices, shards(): lax.all_gather(values, 'ctx', axis=2, tiled=True)  37.5 us
    unnamed x36, local copies, waits for them, and re-layouts  29.6 us
    ppermute x3, starting transfers between devices, swapped(): return lax.ppermute(block, axis, route)  27.5 us
    dot_general x2, matrix products, second_update(): jnp.einsum('hgqk,khd->hgqd', shares_low, value_block, preferred_element_t...  12.5 us
  transfers between devices with their start and end apart: 7, of which 4 were waited for; matrix products, arithmetic and copies ran while one was open for 16% of the time, Pallas kernels for 0%

commit v1 on v0

v1 whole, which is shorter than its diff:
```python
import functools
import math

import jax
import jax.numpy as jnp
from jax import lax
from jax.experimental import pallas as pl
from jax.experimental.pallas import tpu as pltpu
from jax.sharding import PartitionSpec as P

HEAD_WIDTH = 128
HQ = 32
KEY_HEADS = 4
QUERY_PER_KV = 8
TILE = 128
DOCS = 4
RELAY_COUNT = 2
LONGEST = 9
REACH = LONGEST // 2
ROWS = QUERY_PER_KV * TILE
KEY_COLS = KEY_HEADS * HEAD_WIDTH
QUERY_COLS = HQ * HEAD_WIDTH
SCALE = 1.0 / math.sqrt(HEAD_WIDTH)
LOG2E = 1.4426950408889634
HIDDEN = -1e30


def dot(left, right, left_dim, right_dim):
    return lax.dot_general(
        left,
        right,
        (((left_dim,), (right_dim,)), ((), ())),
        preferred_element_type=jnp.float32,
    )


def attend_kernel(meta, sink, q_ref, g_ref, *refs):
    mine = refs[: REACH + 1]
    mate = refs[REACH + 1 : 2 * REACH + 2]
    refs = refs[2 * REACH + 2 :]
    if len(refs) > 13:
        refs = refs[2:]
    o_ref, dq_ref, even, odd, sink_part = refs[:5]
    kv, grads, low_shares, low_scores, q_rows, g_rows, in_sem, out_sem = refs[5:]
    head = pl.program_id(0)
    count = meta[0]
    core = meta[1]

    def cols(j):
        return pl.ds(pl.multiple_of(j * HEAD_WIDTH, HEAD_WIDTH), HEAD_WIDTH)

    def fetch(j, slot, source):
        return pltpu.make_async_copy(
            source.at[:, :, cols(j)],
            kv.at[j, :, pl.ds(slot * TILE, TILE), :],
            in_sem.at[j, slot],
        )

    def give(j, slot):
        target = odd if slot % 2 else even
        return pltpu.make_async_copy(
            grads.at[j, :, pl.ds(slot * TILE, TILE), :],
            target.at[slot // 2, :, :, cols(j)],
            out_sem.at[j, slot],
        )

    @pl.when(head == 0)
    def _():
        for j in range(KEY_HEADS):
            for slot in range(LONGEST):

                @pl.when(count > slot)
                def _():
                    if slot % 2 == 0:
                        fetch(j, slot, mine[slot // 2]).start()
                    else:
                        near, far = mate[slot // 2], mate[slot // 2 + 1]
                        pl.when(core == 1)(lambda: fetch(j, slot, near).start())
                        pl.when(core == 0)(lambda: fetch(j, slot, far).start())

    for slot in range(LONGEST):
        pl.when(count > slot)(lambda: fetch(head, slot, mine[0]).wait())

    def case(tiles):
        width = tiles * TILE
        keys = kv[head, 0, :width, :]
        values = kv[head, 1, :width, :]
        heads = [slice(i * HEAD_WIDTH, (i + 1) * HEAD_WIDTH) for i in range(QUERY_PER_KV)]
        q = jnp.concatenate([q_ref[0, 0, :, part] for part in heads], axis=0)
        g = jnp.concatenate([g_ref[0, 0, :, part] for part in heads], axis=0)
        scores = dot(q, keys, 1, 1)
        row = lax.broadcasted_iota(jnp.int32, (TILE, TILE), 0)
        column = lax.broadcasted_iota(jnp.int32, (TILE, TILE), 1)
        seen = jnp.concatenate([column <= row] * QUERY_PER_KV, axis=0)
        own = jnp.where(seen, scores[:, :TILE], HIDDEN)
        scores = jnp.concatenate([own, scores[:, TILE:]], axis=1) if tiles > 1 else own
        logit = jnp.concatenate(
            [
                jnp.full((TILE, 1), sink[head * QUERY_PER_KV + i] * LOG2E, jnp.float32)
                for i in range(QUERY_PER_KV)
            ],
            axis=0,
        )
        top = jnp.maximum(jnp.max(scores, axis=1, keepdims=True) * (SCALE * LOG2E), logit)
        raised = jnp.exp2(scores * (SCALE * LOG2E) - top)
        low = raised.astype(jnp.bfloat16)
        low_shares[:, :width] = low
        sink_raised = jnp.exp2(logit - top)
        with_ones = jnp.concatenate([values, jnp.ones_like(values)], axis=1)
        sums = dot(low, with_ones, 1, 0)
        inverse = 1.0 / (sums[:, HEAD_WIDTH:] + sink_raised)
        out = (sums[:, :HEAD_WIDTH] * inverse).astype(jnp.bfloat16)
        g_wide = g.astype(jnp.float32)
        delta = jnp.sum(out.astype(jnp.float32) * g_wide, axis=1, keepdims=True)
        q_rows[...] = (q.astype(jnp.float32) * inverse).astype(jnp.bfloat16)
        g_rows[...] = (g_wide * inverse).astype(jnp.bfloat16)
        score_grads = (raised * (dot(g, values, 1, 1) - delta)).astype(jnp.bfloat16)
        low_scores[:, :width] = score_grads
        q_grad = (dot(score_grads, keys, 1, 0) * (inverse * SCALE)).astype(jnp.bfloat16)
        sink_rows = sink_raised * inverse * delta
        for i, part in enumerate(heads):
            rows = slice(i * TILE, (i + 1) * TILE)
            o_ref[0, 0, :, part] = out[rows]
            dq_ref[0, 0, :, part] = q_grad[rows]
            sink_part[0, i : i + 1, :] = -jnp.sum(sink_rows[rows], axis=0, keepdims=True)
        grads[head, 0, :width, :] = (
            dot(low_scores[:, :width], q_rows[...], 0, 0) * SCALE
        ).astype(jnp.bfloat16)
        grads[head, 1, :width, :] = dot(low_shares[:, :width], g_rows[...], 0, 0).astype(
            jnp.bfloat16
        )

    for tiles in range(1, LONGEST + 1):
        pl.when(count == tiles)(functools.partial(case, tiles))

    for slot in range(LONGEST):
        pl.when(count > slot)(lambda: give(head, slot).start())

    @pl.when(head == KEY_HEADS - 1)
    def _():
        for j in range(KEY_HEADS):
            for slot in range(LONGEST):
                pl.when(count > slot)(lambda: give(j, slot).wait())


def attend(relay, meta, sink, queries, output_gradient, mine, mate, filled):
    wide = pl.BlockSpec((1, 1, TILE, QUERY_PER_KV * HEAD_WIDTH), lambda j: (relay, 0, 0, j))
    smem = pl.BlockSpec(memory_space=pltpu.SMEM)
    whole = pl.BlockSpec(memory_space=pl.ANY)
    low = jnp.bfloat16
    first = 4 + len(mine) + len(mate)
    piece = (2, TILE, KEY_COLS)
    return pl.pallas_call(
        attend_kernel,
        grid=(KEY_HEADS,),
        in_specs=[smem, smem, wide, wide] + [whole] * (len(mine) + len(mate) + len(filled)),
        out_specs=[
            wide,
            wide,
            whole,
            whole,
            pl.BlockSpec((1, QUERY_PER_KV, HEAD_WIDTH), lambda j: (j, 0, 0)),
        ],
        out_shape=[
            jax.ShapeDtypeStruct((RELAY_COUNT, 1, TILE, QUERY_COLS), low),
            jax.ShapeDtypeStruct((RELAY_COUNT, 1, TILE, QUERY_COLS), low),
            jax.ShapeDtypeStruct((REACH + 1,) + piece, low),
            jax.ShapeDtypeStruct((REACH,) + piece, low),
            jax.ShapeDtypeStruct((KEY_HEADS, QUERY_PER_KV, HEAD_WIDTH), jnp.float32),
        ],
        scratch_shapes=[
            pltpu.VMEM((KEY_HEADS, 2, LONGEST * TILE, HEAD_WIDTH), low),
            pltpu.VMEM((KEY_HEADS, 2, LONGEST * TILE, HEAD_WIDTH), low),
            pltpu.VMEM((ROWS, LONGEST * TILE), low),
            pltpu.VMEM((ROWS, LONGEST * TILE), low),
            pltpu.VMEM((ROWS, HEAD_WIDTH), low),
            pltpu.VMEM((ROWS, HEAD_WIDTH), low),
            pltpu.SemaphoreType.DMA((KEY_HEADS, LONGEST)),
            pltpu.SemaphoreType.DMA((KEY_HEADS, LONGEST)),
        ],
        input_output_aliases={first + i: i for i in range(len(filled))},
        compiler_params=pltpu.CompilerParams(vmem_limit_bytes=48 * 1024 * 1024),
        cost_estimate=pl.CostEstimate(
            flops=10 * 6 * ROWS * KEY_COLS * TILE, bytes_accessed=9 << 20, transcendentals=1 << 20
        ),
        name=f"attend_{relay}",
    )(meta, sink, queries, output_gradient, *mine, *mate, *filled)


def shards(queries, keys, values, output_gradient, doc_tiles, sink_logits):
    ctx_count = lax.axis_size("ctx")
    ctx_pos = lax.axis_index("ctx")
    section_pos = lax.axis_index("section")
    section_count = lax.axis_size("section")
    core = lax.rem(ctx_pos, 2)

    def back(amount):
        return [(c, c - amount) for c in range(ctx_count) if 0 <= c - amount < ctx_count]

    def other(moving):
        return [(c, c ^ 1) for c in range(ctx_count) if moving(c)]

    def seen_by(position):
        ends = jnp.cumsum(doc_tiles[:, 0], axis=-1)
        start = jnp.max(jnp.where(ends <= position, ends, 0), axis=-1)
        return position - start + 1

    counts = seen_by(ctx_pos)
    mate_counts = seen_by(ctx_pos + 1 - 2 * core)

    pieces = [jnp.stack([keys[r, 0], values[r, 0]]) for r in range(RELAY_COUNT)]
    mines, mates = {}, {}
    for relay in (1, 0):
        mine = [pieces[relay]]
        for distance in range(1, REACH + 1):
            mine.append(lax.ppermute(pieces[relay], "ctx", back(-2 * distance)))
        mate = [
            lax.ppermute(
                piece,
                "ctx",
                other(
                    lambda c: (c % 2 == 1 or distance < REACH) and (c % 2 == 0 or distance > 0)
                ),
            )
            for distance, piece in enumerate(mine)
        ]
        mines[relay], mates[relay] = mine, mate

    filled = []
    outs, sinks = {}, {}
    for relay in (1, 0):
        layer = section_pos if relay == 0 else section_count - 1 - section_pos
        sink = lax.dynamic_index_in_dim(sink_logits, layer, 0, keepdims=False)
        meta = jnp.stack([counts[relay], core]).astype(jnp.int32)
        attention, query_grad, even, odd, sink_part = attend(
            relay, meta, sink, queries, output_gradient, mines[relay], mates[relay], filled
        )
        filled = [attention, query_grad]
        sinks[relay] = sink_part[:, :, 0].reshape(HQ)
        from_mate = lax.ppermute(odd, "ctx", other(lambda c: True))
        total = None
        for distance in range(REACH + 1):
            theirs = distance - core
            slot = 2 * theirs + 1
            term = jnp.where(
                counts[relay] > 2 * distance, even[distance].astype(jnp.float32), 0.0
            ) + jnp.where(
                (theirs >= 0) & (theirs < REACH) & (mate_counts[relay] > slot),
                lax.dynamic_index_in_dim(
                    from_mate, jnp.clip(theirs, 0, REACH - 1), 0, keepdims=False
                ).astype(jnp.float32),
                0.0,
            )
            if distance == 0:
                total = term
            else:
                sent = lax.ppermute(term.astype(jnp.bfloat16), "ctx", back(2 * distance))
                total = total + sent.astype(jnp.float32)
        outs[relay] = total.astype(jnp.bfloat16)

    mirrored = lax.ppermute(
        sinks[1], "section", [(s, section_count - 1 - s) for s in range(section_count)]
    )
    sink_grad = sinks[0] + mirrored
    step = 1
    while step < ctx_count:
        sink_grad = sink_grad + lax.ppermute(
            sink_grad, "ctx", [(c, c ^ step) for c in range(ctx_count)]
        )
        step *= 2
    attention, query_grad = filled
    key_gradient = jnp.stack([outs[r][0] for r in range(RELAY_COUNT)])[:, None]
    value_gradient = jnp.stack([outs[r][1] for r in range(RELAY_COUNT)])[:, None]
    return (attention, query_grad, key_gradient, value_gradient, sink_grad[None])


def solution(mesh):
    placed = (
        P(None, "section", "ctx", None),
        P(None, "section", "ctx", None),
        P(None, "section", "ctx", None),
        P(None, "section", "ctx", None),
        P(None, "section", None),
        P(),
    )
    return jax.shard_map(
        shards,
        mesh=mesh,
        in_specs=placed,
        out_specs=(
            P(None, "section", "ctx", None),
            P(None, "section", "ctx", None),
            P(None, "section", "ctx", None),
            P(None, "section", "ctx", None),
            P("section", None),
        ),
        check_vma=False,
    )
```

time: 572 us -> 255 us (0.45)
  the two profiles are of different devices: /device:TPU:1 before, /device:TPU:12 now
where the time goes in v1:
time: 255 us; the launch traced here: 253 us
  Pallas kernels  94.5 us (37%)
  starting transfers between devices  69.6 us (27%)
  waiting for transfers between devices  54.1 us (21%)
  between operations  14.3 us (6%)
  local copies, waits for them, and re-layouts  10.1 us (4%)
  other arithmetic  10 us (4%)
    pallas_call x2, Pallas kernels, attend(): pl.pallas_call(attend_kernel, grid=(KEY_HEADS,), in_specs=[smem, smem, wi...  94.5 us
    ppermute x8, waiting for transfers between devices, shards(): sent = lax.ppermute(term.astype(jnp.bfloat16), 'ctx', back(2 * distance))  26.5 us
    ppermute x8, starting transfers between devices, shards(): mine.append(lax.ppermute(pieces[relay], 'ctx', back(-2 * distance)))  21.9 us
    ppermute x8, starting transfers between devices, shards(): sent = lax.ppermute(term.astype(jnp.bfloat16), 'ctx', back(2 * distance))  20.9 us
    ppermute x8, waiting for transfers between devices, shards(): mine.append(lax.ppermute(pieces[relay], 'ctx', back(-2 * distance)))  15.9 us
    ppermute x4, starting transfers between devices, shards(): lax.ppermute(sink_grad, 'ctx', [(c, c ^ step) for c in range(ctx_count)])  12.9 us
    ppermute x10, starting transfers between devices, shards(): lax.ppermute(piece, 'ctx', other(lambda c: (c % 2 == 1 or distance < REAC...  7.94 us
    unnamed x16, local copies, waits for them, and re-layouts  6.59 us
  transfers between devices with their start and end apart: 33, of which 12 were waited for; matrix products, arithmetic and copies ran while one was open for 4% of the time, Pallas kernels for 26%

profile of v1, /device:TPU:12, one launch (start us, length us, event | category | flops | bytes accessed | tf_op | source)
XLA Modules:
  0.0 252.5 jit_solution(1748110113297897858)
XLA Ops:
  0.6 1.1 slice_bitcast_fusion
  1.8 3.4 %collective-permute-start.9 = (bf16[2,128,512]{2,1,0:T(8,128)(2,1)S(1)}, bf16[2,128,512]{2,1,0:T(8,128)(2,1)S(1)}, u32[]{:S(2)}, u32[]{:S(2)}) collective-permute-start(bf16[2,128,512]{2,1,0:T(8,128)(2,1)S(1)} %pad_maximum_fusion.1.refs_0_), channel_id=1, source_target_pairs={{0,2},{1,3},{2,4},{3,5},{4,6},{5,7},{6,8},{7,9},{8,10},{9,11},{10,... | collective-permute-start | bytes 786440 | tf_op jit(solution)/shard_map/ppermute | solution.py:216
  5.2 3.2 %collective-permute-start.10 = (bf16[2,128,512]{2,1,0:T(8,128)(2,1)S(1)}, bf16[2,128,512]{2,1,0:T(8,128)(2,1)S(1)}, u32[]{:S(2)}, u32[]{:S(2)}) collective-permute-start(bf16[2,128,512]{2,1,0:T(8,128)(2,1)S(1)} %pad_maximum_fusion.1.refs_0_), channel_id=1, source_target_pairs={{0,4},{1,5},{2,6},{3,7},{4,8},{5,9},{6,10},{7,11},{8,12},{9,13},{1... | collective-permute-start | bytes 786440 | tf_op jit(solution)/shard_map/ppermute | solution.py:216
  8.4 3.8 %collective-permute-start.11 = (bf16[2,128,512]{2,1,0:T(8,128)(2,1)S(1)}, bf16[2,128,512]{2,1,0:T(8,128)(2,1)S(1)}, u32[]{:S(2)}, u32[]{:S(2)}) collective-permute-start(bf16[2,128,512]{2,1,0:T(8,128)(2,1)S(1)} %pad_maximum_fusion.1.refs_0_), channel_id=1, source_target_pairs={{0,6},{1,7},{2,8},{3,9},{4,10},{5,11},{6,12},{7,13},{8,14},{9,15},... | collective-permute-start | bytes 786440 | tf_op jit(solution)/shard_map/ppermute | solution.py:216
  12.2 1.3 collective-permute-start.12
  13.5 1.3 collective-permute-start.13
  14.8 0.9 reduce_window_sum.12
  15.7 0.1 fusion.17
  15.9 3.1 %collective-permute-start = (bf16[2,128,512]{2,1,0:T(8,128)(2,1)S(1)}, bf16[2,128,512]{2,1,0:T(8,128)(2,1)S(1)}, u32[]{:S(2)}, u32[]{:S(2)}) collective-permute-start(bf16[2,128,512]{2,1,0:T(8,128)(2,1)S(1)} %pad_maximum_fusion.refs_0_), channel_id=1, source_target_pairs={{0,2},{1,3},{2,4},{3,5},{4,6},{5,7},{6,8},{7,9},{8,10},{9,11},{10,... | collective-permute-start | bytes 786440 | tf_op jit(solution)/shard_map/ppermute | solution.py:216
  19.0 1.7 collective-permute-done.10.refs_2_
  20.6 3.1 %collective-permute-start.1 = (bf16[2,128,512]{2,1,0:T(8,128)(2,1)S(1)}, bf16[2,128,512]{2,1,0:T(8,128)(2,1)}, u32[]{:S(2)}, u32[]{:S(2)}) collective-permute-start(bf16[2,128,512]{2,1,0:T(8,128)(2,1)S(1)} %pad_maximum_fusion.refs_0_), channel_id=1, source_target_pairs={{0,4},{1,5},{2,6},{3,7},{4,8},{5,9},{6,10},{7,11},{8,12},{9,13},{1... | collective-permute-start | bytes 786440 | tf_op jit(solution)/shard_map/ppermute | solution.py:216
  23.7 2.1 collective-permute-start.2
  25.9 0.6 fusion.23
  26.5 2.0 collective-permute-start.3
  28.5 0.5 collective-permute-start.15
  29.0 2.9 %collective-permute-done.1.refs_2_ = bf16[2,128,512]{2,1,0:T(8,128)(2,1)} collective-permute-done((bf16[2,128,512]{2,1,0:T(8,128)(2,1)S(1)}, bf16[2,128,512]{2,1,0:T(8,128)(2,1)}, u32[]{:S(2)}, u32[]{:S(2)}) %collective-permute-start.1) | collective-permute-done | bytes 262176 | tf_op jit(solution)/shard_map/ppermute | solution.py:216
  31.9 11.3 %collective-permute-done.2.refs_3_ = bf16[2,128,512]{2,1,0:T(8,128)(2,1)} collective-permute-done((bf16[2,128,512]{2,1,0:T(8,128)(2,1)S(1)}, bf16[2,128,512]{2,1,0:T(8,128)(2,1)}, u32[]{:S(2)}, u32[]{:S(2)}) %collective-permute-start.2) | collective-permute-done | bytes 262176 | tf_op jit(solution)/shard_map/ppermute | solution.py:216
  43.2 1.3 collective-permute-start.17
  44.5 0.7 pad_add_fusion.1.meta
  45.2 0.8 pad_add_fusion.meta
  46.0 0.8 fusion.19
  46.8 3.0 %collective-permute-start.4 = (bf16[2,128,512]{2,1,0:T(8,128)(2,1)S(1)}, bf16[2,128,512]{2,1,0:T(8,128)(2,1)S(1)}, u32[]{:S(2)}, u32[]{:S(2)}) collective-permute-start(bf16[2,128,512]{2,1,0:T(8,128)(2,1)S(1)} %pad_maximum_fusion.refs_0_), channel_id=1, source_target_pairs={{0,1},{2,3},{4,5},{6,7},{8,9},{10,11},{12,13},{14,15},{16,17},{18,... | collective-permute-start | bytes 786440 | tf_op jit(solution)/shard_map/ppermute | solution.py:218
  49.8 0.7 copy-done
  50.5 0.7 copy-done.2
  51.2 0.5 collective-permute-start.6
  51.8 0.7 copy-done.4
  52.5 0.7 copy-done.6
  53.2 1.3 collective-permute-start.8
  54.5 0.9 copy-done.1
  55.4 0.9 copy-done.3
  56.4 0.9 copy-done.5
  57.3 0.9 copy-done.7
  58.3 66.0 %attend_1.1 = (bf16[2,1,128,4096]{3,2,1,0:T(8,128)(2,1)}, bf16[2,1,128,4096]{3,2,1,0:T(8,128)(2,1)}, bf16[5,2,128,512]{3,2,1,0:T(8,128)(2,1)S(1)}, bf16[4,2,128,512]{3,2,1,0:T(8,128)(2,1)}, f32[4,8,128]{2,1,0:T(8,128)S(1)}) custom-call(s32[2]{0:T(128)S(1)} %pad_add_fusion.1.meta, f32[32]{0:T(128)S(1)} %get-tuple-element.53.sink, ...), custom_call_target="tpu_custom_call" | custom-call | flops 4026531840 | bytes 9437184 | tf_op jit(solution)/shard_map/attend_1/pallas_call | solution.py:153
  124.3 28.6 %attend_0.1 = (bf16[2,1,128,4096]{3,2,1,0:T(8,128)(2,1)}, bf16[2,1,128,4096]{3,2,1,0:T(8,128)(2,1)}, bf16[5,2,128,512]{3,2,1,0:T(8,128)(2,1)S(1)}, bf16[4,2,128,512]{3,2,1,0:T(8,128)(2,1)}, f32[4,8,128]{2,1,0:T(8,128)S(1)}) custom-call(s32[2]{0:T(128)S(1)} %pad_add_fusion.meta, ...), custom_call_target="tpu_custom_call", output_to_operand_aliasing={{0}: (14, {}), {1}: (15, {})} | custom-call | flops 4026531840 | bytes 9437184 | tf_op jit(solution)/shard_map/attend_0/pallas_call | solution.py:153
  152.8 5.8 %collective-permute-start.18 = (bf16[4,2,128,512]{3,2,1,0:T(8,128)(2,1)}, bf16[4,2,128,512]{3,2,1,0:T(8,128)(2,1)}, u32[]{:S(2)}, u32[]{:S(2)}) collective-permute-start(bf16[4,2,128,512]{3,2,1,0:T(8,128)(2,1)} %get-tuple-element.20), channel_id=1, source_target_pairs={{0,1},{1,0},{2,3},{3,2},{4,5},{5,4},{6,7},{7,6},{8,9},{9,8},{10,11... | collective-permute-start | bytes 3145736 | tf_op jit(solution)/shard_map/ppermute | solution.py:240
  158.7 0.1 collective-permute-start.23
  158.7 0.6 fusion.22
  172.4 0.1 slice_reduce_fusion
  172.8 5.5 %collective-permute-done.28 = f32[32]{0:T(128)S(1)} collective-permute-done((f32[32]{0:T(128)S(1)}, f32[32]{0:T(128)S(1)}, u32[]{:S(2)}, u32[]{:S(2)}) %collective-permute-start.28) | collective-permute-done | bytes 160 | tf_op jit(solution)/shard_map/ppermute | solution.py:261
  178.2 1.1 collective-permute-done.29
  179.4 4.2 %collective-permute-start.30 = (f32[32]{0:T(128)S(1)}, f32[32]{0:T(128)S(1)}, u32[]{:S(2)}, u32[]{:S(2)}) collective-permute-start(f32[32]{0:T(128)S(1)} %add.162), channel_id=1, source_target_pairs={{0,2},{1,3},{2,0},{3,1},{4,6},{5,7},{6,4},{7,5},{8,10},{9,11},{10,... | collective-permute-start | bytes 392 | tf_op jit(solution)/shard_map/ppermute | solution.py:267
  183.5 1.5 collective-permute-done.30
  185.1 3.5 %collective-permute-done.31 = f32[32]{0:T(128)S(1)} collective-permute-done((f32[32]{0:T(128)S(1)}, f32[32]{0:T(128)S(1)}, u32[]{:S(2)}, u32[]{:S(2)}) %collective-permute-start.31) | collective-permute-done | bytes 160 | tf_op jit(solution)/shard_map/ppermute | solution.py:267
  188.6 8.7 %collective-permute-start.32 = (f32[32]{0:T(128)S(1)}, f32[32]{0:T(128)S(1)}, u32[]{:S(2)}, u32[]{:S(2)}) collective-permute-start(f32[32]{0:T(128)S(1)} %add.164), channel_id=1, source_target_pairs={{0,8},{1,9},{2,10},{3,11},{4,12},{5,13},{6,14},{7,15},{8,0},{9,1},... | collective-permute-start | bytes 392 | tf_op jit(solution)/shard_map/ppermute | solution.py:267
  197.3 1.6 fusion.8
  198.9 5.4 %collective-permute-start.19 = (bf16[2,128,512]{2,1,0:T(8,128)(2,1)S(1)}, bf16[2,128,512]{2,1,0:T(8,128)(2,1)S(1)}, u32[]{:S(2)}, u32[]{:S(2)}) collective-permute-start(bf16[2,128,512]{2,1,0:T(8,128)(2,1)S(1)} %get-tuple-element.37), channel_id=1, source_target_pairs={{2,0},{3,1},{4,2},{5,3},{6,4},{7,5},{8,6},{9,7},{10,8},{11,9},{12,... | collective-permute-start | bytes 786440 | tf_op jit(solution)/shard_map/ppermute | solution.py:257
  204.3 4.5 %collective-permute-start.20 = (bf16[2,128,512]{2,1,0:T(8,128)(2,1)S(1)}, bf16[2,128,512]{2,1,0:T(8,128)(2,1)S(1)}, u32[]{:S(2)}, u32[]{:S(2)}) collective-permute-start(bf16[2,128,512]{2,1,0:T(8,128)(2,1)S(1)} %get-tuple-element.40), channel_id=1, source_target_pairs={{4,0},{5,1},{6,2},{7,3},{8,4},{9,5},{10,6},{11,7},{12,8},{13,9},{1... | collective-permute-start | bytes 786440 | tf_op jit(solution)/shard_map/ppermute | solution.py:257
  208.9 1.9 collective-permute-start.21
  210.8 1.3 collective-permute-start.22
  212.1 0.5 add_bitcast_fusion
  212.6 1.6 fusion.12
  214.2 1.9 collective-permute-start.24
  216.1 1.9 collective-permute-start.25
  218.1 0.1 collective-permute-done.20
  218.2 2.6 %collective-permute-start.26 = (bf16[2,128,512]{2,1,0:T(8,128)(2,1)S(1)}, bf16[2,128,512]{2,1,0:T(8,128)(2,1)S(1)}, u32[]{:S(2)}, u32[]{:S(2)}) collective-permute-start(bf16[2,128,512]{2,1,0:T(8,128)(2,1)S(1)} %get-tuple-element.43), channel_id=1, source_target_pairs={{6,0},{7,1},{8,2},{9,3},{10,4},{11,5},{12,6},{13,7},{14,8},{15,9},... | collective-permute-start | bytes 786440 | tf_op jit(solution)/shard_map/ppermute | solution.py:257
  220.8 3.5 %collective-permute-done.21 = bf16[2,128,512]{2,1,0:T(8,128)(2,1)S(1)} collective-permute-done((bf16[2,128,512]{2,1,0:T(8,128)(2,1)S(1)}, bf16[2,128,512]{2,1,0:T(8,128)(2,1)S(1)}, u32[]{:S(2)}, u32[]{:S(2)}) %collective-permute-start.21) | collective-permute-done | bytes 262176 | tf_op jit(solution)/shard_map/ppermute | solution.py:257
  224.2 1.3 collective-permute-start.27
  225.5 13.1 %collective-permute-done.22 = bf16[2,128,512]{2,1,0:T(8,128)(2,1)S(1)} collective-permute-done((bf16[2,128,512]{2,1,0:T(8,128)(2,1)S(1)}, bf16[2,128,512]{2,1,0:T(8,128)(2,1)S(1)}, u32[]{:S(2)}, u32[]{:S(2)}) %collective-permute-start.22) | collective-permute-done | bytes 262176 | tf_op jit(solution)/shard_map/ppermute | solution.py:257
  238.6 1.2 fusion.7
  239.9 3.5 %collective-permute-done.25 = bf16[2,128,512]{2,1,0:T(8,128)(2,1)S(1)} collective-permute-done((bf16[2,128,512]{2,1,0:T(8,128)(2,1)S(1)}, bf16[2,128,512]{2,1,0:T(8,128)(2,1)S(1)}, u32[]{:S(2)}, u32[]{:S(2)}) %collective-permute-start.25) | collective-permute-done | bytes 262176 | tf_op jit(solution)/shard_map/ppermute | solution.py:257
  243.3 6.3 %collective-permute-done.27 = bf16[2,128,512]{2,1,0:T(8,128)(2,1)S(1)} collective-permute-done((bf16[2,128,512]{2,1,0:T(8,128)(2,1)S(1)}, bf16[2,128,512]{2,1,0:T(8,128)(2,1)S(1)}, u32[]{:S(2)}, u32[]{:S(2)}) %collective-permute-start.27) | collective-permute-done | bytes 262176 | tf_op jit(solution)/shard_map/ppermute | solution.py:257
  249.7 1.2 fusion.3
  250.9 0.7 maximum_bitcast_fusion.1
  251.6 0.7 maximum_bitcast_fusion
  (48 shorter events, 0.5 us)
Async XLA Ops:
  1.8 14.1 %collective-permute-start.9 = (bf16[2,128,512]{2,1,0:T(8,128)(2,1)S(1)}, bf16[2,128,512]{2,1,0:T(8,128)(2,1)S(1)}, u32[]{:S(2)}, u32[]{:S(2)}) collective-permute-start(bf16[2,128,512]{2,1,0:T(8,128)(2,1)S(1)} %pad_maximum_fusion.1.refs_0_), channel_id=1, source_target_pairs={{0,2},{1,3},{2,4},{3,5},{4,6},{5,7},{6,8},{7,9},{8,10},{9,11},{10,... | collective-permute-start | bytes 786440 | tf_op jit(solution)/shard_map/ppermute | solution.py:216
  5.2 15.4 %collective-permute-start.10 = (bf16[2,128,512]{2,1,0:T(8,128)(2,1)S(1)}, bf16[2,128,512]{2,1,0:T(8,128)(2,1)S(1)}, u32[]{:S(2)}, u32[]{:S(2)}) collective-permute-start(bf16[2,128,512]{2,1,0:T(8,128)(2,1)S(1)} %pad_maximum_fusion.1.refs_0_), channel_id=1, source_target_pairs={{0,4},{1,5},{2,6},{3,7},{4,8},{5,9},{6,10},{7,11},{8,12},{9,13},{1... | collective-permute-start | bytes 786440 | tf_op jit(solution)/shard_map/ppermute | solution.py:216
  8.4 15.3 %collective-permute-start.11 = (bf16[2,128,512]{2,1,0:T(8,128)(2,1)S(1)}, bf16[2,128,512]{2,1,0:T(8,128)(2,1)S(1)}, u32[]{:S(2)}, u32[]{:S(2)}) collective-permute-start(bf16[2,128,512]{2,1,0:T(8,128)(2,1)S(1)} %pad_maximum_fusion.1.refs_0_), channel_id=1, source_target_pairs={{0,6},{1,7},{2,8},{3,9},{4,10},{5,11},{6,12},{7,13},{8,14},{9,15},... | collective-permute-start | bytes 786440 | tf_op jit(solution)/shard_map/ppermute | solution.py:216
  12.2 14.3 %collective-permute-start.12 = (bf16[2,128,512]{2,1,0:T(8,128)(2,1)S(1)}, bf16[2,128,512]{2,1,0:T(8,128)(2,1)S(1)}, u32[]{:S(2)}, u32[]{:S(2)}) collective-permute-start(bf16[2,128,512]{2,1,0:T(8,128)(2,1)S(1)} %pad_maximum_fusion.1.refs_0_), channel_id=1, source_target_pairs={{0,8},{1,9},{2,10},{3,11},{4,12},{5,13},{6,14},{7,15},{16,24},{17,... | collective-permute-start | bytes 786440 | tf_op jit(solution)/shard_map/ppermute | solution.py:216
  13.5 15.0 %collective-permute-start.13 = (bf16[2,128,512]{2,1,0:T(8,128)(2,1)S(1)}, bf16[2,128,512]{2,1,0:T(8,128)(2,1)S(1)}, u32[]{:S(2)}, u32[]{:S(2)}) collective-permute-start(bf16[2,128,512]{2,1,0:T(8,128)(2,1)S(1)} %pad_maximum_fusion.1.refs_0_), channel_id=1, source_target_pairs={{0,1},{2,3},{4,5},{6,7},{8,9},{10,11},{12,13},{14,15},{16,17},{18,... | collective-permute-start | bytes 786440 | tf_op jit(solution)/shard_map/ppermute | solution.py:218
  15.9 12.6 %collective-permute-start = (bf16[2,128,512]{2,1,0:T(8,128)(2,1)S(1)}, bf16[2,128,512]{2,1,0:T(8,128)(2,1)S(1)}, u32[]{:S(2)}, u32[]{:S(2)}) collective-permute-start(bf16[2,128,512]{2,1,0:T(8,128)(2,1)S(1)} %pad_maximum_fusion.refs_0_), channel_id=1, source_target_pairs={{0,2},{1,3},{2,4},{3,5},{4,6},{5,7},{6,8},{7,9},{8,10},{9,11},{10,... | collective-permute-start | bytes 786440 | tf_op jit(solution)/shard_map/ppermute | solution.py:216
  20.6 11.3 %collective-permute-start.1 = (bf16[2,128,512]{2,1,0:T(8,128)(2,1)S(1)}, bf16[2,128,512]{2,1,0:T(8,128)(2,1)}, u32[]{:S(2)}, u32[]{:S(2)}) collective-permute-start(bf16[2,128,512]{2,1,0:T(8,128)(2,1)S(1)} %pad_maximum_fusion.refs_0_), channel_id=1, source_target_pairs={{0,4},{1,5},{2,6},{3,7},{4,8},{5,9},{6,10},{7,11},{8,12},{9,13},{1... | collective-permute-start | bytes 786440 | tf_op jit(solution)/shard_map/ppermute | solution.py:216
  23.7 19.5 %collective-permute-start.2 = (bf16[2,128,512]{2,1,0:T(8,128)(2,1)S(1)}, bf16[2,128,512]{2,1,0:T(8,128)(2,1)}, u32[]{:S(2)}, u32[]{:S(2)}) collective-permute-start(bf16[2,128,512]{2,1,0:T(8,128)(2,1)S(1)} %pad_maximum_fusion.refs_0_), channel_id=1, source_target_pairs={{0,6},{1,7},{2,8},{3,9},{4,10},{5,11},{6,12},{7,13},{8,14},{9,15},... | collective-permute-start | bytes 786440 | tf_op jit(solution)/shard_map/ppermute | solution.py:216
  26.5 20.2 %collective-permute-start.3 = (bf16[2,128,512]{2,1,0:T(8,128)(2,1)S(1)}, bf16[2,128,512]{2,1,0:T(8,128)(2,1)}, u32[]{:S(2)}, u32[]{:S(2)}) collective-permute-start(bf16[2,128,512]{2,1,0:T(8,128)(2,1)S(1)} %pad_maximum_fusion.refs_0_), channel_id=1, source_target_pairs={{0,8},{1,9},{2,10},{3,11},{4,12},{5,13},{6,14},{7,15},{16,24},{17,... | collective-permute-start | bytes 786440 | tf_op jit(solution)/shard_map/ppermute | solution.py:216
  28.5 21.3 %collective-permute-start.14 = (bf16[2,128,512]{2,1,0:T(8,128)(2,1)S(1)}, bf16[2,128,512]{2,1,0:T(8,128)(2,1)S(1)}, u32[]{:S(2)}, u32[]{:S(2)}) collective-permute-start(bf16[2,128,512]{2,1,0:T(8,128)(2,1)S(1)} %collective-permute-done.9.refs_1_), channel_id=1, source_target_pairs={{0,1},{1,0},{2,3},{3,2},{4,5},{5,4},{6,7},{7,6},{8,9},{9,8},{10,11... | collective-permute-start | bytes 786440 | tf_op jit(solution)/shard_map/ppermute | solution.py:218
  28.5 22.0 %collective-permute-start.15 = (bf16[2,128,512]{2,1,0:T(8,128)(2,1)S(1)}, bf16[2,128,512]{2,1,0:T(8,128)(2,1)S(1)}, u32[]{:S(2)}, u32[]{:S(2)}) collective-permute-start(bf16[2,128,512]{2,1,0:T(8,128)(2,1)S(1)} %collective-permute-done.10.refs_2_), channel_id=1, source_target_pairs={{0,1},{1,0},{2,3},{3,2},{4,5},{5,4},{6,7},{7,6},{8,9},{9,8},{10,11... | collective-permute-start | bytes 786440 | tf_op jit(solution)/shard_map/ppermute | solution.py:218
  31.9 19.9 %collective-permute-start.16 = (bf16[2,128,512]{2,1,0:T(8,128)(2,1)S(1)}, bf16[2,128,512]{2,1,0:T(8,128)(2,1)S(1)}, u32[]{:S(2)}, u32[]{:S(2)}) collective-permute-start(bf16[2,128,512]{2,1,0:T(8,128)(2,1)S(1)} %collective-permute-done.11.refs_3_), channel_id=1, source_target_pairs={{0,1},{1,0},{2,3},{3,2},{4,5},{5,4},{6,7},{7,6},{8,9},{9,8},{10,11... | collective-permute-start | bytes 786440 | tf_op jit(solution)/shard_map/ppermute | solution.py:218
  43.2 9.2 %collective-permute-start.17 = (bf16[2,128,512]{2,1,0:T(8,128)(2,1)S(1)}, bf16[2,128,512]{2,1,0:T(8,128)(2,1)S(1)}, u32[]{:S(2)}, u32[]{:S(2)}) collective-permute-start(bf16[2,128,512]{2,1,0:T(8,128)(2,1)S(1)} %collective-permute-done.12.refs_4_), channel_id=1, source_target_pairs={{1,0},{3,2},{5,4},{7,6},{9,8},{11,10},{13,12},{15,14},{17,16},{19,... | collective-permute-start | bytes 786440 | tf_op jit(solution)/shard_map/ppermute | solution.py:218
  46.8 77.5 %collective-permute-start.4 = (bf16[2,128,512]{2,1,0:T(8,128)(2,1)S(1)}, bf16[2,128,512]{2,1,0:T(8,128)(2,1)S(1)}, u32[]{:S(2)}, u32[]{:S(2)}) collective-permute-start(bf16[2,128,512]{2,1,0:T(8,128)(2,1)S(1)} %pad_maximum_fusion.refs_0_), channel_id=1, source_target_pairs={{0,1},{2,3},{4,5},{6,7},{8,9},{10,11},{12,13},{14,15},{16,17},{18,... | collective-permute-start | bytes 786440 | tf_op jit(solution)/shard_map/ppermute | solution.py:218
  49.8 0.7 copy-start
  50.5 73.7 %collective-permute-start.5 = (bf16[2,128,512]{2,1,0:T(8,128)(2,1)S(1)}, bf16[2,128,512]{2,1,0:T(8,128)(2,1)S(1)}, u32[]{:S(2)}, u32[]{:S(2)}) collective-permute-start(bf16[2,128,512]{2,1,0:T(8,128)(2,1)S(1)} %collective-permute-done.refs_1_), channel_id=1, source_target_pairs={{0,1},{1,0},{2,3},{3,2},{4,5},{5,4},{6,7},{7,6},{8,9},{9,8},{10,11... | collective-permute-start | bytes 786440 | tf_op jit(solution)/shard_map/ppermute | solution.py:218
  50.5 0.7 copy-start.2
  51.2 73.0 %collective-permute-start.6 = (bf16[2,128,512]{2,1,0:T(8,128)(2,1)}, bf16[2,128,512]{2,1,0:T(8,128)(2,1)S(1)}, u32[]{:S(2)}, u32[]{:S(2)}) collective-permute-start(bf16[2,128,512]{2,1,0:T(8,128)(2,1)} %collective-permute-done.1.refs_2_), channel_id=1, source_target_pairs={{0,1},{1,0},{2,3},{3,2},{4,5},{5,4},{6,7},{7,6},{8,9},{9,8},{10,11... | collective-permute-start | bytes 786440 | tf_op jit(solution)/shard_map/ppermute | solution.py:218
  51.7 0.7 copy-start.4
  52.5 71.8 %collective-permute-start.7 = (bf16[2,128,512]{2,1,0:T(8,128)(2,1)}, bf16[2,128,512]{2,1,0:T(8,128)(2,1)S(1)}, u32[]{:S(2)}, u32[]{:S(2)}) collective-permute-start(bf16[2,128,512]{2,1,0:T(8,128)(2,1)} %collective-permute-done.2.refs_3_), channel_id=1, source_target_pairs={{0,1},{1,0},{2,3},{3,2},{4,5},{5,4},{6,7},{7,6},{8,9},{9,8},{10,11... | collective-permute-start | bytes 786440 | tf_op jit(solution)/shard_map/ppermute | solution.py:218
  52.5 0.7 copy-start.6
  53.2 71.1 %collective-permute-start.8 = (bf16[2,128,512]{2,1,0:T(8,128)(2,1)}, bf16[2,128,512]{2,1,0:T(8,128)(2,1)S(1)}, u32[]{:S(2)}, u32[]{:S(2)}) collective-permute-start(bf16[2,128,512]{2,1,0:T(8,128)(2,1)} %collective-permute-done.3.refs_4_), channel_id=1, source_target_pairs={{1,0},{3,2},{5,4},{7,6},{9,8},{11,10},{13,12},{15,14},{17,16},{19,... | collective-permute-start | bytes 786440 | tf_op jit(solution)/shard_map/ppermute | solution.py:218
  54.5 1.0 copy-start.1
  55.4 0.9 copy-start.3
  56.4 0.9 copy-start.5
  57.3 0.9 copy-start.7
  152.8 44.5 %collective-permute-start.18 = (bf16[4,2,128,512]{3,2,1,0:T(8,128)(2,1)}, bf16[4,2,128,512]{3,2,1,0:T(8,128)(2,1)}, u32[]{:S(2)}, u32[]{:S(2)}) collective-permute-start(bf16[4,2,128,512]{3,2,1,0:T(8,128)(2,1)} %get-tuple-element.20), channel_id=1, source_target_pairs={{0,1},{1,0},{2,3},{3,2},{4,5},{5,4},{6,7},{7,6},{8,9},{9,8},{10,11... | collective-permute-start | bytes 3145736 | tf_op jit(solution)/shard_map/ppermute | solution.py:240
  158.7 54.0 %collective-permute-start.23 = (bf16[4,2,128,512]{3,2,1,0:T(8,128)(2,1)}, bf16[4,2,128,512]{3,2,1,0:T(8,128)(2,1)}, u32[]{:S(2)}, u32[]{:S(2)}) collective-permute-start(bf16[4,2,128,512]{3,2,1,0:T(8,128)(2,1)} %get-tuple-element.22), channel_id=1, source_target_pairs={{0,1},{1,0},{2,3},{3,2},{4,5},{5,4},{6,7},{7,6},{8,9},{9,8},{10,11... | collective-permute-start | bytes 3145736 | tf_op jit(solution)/shard_map/ppermute | solution.py:240
  172.6 5.7 %collective-permute-start.28 = (f32[32]{0:T(128)S(1)}, f32[32]{0:T(128)S(1)}, u32[]{:S(2)}, u32[]{:S(2)}) collective-permute-start(f32[32]{0:T(128)S(1)} %reshape_squeeze.7), channel_id=1, source_target_pairs={{0,112},{16,96},{32,80},{48,64},{64,48},{80,32},{96,16},{112,0},{1... | collective-permute-start | bytes 392 | tf_op jit(solution)/shard_map/ppermute | solution.py:261
  178.2 1.1 collective-permute-start.29
  179.4 5.7 %collective-permute-start.30 = (f32[32]{0:T(128)S(1)}, f32[32]{0:T(128)S(1)}, u32[]{:S(2)}, u32[]{:S(2)}) collective-permute-start(f32[32]{0:T(128)S(1)} %add.162), channel_id=1, source_target_pairs={{0,2},{1,3},{2,0},{3,1},{4,6},{5,7},{6,4},{7,5},{8,10},{9,11},{10,... | collective-permute-start | bytes 392 | tf_op jit(solution)/shard_map/ppermute | solution.py:267
  185.1 3.5 %collective-permute-start.31 = (f32[32]{0:T(128)S(1)}, f32[32]{0:T(128)S(1)}, u32[]{:S(2)}, u32[]{:S(2)}) collective-permute-start(f32[32]{0:T(128)S(1)} %add.163), channel_id=1, source_target_pairs={{0,4},{1,5},{2,6},{3,7},{4,0},{5,1},{6,2},{7,3},{8,12},{9,13},{10,... | collective-permute-start | bytes 392 | tf_op jit(solution)/shard_map/ppermute | solution.py:267
  188.6 22.2 %collective-permute-start.32 = (f32[32]{0:T(128)S(1)}, f32[32]{0:T(128)S(1)}, u32[]{:S(2)}, u32[]{:S(2)}) collective-permute-start(f32[32]{0:T(128)S(1)} %add.164), channel_id=1, source_target_pairs={{0,8},{1,9},{2,10},{3,11},{4,12},{5,13},{6,14},{7,15},{8,0},{9,1},... | collective-permute-start | bytes 392 | tf_op jit(solution)/shard_map/ppermute | solution.py:267
  198.9 17.2 %collective-permute-start.19 = (bf16[2,128,512]{2,1,0:T(8,128)(2,1)S(1)}, bf16[2,128,512]{2,1,0:T(8,128)(2,1)S(1)}, u32[]{:S(2)}, u32[]{:S(2)}) collective-permute-start(bf16[2,128,512]{2,1,0:T(8,128)(2,1)S(1)} %get-tuple-element.37), channel_id=1, source_target_pairs={{2,0},{3,1},{4,2},{5,3},{6,4},{7,5},{8,6},{9,7},{10,8},{11,9},{12,... | collective-permute-start | bytes 786440 | tf_op jit(solution)/shard_map/ppermute | solution.py:257
  204.3 13.9 %collective-permute-start.20 = (bf16[2,128,512]{2,1,0:T(8,128)(2,1)S(1)}, bf16[2,128,512]{2,1,0:T(8,128)(2,1)S(1)}, u32[]{:S(2)}, u32[]{:S(2)}) collective-permute-start(bf16[2,128,512]{2,1,0:T(8,128)(2,1)S(1)} %get-tuple-element.40), channel_id=1, source_target_pairs={{4,0},{5,1},{6,2},{7,3},{8,4},{9,5},{10,6},{11,7},{12,8},{13,9},{1... | collective-permute-start | bytes 786440 | tf_op jit(solution)/shard_map/ppermute | solution.py:257
  208.9 15.4 %collective-permute-start.21 = (bf16[2,128,512]{2,1,0:T(8,128)(2,1)S(1)}, bf16[2,128,512]{2,1,0:T(8,128)(2,1)S(1)}, u32[]{:S(2)}, u32[]{:S(2)}) collective-permute-start(bf16[2,128,512]{2,1,0:T(8,128)(2,1)S(1)} %get-tuple-element.39), channel_id=1, source_target_pairs={{6,0},{7,1},{8,2},{9,3},{10,4},{11,5},{12,6},{13,7},{14,8},{15,9},... | collective-permute-start | bytes 786440 | tf_op jit(solution)/shard_map/ppermute | solution.py:257
  210.8 27.8 %collective-permute-start.22 = (bf16[2,128,512]{2,1,0:T(8,128)(2,1)S(1)}, bf16[2,128,512]{2,1,0:T(8,128)(2,1)S(1)}, u32[]{:S(2)}, u32[]{:S(2)}) collective-permute-start(bf16[2,128,512]{2,1,0:T(8,128)(2,1)S(1)} %get-tuple-element.38), channel_id=1, source_target_pairs={{8,0},{9,1},{10,2},{11,3},{12,4},{13,5},{14,6},{15,7},{24,16},{25,... | collective-permute-start | bytes 786440 | tf_op jit(solution)/shard_map/ppermute | solution.py:257
  214.2 25.6 %collective-permute-start.24 = (bf16[2,128,512]{2,1,0:T(8,128)(2,1)S(1)}, bf16[2,128,512]{2,1,0:T(8,128)(2,1)S(1)}, u32[]{:S(2)}, u32[]{:S(2)}) collective-permute-start(bf16[2,128,512]{2,1,0:T(8,128)(2,1)S(1)} %get-tuple-element.41), channel_id=1, source_target_pairs={{2,0},{3,1},{4,2},{5,3},{6,4},{7,5},{8,6},{9,7},{10,8},{11,9},{12,... | collective-permute-start | bytes 786440 | tf_op jit(solution)/shard_map/ppermute | solution.py:257
  216.1 27.2 %collective-permute-start.25 = (bf16[2,128,512]{2,1,0:T(8,128)(2,1)S(1)}, bf16[2,128,512]{2,1,0:T(8,128)(2,1)S(1)}, u32[]{:S(2)}, u32[]{:S(2)}) collective-permute-start(bf16[2,128,512]{2,1,0:T(8,128)(2,1)S(1)} %get-tuple-element.44), channel_id=1, source_target_pairs={{4,0},{5,1},{6,2},{7,3},{8,4},{9,5},{10,6},{11,7},{12,8},{13,9},{1... | collective-permute-start | bytes 786440 | tf_op jit(solution)/shard_map/ppermute | solution.py:257
  218.2 25.1 %collective-permute-start.26 = (bf16[2,128,512]{2,1,0:T(8,128)(2,1)S(1)}, bf16[2,128,512]{2,1,0:T(8,128)(2,1)S(1)}, u32[]{:S(2)}, u32[]{:S(2)}) collective-permute-start(bf16[2,128,512]{2,1,0:T(8,128)(2,1)S(1)} %get-tuple-element.43), channel_id=1, source_target_pairs={{6,0},{7,1},{8,2},{9,3},{10,4},{11,5},{12,6},{13,7},{14,8},{15,9},... | collective-permute-start | bytes 786440 | tf_op jit(solution)/shard_map/ppermute | solution.py:257
  224.2 25.4 %collective-permute-start.27 = (bf16[2,128,512]{2,1,0:T(8,128)(2,1)S(1)}, bf16[2,128,512]{2,1,0:T(8,128)(2,1)S(1)}, u32[]{:S(2)}, u32[]{:S(2)}) collective-permute-start(bf16[2,128,512]{2,1,0:T(8,128)(2,1)S(1)} %get-tuple-element.42), channel_id=1, source_target_pairs={{8,0},{9,1},{10,2},{11,3},{12,4},{13,5},{14,6},{15,7},{24,16},{25,... | collective-permute-start | bytes 786440 | tf_op jit(solution)/shard_map/ppermute | solution.py:257

commit v2 on v1

v2 whole, which is shorter than its diff:
```python
import functools
import math

import jax
import jax.numpy as jnp
from jax import lax
from jax.experimental import pallas as pl
from jax.experimental.pallas import tpu as pltpu
from jax.sharding import PartitionSpec as P

HEAD_WIDTH = 128
HQ = 32
KEY_HEADS = 4
QUERY_PER_KV = 8
TILE = 128
DOCS = 4
RELAY_COUNT = 2
LONGEST = 9
REACH = LONGEST // 2
ROWS = QUERY_PER_KV * TILE
KEY_COLS = KEY_HEADS * HEAD_WIDTH
QUERY_COLS = HQ * HEAD_WIDTH
SCALE = 1.0 / math.sqrt(HEAD_WIDTH)
LOG2E = 1.4426950408889634
HIDDEN = -1e30
GROUP = 3
SLOTS = -(-LONGEST // GROUP) * GROUP
PART = 1024


def dot(left, right, left_dim, right_dim):
    return lax.dot_general(
        left,
        right,
        (((left_dim,), (right_dim,)), ((), ())),
        preferred_element_type=jnp.float32,
    )


def attend_kernel(meta, sink, q_ref, g_ref, *refs):
    mine = refs[: REACH + 1]
    mate = refs[REACH + 1 : 2 * REACH + 2]
    refs = refs[2 * REACH + 2 :]
    if len(refs) > 16:
        refs = refs[2:]
    o_ref, dq_ref, even, odd, sink_part = refs[:5]
    kv, grads, q_turned, g_turned, q_rows, g_rows, scores, shares, out_sum, dq_sum = refs[5:15]
    (sems,) = refs[15:]
    in_sem, out_sem = sems.at[0], sems.at[1]
    head = pl.program_id(0)
    count = meta[0]
    core = meta[1]
    pairs = lax.div(count + GROUP - 1, GROUP)
    PAIR = GROUP * TILE

    def cols(j):
        return pl.ds(pl.multiple_of(j * HEAD_WIDTH, HEAD_WIDTH), HEAD_WIDTH)

    def fetch(j, slot, source):
        return pltpu.make_async_copy(
            source.at[:, :, cols(j)],
            kv.at[j, :, pl.ds(slot * TILE, TILE), :],
            in_sem.at[j, slot],
        )

    def give(j, slot):
        target = odd if slot % 2 else even
        return pltpu.make_async_copy(
            grads.at[j, :, pl.ds(slot * TILE, TILE), :],
            target.at[slot // 2, :, :, cols(j)],
            out_sem.at[j, slot],
        )

    @pl.when(head == 0)
    def _():
        for j in range(KEY_HEADS):
            for slot in range(LONGEST):

                @pl.when(count > slot)
                def _():
                    if slot % 2 == 0:
                        fetch(j, slot, mine[slot // 2]).start()
                    else:
                        near, far = mate[slot // 2], mate[slot // 2 + 1]
                        pl.when(core == 1)(lambda: fetch(j, slot, near).start())
                        pl.when(core == 0)(lambda: fetch(j, slot, far).start())

        for slot in range(1, SLOTS):

            @pl.when((slot >= count) & (slot < pairs * GROUP))
            def _():
                for j in range(KEY_HEADS):
                    kv[j, :, slot * TILE : (slot + 1) * TILE, :] = jnp.zeros(
                        (2, TILE, HEAD_WIDTH), jnp.bfloat16
                    )

    heads = [slice(i * HEAD_WIDTH, (i + 1) * HEAD_WIDTH) for i in range(QUERY_PER_KV)]
    parts = [slice(i * PART, (i + 1) * PART) for i in range(ROWS // PART)]
    for part in heads:
        q, g = q_ref[0, 0, :, part], g_ref[0, 0, :, part]
        q_rows[part, :] = q
        g_rows[part, :] = g
        q_turned[:, part] = q.T
        g_turned[:, part] = g.T

    for slot in range(LONGEST):
        pl.when(count > slot)(lambda: fetch(head, slot, mine[0]).wait())

    def block(pair):
        return pl.ds(pl.multiple_of(pair * PAIR, PAIR), PAIR)

    def hide_spare(pair, score):
        rows = [score[:TILE]]
        for i in range(1, GROUP):
            bias = jnp.where(GROUP * pair + i < count, 0.0, HIDDEN).astype(jnp.float32)
            rows.append(score[i * TILE : (i + 1) * TILE] + bias)
        return jnp.concatenate(rows, axis=0)

    row = lax.broadcasted_iota(jnp.int32, (TILE, TILE), 0)
    column = lax.broadcasted_iota(jnp.int32, (TILE, TILE), 1)
    seen = jnp.concatenate([row <= column] * (PART // TILE), axis=1)
    tops = []
    for part in parts:
        score = hide_spare(0, dot(kv[head, 0, :PAIR, :], q_turned[:, part], 1, 0))
        score = jnp.concatenate([jnp.where(seen, score[:TILE], HIDDEN), score[TILE:]], axis=0)
        scores[:PAIR, part] = score
        tops.append(jnp.max(score.reshape(-1, 8, PART), axis=0))

    def score_step(pair, tops):
        keys = kv[head, 0, block(pair), :]
        new = []
        for part, top in zip(parts, tops):
            score = hide_spare(pair, dot(keys, q_turned[:, part], 1, 0))
            scores[block(pair), part] = score
            new.append(jnp.maximum(top, jnp.max(score.reshape(-1, 8, PART), axis=0)))
        return tuple(new)

    tops = lax.fori_loop(1, pairs, score_step, tuple(tops))
    logit = jnp.concatenate(
        [
            jnp.full((1, TILE), sink[head * QUERY_PER_KV + i] * LOG2E, jnp.float32)
            for i in range(QUERY_PER_KV)
        ],
        axis=1,
    )
    logits = [logit[:, part] for part in parts]
    tops = [
        jnp.maximum(jnp.max(top, axis=0, keepdims=True) * (SCALE * LOG2E), one)
        for top, one in zip(tops, logits)
    ]

    out_sum[...] = jnp.zeros_like(out_sum)
    dq_sum[...] = jnp.zeros_like(dq_sum)
    ones = jnp.ones((16, PAIR), jnp.bfloat16)

    def share_step(pair, carry):
        turned = jnp.concatenate([kv[head, 1, block(pair), :].T, ones], axis=0)
        for part, top in zip(parts, tops):
            low = jnp.exp2(scores[block(pair), part] * (SCALE * LOG2E) - top).astype(jnp.bfloat16)
            shares[block(pair), part] = low
            out_sum[:, part] += dot(turned, low, 1, 0)
        return carry

    lax.fori_loop(0, pairs, share_step, 0)
    inverses, deltas = [], []
    for i, part in enumerate(parts):
        sink_raised = jnp.exp2(logits[i] - tops[i])
        inverse = 1.0 / (out_sum[HEAD_WIDTH : HEAD_WIDTH + 1, part] + sink_raised)
        out = (out_sum[:HEAD_WIDTH, part] * inverse).astype(jnp.bfloat16)
        delta = jnp.sum(
            out.astype(jnp.float32) * g_turned[:, part].astype(jnp.float32), axis=0, keepdims=True
        )
        sink_rows = sink_raised * inverse * delta
        for k in range(PART // TILE):
            h = i * (PART // TILE) + k
            inner = slice(k * TILE, (k + 1) * TILE)
            o_ref[0, 0, :, heads[h]] = out[:, inner].T
            sink_part[0, h : h + 1, :] = jnp.broadcast_to(
                -jnp.sum(sink_rows[:, inner], axis=1, keepdims=True), (1, HEAD_WIDTH)
            )
        inverses.append(inverse)
        deltas.append(delta)

    def grad_step(pair, carry):
        keys = kv[head, 0, block(pair), :]
        values = kv[head, 1, block(pair), :]
        turned = keys.T
        key_grad = value_grad = None
        for i, part in enumerate(parts):
            share = shares[block(pair), part].astype(jnp.float32) * inverses[i]
            share_grad = dot(values, g_turned[:, part], 1, 0)
            score_grad = (share * (share_grad - deltas[i])).astype(jnp.bfloat16)
            dq_sum[:, part] += dot(turned, score_grad, 1, 0)
            one = dot(score_grad, q_rows[part, :], 1, 0)
            two = dot(share.astype(jnp.bfloat16), g_rows[part, :], 1, 0)
            key_grad = one if key_grad is None else key_grad + one
            value_grad = two if value_grad is None else value_grad + two
        grads[head, 0, block(pair), :] = (key_grad * SCALE).astype(jnp.bfloat16)
        grads[head, 1, block(pair), :] = value_grad.astype(jnp.bfloat16)
        return carry

    lax.fori_loop(0, pairs, grad_step, 0)
    for slot in range(LONGEST):
        pl.when(count > slot)(lambda: give(head, slot).start())
    for part in heads:
        dq_ref[0, 0, :, part] = (dq_sum[:, part] * SCALE).astype(jnp.bfloat16).T

    @pl.when(head == KEY_HEADS - 1)
    def _():
        for j in range(KEY_HEADS):
            for slot in range(LONGEST):
                pl.when(count > slot)(lambda: give(j, slot).wait())


def attend(relay, meta, sink, queries, output_gradient, mine, mate, filled):
    wide = pl.BlockSpec((1, 1, TILE, QUERY_PER_KV * HEAD_WIDTH), lambda j: (relay, 0, 0, j))
    smem = pl.BlockSpec(memory_space=pltpu.SMEM)
    whole = pl.BlockSpec(memory_space=pl.ANY)
    low = jnp.bfloat16
    first = 4 + len(mine) + len(mate)
    piece = (2, TILE, KEY_COLS)
    return pl.pallas_call(
        attend_kernel,
        grid=(KEY_HEADS,),
        in_specs=[smem, smem, wide, wide] + [whole] * (len(mine) + len(mate) + len(filled)),
        out_specs=[
            wide,
            wide,
            whole,
            whole,
            pl.BlockSpec((1, QUERY_PER_KV, HEAD_WIDTH), lambda j: (j, 0, 0)),
        ],
        out_shape=[
            jax.ShapeDtypeStruct((RELAY_COUNT, 1, TILE, QUERY_COLS), low),
            jax.ShapeDtypeStruct((RELAY_COUNT, 1, TILE, QUERY_COLS), low),
            jax.ShapeDtypeStruct((REACH + 1,) + piece, low),
            jax.ShapeDtypeStruct((REACH,) + piece, low),
            jax.ShapeDtypeStruct((KEY_HEADS, QUERY_PER_KV, HEAD_WIDTH), jnp.float32),
        ],
        scratch_shapes=[
            pltpu.VMEM((KEY_HEADS, 2, SLOTS * TILE, HEAD_WIDTH), low),
            pltpu.VMEM((KEY_HEADS, 2, SLOTS * TILE, HEAD_WIDTH), low),
            pltpu.VMEM((HEAD_WIDTH, ROWS), low),
            pltpu.VMEM((HEAD_WIDTH, ROWS), low),
            pltpu.VMEM((ROWS, HEAD_WIDTH), low),
            pltpu.VMEM((ROWS, HEAD_WIDTH), low),
            pltpu.VMEM((SLOTS * TILE, ROWS), jnp.float32),
            pltpu.VMEM((SLOTS * TILE, ROWS), low),
            pltpu.VMEM((HEAD_WIDTH + 16, ROWS), jnp.float32),
            pltpu.VMEM((HEAD_WIDTH, ROWS), jnp.float32),
            pltpu.SemaphoreType.DMA((2, KEY_HEADS, LONGEST)),
        ],
        input_output_aliases={first + i: i for i in range(len(filled))},
        compiler_params=pltpu.CompilerParams(vmem_limit_bytes=36 * 1024 * 1024),
        cost_estimate=pl.CostEstimate(
            flops=12 * LONGEST * HQ * TILE * TILE * HEAD_WIDTH * 4,
            bytes_accessed=9 << 20,
            transcendentals=LONGEST * HQ * TILE * TILE,
        ),
        name=f"attend_{relay}",
    )(meta, sink, queries, output_gradient, *mine, *mate, *filled)


def shards(queries, keys, values, output_gradient, doc_tiles, sink_logits):
    ctx_count = lax.axis_size("ctx")
    ctx_pos = lax.axis_index("ctx")
    section_pos = lax.axis_index("section")
    section_count = lax.axis_size("section")
    core = lax.rem(ctx_pos, 2)

    def back(amount):
        return [(c, c - amount) for c in range(ctx_count) if 0 <= c - amount < ctx_count]

    def other(moving):
        return [(c, c ^ 1) for c in range(ctx_count) if moving(c)]

    def seen_by(position):
        counts = []
        for relay in range(RELAY_COUNT):
            end = start = jnp.zeros((), jnp.int32)
            for document in range(DOCS):
                end = end + doc_tiles[relay, 0, document]
                start = jnp.where(end <= position, end, start)
            counts.append(position - start + 1)
        return counts

    counts = seen_by(ctx_pos)
    mate_counts = seen_by(ctx_pos + 1 - 2 * core)

    def sink_of(relay):
        layer = section_pos if relay == 0 else section_count - 1 - section_pos
        return lax.dynamic_index_in_dim(sink_logits, layer, 0, keepdims=False)

    def meta_of(relay):
        return jnp.stack([counts[relay], core]).astype(jnp.int32)

    def fetched(piece):
        return [piece] + [
            lax.ppermute(piece, "ctx", back(-2 * distance)) for distance in range(1, REACH + 1)
        ]

    def swapped(pieces):
        return [lax.ppermute(piece, "ctx", other(lambda c: True)) for piece in pieces]

    def chip_terms(relay, even, odd):
        from_mate = lax.ppermute(odd, "ctx", other(lambda c: True))
        terms = []
        for distance in range(REACH + 1):
            theirs = distance - core
            known = (theirs >= 0) & (theirs < REACH) & (mate_counts[relay] > 2 * theirs + 1)
            own = even[distance].astype(jnp.float32)
            added = lax.dynamic_index_in_dim(
                from_mate, jnp.clip(theirs, 0, REACH - 1), 0, keepdims=False
            ).astype(jnp.float32)
            term = jnp.where(counts[relay] > 2 * distance, own, 0.0) + jnp.where(known, added, 0.0)
            terms.append(term if distance == 0 else term.astype(jnp.bfloat16))
        return terms

    def returned(terms):
        return [
            lax.ppermute(terms[distance], "ctx", back(2 * distance))
            for distance in range(1, REACH + 1)
        ]

    def summed(own, others):
        for other_term in others:
            own = own + other_term.astype(jnp.float32)
        return own.astype(jnp.bfloat16)

    first, second = 1, 0
    pieces = [jnp.stack([keys[r, 0], values[r, 0]]) for r in range(RELAY_COUNT)]
    mine_first = fetched(pieces[first])
    own_swapped = swapped([pieces[second]])
    mine_second = fetched(pieces[second])
    attention, query_grad, even, odd, sink_part = attend(
        first,
        meta_of(first),
        sink_of(first),
        queries,
        output_gradient,
        mine_first,
        swapped(mine_first),
        [],
    )
    mine_second, sink_part, odd = lax.optimization_barrier((mine_second, sink_part, odd))
    terms_first = chip_terms(first, even, odd)
    mate_second = own_swapped + swapped(mine_second[1:])
    mirrored = lax.ppermute(
        sink_part[:, :, 0].reshape(HQ),
        "section",
        [(s, section_count - 1 - s) for s in range(section_count)],
    )
    meta, mate_second, mirrored, terms_first = lax.optimization_barrier(
        (meta_of(second), mate_second, mirrored, terms_first)
    )
    sent_first = returned(terms_first)
    attention, query_grad, even, odd, sink_part = attend(
        second,
        meta,
        sink_of(second),
        queries,
        output_gradient,
        mine_second,
        mate_second,
        [attention, query_grad],
    )
    sent_first, sink_part, odd = lax.optimization_barrier((sent_first, sink_part, odd))
    terms_second = chip_terms(second, even, odd)
    sink_grad = sink_part[:, :, 0].reshape(HQ) + mirrored
    sink_grad, terms_second = lax.optimization_barrier((sink_grad, terms_second))
    sent_second = returned(terms_second)
    step = 1
    while step < ctx_count:
        sink_grad = sink_grad + lax.ppermute(
            sink_grad, "ctx", [(c, c ^ step) for c in range(ctx_count)]
        )
        step *= 2
    first_sum = summed(terms_first[0], sent_first)
    sent_second, sink_grad, first_sum = lax.optimization_barrier(
        (sent_second, sink_grad, first_sum)
    )
    second_sum = summed(terms_second[0], sent_second)
    key_gradient = jnp.stack([second_sum[0], first_sum[0]])[:, None]
    value_gradient = jnp.stack([second_sum[1], first_sum[1]])[:, None]
    return (attention, query_grad, key_gradient, value_gradient, sink_grad[None])


def solution(mesh):
    placed = (
        P(None, "section", "ctx", None),
        P(None, "section", "ctx", None),
        P(None, "section", "ctx", None),
        P(None, "section", "ctx", None),
        P(None, "section", None),
        P(),
    )
    return jax.shard_map(
        shards,
        mesh=mesh,
        in_specs=placed,
        out_specs=(
            P(None, "section", "ctx", None),
            P(None, "section", "ctx", None),
            P(None, "section", "ctx", None),
            P(None, "section", "ctx", None),
            P("section", None),
        ),
        check_vma=False,
    )
```

time: 255 us -> 176 us (0.69)
  the two profiles are of different devices: /device:TPU:12 before, /device:TPU:45 now
where the time goes in v2:
time: 176 us; the launch traced here: 175 us
  starting transfers between devices  84.7 us (48%)
  Pallas kernels  25.6 us (15%)
  local copies, waits for them, and re-layouts  23.2 us (13%)
  waiting for transfers between devices  21.4 us (12%)
  between operations  11.5 us (7%)
  other arithmetic  8.9 us (5%)
    pallas_call x2, Pallas kernels, attend(): pl.pallas_call(attend_kernel, grid=(KEY_HEADS,), in_specs=[smem, smem, wi...  25.6 us
    ppermute x8, starting transfers between devices, fetched(): lax.ppermute(piece, 'ctx', back(-2 * distance))  24.7 us
    ppermute x4, starting transfers between devices, shards(): lax.ppermute(sink_grad, 'ctx', [(c, c ^ step) for c in range(ctx_count)])  21.3 us
    unnamed x70, local copies, waits for them, and re-layouts  19.4 us
    ppermute x1, starting transfers between devices, shards(): lax.ppermute(sink_part[:, :, 0].reshape(HQ), 'section', [(s, section_coun...  17.5 us
    ppermute x8, starting transfers between devices, returned(): lax.ppermute(terms[distance], 'ctx', back(2 * distance))  14.3 us
    ppermute x4, waiting for transfers between devices, shards(): lax.ppermute(sink_grad, 'ctx', [(c, c ^ step) for c in range(ctx_count)])  10.4 us
    ppermute x8, waiting for transfers between devices, returned(): lax.ppermute(terms[distance], 'ctx', back(2 * distance))  6.51 us
  transfers between devices with their start and end apart: 33, of which 6 were waited for; matrix products, arithmetic and copies ran while one was open for 4% of the time, Pallas kernels for 15%

profile of v2, /device:TPU:45, one launch (start us, length us, event | category | flops | bytes accessed | tf_op | source)
XLA Modules:
  0.0 175.2 jit_solution(18237873504089453414)
XLA Ops:
  0.6 1.1 slice_bitcast_fusion
  1.8 3.9 %collective-permute-start.8 = (bf16[2,128,512]{2,1,0:T(8,128)(2,1)S(1)}, bf16[2,128,512]{2,1,0:T(8,128)(2,1)S(1)}, u32[]{:S(2)}, u32[]{:S(2)}) collective-permute-start(bf16[2,128,512]{2,1,0:T(8,128)(2,1)S(1)} %pad_maximum_fusion.1.refs_0_), channel_id=1, source_target_pairs={{0,8},{1,9},{2,10},{3,11},{4,12},{5,13},{6,14},{7,15},{16,24},{17,... | collective-permute-start | bytes 786440 | tf_op jit(solution)/shard_map/ppermute | solution.py:299
  5.7 1.9 %collective-permute-start.7 = (bf16[2,128,512]{2,1,0:T(8,128)(2,1)S(1)}, bf16[2,128,512]{2,1,0:T(8,128)(2,1)S(1)}, u32[]{:S(2)}, u32[]{:S(2)}) collective-permute-start(bf16[2,128,512]{2,1,0:T(8,128)(2,1)S(1)} %pad_maximum_fusion.1.refs_0_), channel_id=1, source_target_pairs={{0,6},{1,7},{2,8},{3,9},{4,10},{5,11},{6,12},{7,13},{8,14},{9,15},... | collective-permute-start | bytes 786440 | tf_op jit(solution)/shard_map/ppermute | solution.py:299
  7.7 1.9 %collective-permute-start.6 = (bf16[2,128,512]{2,1,0:T(8,128)(2,1)S(1)}, bf16[2,128,512]{2,1,0:T(8,128)(2,1)S(1)}, u32[]{:S(2)}, u32[]{:S(2)}) collective-permute-start(bf16[2,128,512]{2,1,0:T(8,128)(2,1)S(1)} %pad_maximum_fusion.1.refs_0_), channel_id=1, source_target_pairs={{0,4},{1,5},{2,6},{3,7},{4,8},{5,9},{6,10},{7,11},{8,12},{9,13},{1... | collective-permute-start | bytes 786440 | tf_op jit(solution)/shard_map/ppermute | solution.py:299
  9.6 4.0 %collective-permute-start.5 = (bf16[2,128,512]{2,1,0:T(8,128)(2,1)S(1)}, bf16[2,128,512]{2,1,0:T(8,128)(2,1)S(1)}, u32[]{:S(2)}, u32[]{:S(2)}) collective-permute-start(bf16[2,128,512]{2,1,0:T(8,128)(2,1)S(1)} %pad_maximum_fusion.1.refs_0_), channel_id=1, source_target_pairs={{0,2},{1,3},{2,4},{3,5},{4,6},{5,7},{6,8},{7,9},{8,10},{9,11},{10,... | collective-permute-start | bytes 786440 | tf_op jit(solution)/shard_map/ppermute | solution.py:299
  13.6 1.3 collective-permute-start.9
  14.9 1.5 fusion.12
  20.6 0.5 collective-permute-start.12
  21.0 3.5 %collective-permute-done.6.refs_2_ = bf16[2,128,512]{2,1,0:T(8,128)(2,1)S(1)} collective-permute-done((bf16[2,128,512]{2,1,0:T(8,128)(2,1)S(1)}, bf16[2,128,512]{2,1,0:T(8,128)(2,1)S(1)}, u32[]{:S(2)}, u32[]{:S(2)}) %collective-permute-start.6) | collective-permute-done | bytes 262176 | tf_op jit(solution)/shard_map/ppermute | solution.py:299
  24.5 1.5 collective-permute-start.11
  26.1 0.7 copy-done.12
  26.8 0.7 copy-done.14
  27.6 0.8 fusion.9
  28.4 0.7 copy-done.16
  29.1 1.3 collective-permute-start.4
  30.4 0.7 copy-done.18
  31.1 1.9 %collective-permute-start.3 = (bf16[2,128,512]{2,1,0:T(8,128)(2,1)S(1)}, bf16[2,128,512]{2,1,0:T(8,128)(2,1)S(1)}, u32[]{:S(2)}, u32[]{:S(2)}) collective-permute-start(bf16[2,128,512]{2,1,0:T(8,128)(2,1)S(1)} %pad_maximum_fusion.refs_0_), channel_id=1, source_target_pairs={{0,6},{1,7},{2,8},{3,9},{4,10},{5,11},{6,12},{7,13},{8,14},{9,15},... | collective-permute-start | bytes 786440 | tf_op jit(solution)/shard_map/ppermute | solution.py:299
  33.0 0.7 copy-done.20
  33.7 1.9 %collective-permute-start.2 = (bf16[2,128,512]{2,1,0:T(8,128)(2,1)S(1)}, bf16[2,128,512]{2,1,0:T(8,128)(2,1)S(1)}, u32[]{:S(2)}, u32[]{:S(2)}) collective-permute-start(bf16[2,128,512]{2,1,0:T(8,128)(2,1)S(1)} %pad_maximum_fusion.refs_0_), channel_id=1, source_target_pairs={{0,4},{1,5},{2,6},{3,7},{4,8},{5,9},{6,10},{7,11},{8,12},{9,13},{1... | collective-permute-start | bytes 786440 | tf_op jit(solution)/shard_map/ppermute | solution.py:299
  35.6 0.7 copy-done.22
  36.3 7.8 %collective-permute-start.1 = (bf16[2,128,512]{2,1,0:T(8,128)(2,1)S(1)}, bf16[2,128,512]{2,1,0:T(8,128)(2,1)S(1)}, u32[]{:S(2)}, u32[]{:S(2)}) collective-permute-start(bf16[2,128,512]{2,1,0:T(8,128)(2,1)S(1)} %pad_maximum_fusion.refs_0_), channel_id=1, source_target_pairs={{0,2},{1,3},{2,4},{3,5},{4,6},{5,7},{6,8},{7,9},{8,10},{9,11},{10,... | collective-permute-start | bytes 786440 | tf_op jit(solution)/shard_map/ppermute | solution.py:299
  44.2 0.7 copy-done.24
  44.9 1.6 copy-done
  46.5 1.6 copy-done.2
  48.1 0.9 copy-done.9
  49.0 0.9 copy-done.11
  50.0 0.9 copy-done.13
  50.9 0.9 copy-done.15
  51.9 0.9 copy-done.17
  52.8 0.9 copy-done.19
  53.8 0.9 copy-done.21
  54.7 0.9 copy-done.23
  55.7 0.9 copy-done.25
  56.6 12.8 %attend_1.1 = (bf16[2,1,128,4096]{3,2,1,0:T(8,128)(2,1)}, bf16[2,1,128,4096]{3,2,1,0:T(8,128)(2,1)}, bf16[5,2,128,512]{3,2,1,0:T(8,128)(2,1)S(1)}, bf16[4,2,128,512]{3,2,1,0:T(8,128)(2,1)S(1)}, f32[4,8,128]{2,1,0:T(8,128)S(1)}) custom-call(s32[2]{0:T(128)S(1)} %pad_add_fusion.1.meta, f32[32]{0:T(128)S(1)} %get-tuple-element.126.sink, ...), custom_call_target="tpu_custom_call" | custom-call | flops 28991029248 | bytes 9437184 | tf_op jit(solution)/shard_map/attend_1/pallas_call | solution.py:222
  69.5 0.8 collective-permute-start.19
  70.3 0.7 collective-permute-start
  76.3 0.5 collective-permute-start.15
  77.3 1.7 fusion.3
  79.1 17.5 %collective-permute-start.18 = (f32[32]{0:T(128)S(1)}, f32[32]{0:T(128)S(1)}, u32[]{:S(2)}, u32[]{:S(2)}) collective-permute-start(f32[32]{0:T(128)S(1)} %reshape_squeeze.6), channel_id=1, source_target_pairs={{0,112},{16,96},{32,80},{48,64},{64,48},{80,32},{96,16},{112,0},{1... | collective-permute-start | bytes 392 | tf_op jit(solution)/shard_map/ppermute | solution.py:348
  96.6 1.8 %add_bitcast_fusion.1 = f32[2,128,512]{2,1,0:T(8,128)} fusion(bf16[4,2,128,512]{3,2,1,0:T(8,128)(2,1)} %collective-permute-done.19, s32[]{:T(128)S(6)} %min.21, bf16[5,2,128,512]{3,2,1,0:T(8,128)(2,1)S(1)} %get-tuple-element.59, pred[]{:T(512)S(6)} %and.54, pred[]{:T(512)S(6)} %gt.60), kind=kLoop, calls=%fused_computation.11 | loop fusion | flops 655360 | bytes 1048582 | tf_op jit(solution)/shard_map/add | solution.py:315
  98.5 1.9 %collective-permute-start.20 = (bf16[2,128,512]{2,1,0:T(8,128)(2,1)S(1)}, bf16[2,128,512]{2,1,0:T(8,128)(2,1)S(1)}, u32[]{:S(2)}, u32[]{:S(2)}) collective-permute-start(bf16[2,128,512]{2,1,0:T(8,128)(2,1)S(1)} %get-tuple-element.72), channel_id=1, source_target_pairs={{2,0},{3,1},{4,2},{5,3},{6,4},{7,5},{8,6},{9,7},{10,8},{11,9},{12,... | collective-permute-start | bytes 786440 | tf_op jit(solution)/shard_map/ppermute | solution.py:321
  100.4 1.9 %collective-permute-start.21 = (bf16[2,128,512]{2,1,0:T(8,128)(2,1)S(1)}, bf16[2,128,512]{2,1,0:T(8,128)(2,1)S(1)}, u32[]{:S(2)}, u32[]{:S(2)}) collective-permute-start(bf16[2,128,512]{2,1,0:T(8,128)(2,1)S(1)} %get-tuple-element.73), channel_id=1, source_target_pairs={{4,0},{5,1},{6,2},{7,3},{8,4},{9,5},{10,6},{11,7},{12,8},{13,9},{1... | collective-permute-start | bytes 786440 | tf_op jit(solution)/shard_map/ppermute | solution.py:321
  102.3 1.9 %collective-permute-start.22 = (bf16[2,128,512]{2,1,0:T(8,128)(2,1)S(1)}, bf16[2,128,512]{2,1,0:T(8,128)(2,1)S(1)}, u32[]{:S(2)}, u32[]{:S(2)}) collective-permute-start(bf16[2,128,512]{2,1,0:T(8,128)(2,1)S(1)} %get-tuple-element.74), channel_id=1, source_target_pairs={{6,0},{7,1},{8,2},{9,3},{10,4},{11,5},{12,6},{13,7},{14,8},{15,9},... | collective-permute-start | bytes 786440 | tf_op jit(solution)/shard_map/ppermute | solution.py:321
  104.3 1.5 collective-permute-start.23
  105.8 0.9 copy-done.5
  106.7 0.9 copy-done.7
  107.7 12.7 %attend_0.1 = (bf16[2,1,128,4096]{3,2,1,0:T(8,128)(2,1)}, bf16[2,1,128,4096]{3,2,1,0:T(8,128)(2,1)}, bf16[5,2,128,512]{3,2,1,0:T(8,128)(2,1)S(1)}, bf16[4,2,128,512]{3,2,1,0:T(8,128)(2,1)S(1)}, f32[4,8,128]{2,1,0:T(8,128)S(1)}) custom-call(s32[2]{0:T(128)S(1)} %pad_add_fusion.meta, ...), custom_call_target="tpu_custom_call", output_to_operand_aliasing={{0}: (14, {}), {1}: (15, {})} | custom-call | flops 28991029248 | bytes 9437184 | tf_op jit(solution)/shard_map/attend_0/pallas_call | solution.py:222
  120.4 6.5 %collective-permute-done.21 = bf16[2,128,512]{2,1,0:T(8,128)(2,1)S(1)} collective-permute-done((bf16[2,128,512]{2,1,0:T(8,128)(2,1)S(1)}, bf16[2,128,512]{2,1,0:T(8,128)(2,1)S(1)}, u32[]{:S(2)}, u32[]{:S(2)}) %collective-permute-start.21) | collective-permute-done | bytes 262176 | tf_op jit(solution)/shard_map/ppermute | solution.py:321
  127.0 0.7 copy-done.29
  127.8 0.9 collective-permute-start.24
  130.1 1.0 collective-permute-done.24
  131.2 1.2 add_bitcast_fusion
  132.3 1.6 fusion.7
  134.4 1.9 %collective-permute-start.25 = (bf16[2,128,512]{2,1,0:T(8,128)(2,1)S(1)}, bf16[2,128,512]{2,1,0:T(8,128)(2,1)S(1)}, u32[]{:S(2)}, u32[]{:S(2)}) collective-permute-start(bf16[2,128,512]{2,1,0:T(8,128)(2,1)S(1)} %get-tuple-element.83), channel_id=1, source_target_pairs={{2,0},{3,1},{4,2},{5,3},{6,4},{7,5},{8,6},{9,7},{10,8},{11,9},{12,... | collective-permute-start | bytes 786440 | tf_op jit(solution)/shard_map/ppermute | solution.py:321
  136.3 1.9 %collective-permute-start.26 = (bf16[2,128,512]{2,1,0:T(8,128)(2,1)S(1)}, bf16[2,128,512]{2,1,0:T(8,128)(2,1)S(1)}, u32[]{:S(2)}, u32[]{:S(2)}) collective-permute-start(bf16[2,128,512]{2,1,0:T(8,128)(2,1)S(1)} %get-tuple-element.84), channel_id=1, source_target_pairs={{4,0},{5,1},{6,2},{7,3},{8,4},{9,5},{10,6},{11,7},{12,8},{13,9},{1... | collective-permute-start | bytes 786440 | tf_op jit(solution)/shard_map/ppermute | solution.py:321
  138.4 1.9 %collective-permute-start.27 = (bf16[2,128,512]{2,1,0:T(8,128)(2,1)S(1)}, bf16[2,128,512]{2,1,0:T(8,128)(2,1)S(1)}, u32[]{:S(2)}, u32[]{:S(2)}) collective-permute-start(bf16[2,128,512]{2,1,0:T(8,128)(2,1)S(1)} %get-tuple-element.85), channel_id=1, source_target_pairs={{6,0},{7,1},{8,2},{9,3},{10,4},{11,5},{12,6},{13,7},{14,8},{15,9},... | collective-permute-start | bytes 786440 | tf_op jit(solution)/shard_map/ppermute | solution.py:321
  140.3 2.2 %collective-permute-done.30 = f32[32]{0:T(128)S(1)} collective-permute-done((f32[32]{0:T(128)S(1)}, f32[32]{0:T(128)S(1)}, u32[]{:S(2)}, u32[]{:S(2)}) %collective-permute-start.30) | collective-permute-done | bytes 160 | tf_op jit(solution)/shard_map/ppermute | solution.py:374
  142.6 1.3 collective-permute-start.28
  143.8 2.0 %collective-permute-done.31 = f32[32]{0:T(128)S(1)} collective-permute-done((f32[32]{0:T(128)S(1)}, f32[32]{0:T(128)S(1)}, u32[]{:S(2)}, u32[]{:S(2)}) %collective-permute-start.31) | collective-permute-done | bytes 160 | tf_op jit(solution)/shard_map/ppermute | solution.py:374
  145.9 20.8 %collective-permute-start.32 = (f32[32]{0:T(128)S(1)}, f32[32]{0:T(128)S(1)}, u32[]{:S(2)}, u32[]{:S(2)}) collective-permute-start(f32[32]{0:T(128)S(1)} %add.194), channel_id=1, source_target_pairs={{0,8},{1,9},{2,10},{3,11},{4,12},{5,13},{6,14},{7,15},{8,0},{9,1},... | collective-permute-start | bytes 392 | tf_op jit(solution)/shard_map/ppermute | solution.py:374
  166.8 6.1 %collective-permute-done.32 = f32[32]{0:T(128)S(1)} collective-permute-done((f32[32]{0:T(128)S(1)}, f32[32]{0:T(128)S(1)}, u32[]{:S(2)}, u32[]{:S(2)}) %collective-permute-start.32) | collective-permute-done | bytes 160 | tf_op jit(solution)/shard_map/ppermute | solution.py:374
  172.9 0.5 add.195
  173.7 0.7 maximum_bitcast_fusion.1
  174.5 0.7 maximum_bitcast_fusion
  (100 shorter events, 2.5 us)
Async XLA Ops:
  1.8 18.6 %collective-permute-start.8 = (bf16[2,128,512]{2,1,0:T(8,128)(2,1)S(1)}, bf16[2,128,512]{2,1,0:T(8,128)(2,1)S(1)}, u32[]{:S(2)}, u32[]{:S(2)}) collective-permute-start(bf16[2,128,512]{2,1,0:T(8,128)(2,1)S(1)} %pad_maximum_fusion.1.refs_0_), channel_id=1, source_target_pairs={{0,8},{1,9},{2,10},{3,11},{4,12},{5,13},{6,14},{7,15},{16,24},{17,... | collective-permute-start | bytes 786440 | tf_op jit(solution)/shard_map/ppermute | solution.py:299
  5.7 14.8 %collective-permute-start.7 = (bf16[2,128,512]{2,1,0:T(8,128)(2,1)S(1)}, bf16[2,128,512]{2,1,0:T(8,128)(2,1)S(1)}, u32[]{:S(2)}, u32[]{:S(2)}) collective-permute-start(bf16[2,128,512]{2,1,0:T(8,128)(2,1)S(1)} %pad_maximum_fusion.1.refs_0_), channel_id=1, source_target_pairs={{0,6},{1,7},{2,8},{3,9},{4,10},{5,11},{6,12},{7,13},{8,14},{9,15},... | collective-permute-start | bytes 786440 | tf_op jit(solution)/shard_map/ppermute | solution.py:299
  7.7 16.8 %collective-permute-start.6 = (bf16[2,128,512]{2,1,0:T(8,128)(2,1)S(1)}, bf16[2,128,512]{2,1,0:T(8,128)(2,1)S(1)}, u32[]{:S(2)}, u32[]{:S(2)}) collective-permute-start(bf16[2,128,512]{2,1,0:T(8,128)(2,1)S(1)} %pad_maximum_fusion.1.refs_0_), channel_id=1, source_target_pairs={{0,4},{1,5},{2,6},{3,7},{4,8},{5,9},{6,10},{7,11},{8,12},{9,13},{1... | collective-permute-start | bytes 786440 | tf_op jit(solution)/shard_map/ppermute | solution.py:299
  9.6 17.2 %collective-permute-start.5 = (bf16[2,128,512]{2,1,0:T(8,128)(2,1)S(1)}, bf16[2,128,512]{2,1,0:T(8,128)(2,1)S(1)}, u32[]{:S(2)}, u32[]{:S(2)}) collective-permute-start(bf16[2,128,512]{2,1,0:T(8,128)(2,1)S(1)} %pad_maximum_fusion.1.refs_0_), channel_id=1, source_target_pairs={{0,2},{1,3},{2,4},{3,5},{4,6},{5,7},{6,8},{7,9},{8,10},{9,11},{10,... | collective-permute-start | bytes 786440 | tf_op jit(solution)/shard_map/ppermute | solution.py:299
  13.6 14.8 %collective-permute-start.9 = (bf16[2,128,512]{2,1,0:T(8,128)(2,1)S(1)}, bf16[2,128,512]{2,1,0:T(8,128)(2,1)S(1)}, u32[]{:S(2)}, u32[]{:S(2)}) collective-permute-start(bf16[2,128,512]{2,1,0:T(8,128)(2,1)S(1)} %pad_maximum_fusion.1.refs_0_), channel_id=1, source_target_pairs={{0,1},{1,0},{2,3},{3,2},{4,5},{5,4},{6,7},{7,6},{8,9},{9,8},{10,11... | collective-permute-start | bytes 786440 | tf_op jit(solution)/shard_map/ppermute | solution.py:303
  20.4 9.9 %copy-start.8 = (bf16[2,128,512]{2,1,0:T(8,128)(2,1)}, bf16[2,128,512]{2,1,0:T(8,128)(2,1)S(1)}, u32[]{:S(2)}) copy-start(bf16[2,128,512]{2,1,0:T(8,128)(2,1)S(1)} %collective-permute-done.8.refs_4_) | copy-start | bytes 786436
  20.5 9.9 %collective-permute-start.13 = (bf16[2,128,512]{2,1,0:T(8,128)(2,1)S(1)}, bf16[2,128,512]{2,1,0:T(8,128)(2,1)S(1)}, u32[]{:S(2)}, u32[]{:S(2)}) collective-permute-start(bf16[2,128,512]{2,1,0:T(8,128)(2,1)S(1)} %collective-permute-done.8.refs_4_), channel_id=1, source_target_pairs={{0,1},{1,0},{2,3},{3,2},{4,5},{5,4},{6,7},{7,6},{8,9},{9,8},{10,11... | collective-permute-start | bytes 786440 | tf_op jit(solution)/shard_map/ppermute | solution.py:303
  20.6 23.6 %copy-start.10 = (bf16[2,128,512]{2,1,0:T(8,128)(2,1)}, bf16[2,128,512]{2,1,0:T(8,128)(2,1)S(1)}, u32[]{:S(2)}) copy-start(bf16[2,128,512]{2,1,0:T(8,128)(2,1)S(1)} %collective-permute-done.7.refs_3_) | copy-start | bytes 786436
  20.6 12.4 %collective-permute-start.12 = (bf16[2,128,512]{2,1,0:T(8,128)(2,1)S(1)}, bf16[2,128,512]{2,1,0:T(8,128)(2,1)S(1)}, u32[]{:S(2)}, u32[]{:S(2)}) collective-permute-start(bf16[2,128,512]{2,1,0:T(8,128)(2,1)S(1)} %collective-permute-done.7.refs_3_), channel_id=1, source_target_pairs={{0,1},{1,0},{2,3},{3,2},{4,5},{5,4},{6,7},{7,6},{8,9},{9,8},{10,11... | collective-permute-start | bytes 786440 | tf_op jit(solution)/shard_map/ppermute | solution.py:303
  24.5 11.1 %collective-permute-start.11 = (bf16[2,128,512]{2,1,0:T(8,128)(2,1)S(1)}, bf16[2,128,512]{2,1,0:T(8,128)(2,1)S(1)}, u32[]{:S(2)}, u32[]{:S(2)}) collective-permute-start(bf16[2,128,512]{2,1,0:T(8,128)(2,1)S(1)} %collective-permute-done.6.refs_2_), channel_id=1, source_target_pairs={{0,1},{1,0},{2,3},{3,2},{4,5},{5,4},{6,7},{7,6},{8,9},{9,8},{10,11... | collective-permute-start | bytes 786440 | tf_op jit(solution)/shard_map/ppermute | solution.py:303
  26.1 0.7 copy-start.12
  26.8 17.4 %collective-permute-start.10 = (bf16[2,128,512]{2,1,0:T(8,128)(2,1)S(1)}, bf16[2,128,512]{2,1,0:T(8,128)(2,1)S(1)}, u32[]{:S(2)}, u32[]{:S(2)}) collective-permute-start(bf16[2,128,512]{2,1,0:T(8,128)(2,1)S(1)} %collective-permute-done.5.refs_1_), channel_id=1, source_target_pairs={{0,1},{1,0},{2,3},{3,2},{4,5},{5,4},{6,7},{7,6},{8,9},{9,8},{10,11... | collective-permute-start | bytes 786440 | tf_op jit(solution)/shard_map/ppermute | solution.py:303
  26.8 0.7 copy-start.14
  28.4 0.7 copy-start.16
  29.1 40.4 %collective-permute-start.4 = (bf16[2,128,512]{2,1,0:T(8,128)(2,1)S(1)}, bf16[2,128,512]{2,1,0:T(8,128)(2,1)S(1)}, u32[]{:S(2)}, u32[]{:S(2)}) collective-permute-start(bf16[2,128,512]{2,1,0:T(8,128)(2,1)S(1)} %pad_maximum_fusion.refs_0_), channel_id=1, source_target_pairs={{0,8},{1,9},{2,10},{3,11},{4,12},{5,13},{6,14},{7,15},{16,24},{17,... | collective-permute-start | bytes 786440 | tf_op jit(solution)/shard_map/ppermute | solution.py:299
  31.1 38.4 %collective-permute-start.3 = (bf16[2,128,512]{2,1,0:T(8,128)(2,1)S(1)}, bf16[2,128,512]{2,1,0:T(8,128)(2,1)S(1)}, u32[]{:S(2)}, u32[]{:S(2)}) collective-permute-start(bf16[2,128,512]{2,1,0:T(8,128)(2,1)S(1)} %pad_maximum_fusion.refs_0_), channel_id=1, source_target_pairs={{0,6},{1,7},{2,8},{3,9},{4,10},{5,11},{6,12},{7,13},{8,14},{9,15},... | collective-permute-start | bytes 786440 | tf_op jit(solution)/shard_map/ppermute | solution.py:299
  33.7 35.8 %collective-permute-start.2 = (bf16[2,128,512]{2,1,0:T(8,128)(2,1)S(1)}, bf16[2,128,512]{2,1,0:T(8,128)(2,1)S(1)}, u32[]{:S(2)}, u32[]{:S(2)}) collective-permute-start(bf16[2,128,512]{2,1,0:T(8,128)(2,1)S(1)} %pad_maximum_fusion.refs_0_), channel_id=1, source_target_pairs={{0,4},{1,5},{2,6},{3,7},{4,8},{5,9},{6,10},{7,11},{8,12},{9,13},{1... | collective-permute-start | bytes 786440 | tf_op jit(solution)/shard_map/ppermute | solution.py:299
  36.3 33.2 %collective-permute-start.1 = (bf16[2,128,512]{2,1,0:T(8,128)(2,1)S(1)}, bf16[2,128,512]{2,1,0:T(8,128)(2,1)S(1)}, u32[]{:S(2)}, u32[]{:S(2)}) collective-permute-start(bf16[2,128,512]{2,1,0:T(8,128)(2,1)S(1)} %pad_maximum_fusion.refs_0_), channel_id=1, source_target_pairs={{0,2},{1,3},{2,4},{3,5},{4,6},{5,7},{6,8},{7,9},{8,10},{9,11},{10,... | collective-permute-start | bytes 786440 | tf_op jit(solution)/shard_map/ppermute | solution.py:299
  44.9 1.6 copy-start
  46.5 1.6 copy-start.2
  48.1 0.9 copy-start.9
  49.0 0.9 copy-start.11
  50.0 0.9 copy-start.13
  50.9 0.9 copy-start.15
  51.9 0.9 copy-start.17
  52.8 0.9 copy-start.19
  53.8 0.9 copy-start.21
  54.7 0.9 copy-start.23
  55.7 0.9 copy-start.25
  69.5 0.8 copy-start.4
  69.5 0.8 copy-start.6
  69.5 7.4 %collective-permute-start.19 = (bf16[4,2,128,512]{3,2,1,0:T(8,128)(2,1)S(1)}, bf16[4,2,128,512]{3,2,1,0:T(8,128)(2,1)}, u32[]{:S(2)}, u32[]{:S(2)}) collective-permute-start(bf16[4,2,128,512]{3,2,1,0:T(8,128)(2,1)S(1)} %get-tuple-element.60), channel_id=1, source_target_pairs={{0,1},{1,0},{2,3},{3,2},{4,5},{5,4},{6,7},{7,6},{8,9},{9,8},{10,11... | collective-permute-start | bytes 3145736 | tf_op jit(solution)/shard_map/ppermute | solution.py:306
  70.3 8.7 %collective-permute-start = (bf16[2,128,512]{2,1,0:T(8,128)(2,1)S(1)}, bf16[2,128,512]{2,1,0:T(8,128)(2,1)S(1)}, u32[]{:S(2)}, u32[]{:S(2)}) collective-permute-start(bf16[2,128,512]{2,1,0:T(8,128)(2,1)S(1)} %pad_maximum_fusion.refs_0_), channel_id=1, source_target_pairs={{0,1},{1,0},{2,3},{3,2},{4,5},{5,4},{6,7},{7,6},{8,9},{9,8},{10,11... | collective-permute-start | bytes 786440 | tf_op jit(solution)/shard_map/ppermute | solution.py:303
  76.3 22.2 %collective-permute-start.14 = (bf16[2,128,512]{2,1,0:T(8,128)(2,1)}, bf16[2,128,512]{2,1,0:T(8,128)(2,1)S(1)}, u32[]{:S(2)}, u32[]{:S(2)}) collective-permute-start(bf16[2,128,512]{2,1,0:T(8,128)(2,1)} %copy-done.6), channel_id=1, source_target_pairs={{0,1},{1,0},{2,3},{3,2},{4,5},{5,4},{6,7},{7,6},{8,9},{9,8},{10,11... | collective-permute-start | bytes 786440 | tf_op jit(solution)/shard_map/ppermute | solution.py:303
  76.3 22.2 %collective-permute-start.15 = (bf16[2,128,512]{2,1,0:T(8,128)(2,1)}, bf16[2,128,512]{2,1,0:T(8,128)(2,1)S(1)}, u32[]{:S(2)}, u32[]{:S(2)}) collective-permute-start(bf16[2,128,512]{2,1,0:T(8,128)(2,1)} %copy-done.4), channel_id=1, source_target_pairs={{0,1},{1,0},{2,3},{3,2},{4,5},{5,4},{6,7},{7,6},{8,9},{9,8},{10,11... | collective-permute-start | bytes 786440 | tf_op jit(solution)/shard_map/ppermute | solution.py:303
  76.8 21.7 %collective-permute-start.16 = (bf16[2,128,512]{2,1,0:T(8,128)(2,1)S(1)}, bf16[2,128,512]{2,1,0:T(8,128)(2,1)S(1)}, u32[]{:S(2)}, u32[]{:S(2)}) collective-permute-start(bf16[2,128,512]{2,1,0:T(8,128)(2,1)S(1)} %collective-permute-done.3.refs_3_), channel_id=1, source_target_pairs={{0,1},{1,0},{2,3},{3,2},{4,5},{5,4},{6,7},{7,6},{8,9},{9,8},{10,11... | collective-permute-start | bytes 786440 | tf_op jit(solution)/shard_map/ppermute | solution.py:303
  76.9 21.6 %collective-permute-start.17 = (bf16[2,128,512]{2,1,0:T(8,128)(2,1)S(1)}, bf16[2,128,512]{2,1,0:T(8,128)(2,1)S(1)}, u32[]{:S(2)}, u32[]{:S(2)}) collective-permute-start(bf16[2,128,512]{2,1,0:T(8,128)(2,1)S(1)} %collective-permute-done.4.refs_4_), channel_id=1, source_target_pairs={{0,1},{1,0},{2,3},{3,2},{4,5},{5,4},{6,7},{7,6},{8,9},{9,8},{10,11... | collective-permute-start | bytes 786440 | tf_op jit(solution)/shard_map/ppermute | solution.py:303
  77.3 28.4 %copy-start.1 = (bf16[2,1,128,4096]{3,2,1,0:T(8,128)(2,1)S(1)}, bf16[2,1,128,4096]{3,2,1,0:T(8,128)(2,1)}, u32[]{:S(2)}) copy-start(bf16[2,1,128,4096]{3,2,1,0:T(8,128)(2,1)} %q_ref.3) | copy-start | bytes 6291460
  77.3 28.4 %copy-start.3 = (bf16[2,1,128,4096]{3,2,1,0:T(8,128)(2,1)S(1)}, bf16[2,1,128,4096]{3,2,1,0:T(8,128)(2,1)}, u32[]{:S(2)}) copy-start(bf16[2,1,128,4096]{3,2,1,0:T(8,128)(2,1)} %g_ref.3) | copy-start | bytes 6291460
  79.1 19.4 %collective-permute-start.18 = (f32[32]{0:T(128)S(1)}, f32[32]{0:T(128)S(1)}, u32[]{:S(2)}, u32[]{:S(2)}) collective-permute-start(f32[32]{0:T(128)S(1)} %reshape_squeeze.6), channel_id=1, source_target_pairs={{0,112},{16,96},{32,80},{48,64},{64,48},{80,32},{96,16},{112,0},{1... | collective-permute-start | bytes 392 | tf_op jit(solution)/shard_map/ppermute | solution.py:348
  98.5 21.9 %collective-permute-start.20 = (bf16[2,128,512]{2,1,0:T(8,128)(2,1)S(1)}, bf16[2,128,512]{2,1,0:T(8,128)(2,1)S(1)}, u32[]{:S(2)}, u32[]{:S(2)}) collective-permute-start(bf16[2,128,512]{2,1,0:T(8,128)(2,1)S(1)} %get-tuple-element.72), channel_id=1, source_target_pairs={{2,0},{3,1},{4,2},{5,3},{6,4},{7,5},{8,6},{9,7},{10,8},{11,9},{12,... | collective-permute-start | bytes 786440 | tf_op jit(solution)/shard_map/ppermute | solution.py:321
  100.4 26.5 %collective-permute-start.21 = (bf16[2,128,512]{2,1,0:T(8,128)(2,1)S(1)}, bf16[2,128,512]{2,1,0:T(8,128)(2,1)S(1)}, u32[]{:S(2)}, u32[]{:S(2)}) collective-permute-start(bf16[2,128,512]{2,1,0:T(8,128)(2,1)S(1)} %get-tuple-element.73), channel_id=1, source_target_pairs={{4,0},{5,1},{6,2},{7,3},{8,4},{9,5},{10,6},{11,7},{12,8},{13,9},{1... | collective-permute-start | bytes 786440 | tf_op jit(solution)/shard_map/ppermute | solution.py:321
  102.3 24.6 %collective-permute-start.22 = (bf16[2,128,512]{2,1,0:T(8,128)(2,1)S(1)}, bf16[2,128,512]{2,1,0:T(8,128)(2,1)S(1)}, u32[]{:S(2)}, u32[]{:S(2)}) collective-permute-start(bf16[2,128,512]{2,1,0:T(8,128)(2,1)S(1)} %get-tuple-element.74), channel_id=1, source_target_pairs={{6,0},{7,1},{8,2},{9,3},{10,4},{11,5},{12,6},{13,7},{14,8},{15,9},... | collective-permute-start | bytes 786440 | tf_op jit(solution)/shard_map/ppermute | solution.py:321
  104.3 22.7 %collective-permute-start.23 = (bf16[2,128,512]{2,1,0:T(8,128)(2,1)S(1)}, bf16[2,128,512]{2,1,0:T(8,128)(2,1)S(1)}, u32[]{:S(2)}, u32[]{:S(2)}) collective-permute-start(bf16[2,128,512]{2,1,0:T(8,128)(2,1)S(1)} %get-tuple-element.75), channel_id=1, source_target_pairs={{8,0},{9,1},{10,2},{11,3},{12,4},{13,5},{14,6},{15,7},{24,16},{25,... | collective-permute-start | bytes 786440 | tf_op jit(solution)/shard_map/ppermute | solution.py:321
  105.8 1.0 copy-start.5
  106.7 0.9 copy-start.7
  120.4 6.5 %copy-start.27 = (bf16[2,128,512]{2,1,0:T(8,128)(2,1)}, bf16[2,128,512]{2,1,0:T(8,128)(2,1)S(1)}, u32[]{:S(2)}) copy-start(bf16[2,128,512]{2,1,0:T(8,128)(2,1)S(1)} %collective-permute-done.20) | copy-start | bytes 786436
  126.9 0.7 copy-start.29
  126.9 0.8 copy-start.31
  126.9 0.9 copy-start.33
  127.8 3.4 %collective-permute-start.24 = (bf16[4,2,128,512]{3,2,1,0:T(8,128)(2,1)S(1)}, bf16[4,2,128,512]{3,2,1,0:T(8,128)(2,1)}, u32[]{:S(2)}, u32[]{:S(2)}) collective-permute-start(bf16[4,2,128,512]{3,2,1,0:T(8,128)(2,1)S(1)} %get-tuple-element.81), channel_id=1, source_target_pairs={{0,1},{1,0},{2,3},{3,2},{4,5},{5,4},{6,7},{7,6},{8,9},{9,8},{10,11... | collective-permute-start | bytes 3145736 | tf_op jit(solution)/shard_map/ppermute | solution.py:306
  131.2 35.5 %copy-start.26 = (f32[2,128,512]{2,1,0:T(8,128)S(1)}, f32[2,128,512]{2,1,0:T(8,128)}, u32[]{:S(2)}) copy-start(f32[2,128,512]{2,1,0:T(8,128)} %add_bitcast_fusion.1) | copy-start | bytes 1572868
  131.2 35.5 %copy-start.28 = (bf16[2,128,512]{2,1,0:T(8,128)(2,1)S(1)}, bf16[2,128,512]{2,1,0:T(8,128)(2,1)}, u32[]{:S(2)}) copy-start(bf16[2,128,512]{2,1,0:T(8,128)(2,1)} %copy-done.27) | copy-start | bytes 786436
  131.2 35.5 %copy-start.30 = (bf16[2,128,512]{2,1,0:T(8,128)(2,1)S(1)}, bf16[2,128,512]{2,1,0:T(8,128)(2,1)}, u32[]{:S(2)}) copy-start(bf16[2,128,512]{2,1,0:T(8,128)(2,1)} %copy-done.29) | copy-start | bytes 786436
  131.2 35.5 %copy-start.32 = (bf16[2,128,512]{2,1,0:T(8,128)(2,1)S(1)}, bf16[2,128,512]{2,1,0:T(8,128)(2,1)}, u32[]{:S(2)}) copy-start(bf16[2,128,512]{2,1,0:T(8,128)(2,1)} %copy-done.31) | copy-start | bytes 786436
  131.2 35.5 %copy-start.34 = (bf16[2,128,512]{2,1,0:T(8,128)(2,1)S(1)}, bf16[2,128,512]{2,1,0:T(8,128)(2,1)}, u32[]{:S(2)}) copy-start(bf16[2,128,512]{2,1,0:T(8,128)(2,1)} %copy-done.33) | copy-start | bytes 786436
  133.9 4.3 %collective-permute-start.29 = (f32[32]{0:T(128)S(1)}, f32[32]{0:T(128)S(1)}, u32[]{:S(2)}, u32[]{:S(2)}) collective-permute-start(f32[32]{0:T(128)S(1)} %add.184), channel_id=1, source_target_pairs={{0,1},{1,0},{2,3},{3,2},{4,5},{5,4},{6,7},{7,6},{8,9},{9,8},{10,11... | collective-permute-start | bytes 392 | tf_op jit(solution)/shard_map/ppermute | solution.py:374
  134.4 39.0 %collective-permute-start.25 = (bf16[2,128,512]{2,1,0:T(8,128)(2,1)S(1)}, bf16[2,128,512]{2,1,0:T(8,128)(2,1)S(1)}, u32[]{:S(2)}, u32[]{:S(2)}) collective-permute-start(bf16[2,128,512]{2,1,0:T(8,128)(2,1)S(1)} %get-tuple-element.83), channel_id=1, source_target_pairs={{2,0},{3,1},{4,2},{5,3},{6,4},{7,5},{8,6},{9,7},{10,8},{11,9},{12,... | collective-permute-start | bytes 786440 | tf_op jit(solution)/shard_map/ppermute | solution.py:321
  136.3 37.1 %collective-permute-start.26 = (bf16[2,128,512]{2,1,0:T(8,128)(2,1)S(1)}, bf16[2,128,512]{2,1,0:T(8,128)(2,1)S(1)}, u32[]{:S(2)}, u32[]{:S(2)}) collective-permute-start(bf16[2,128,512]{2,1,0:T(8,128)(2,1)S(1)} %get-tuple-element.84), channel_id=1, source_target_pairs={{4,0},{5,1},{6,2},{7,3},{8,4},{9,5},{10,6},{11,7},{12,8},{13,9},{1... | collective-permute-start | bytes 786440 | tf_op jit(solution)/shard_map/ppermute | solution.py:321
  138.3 4.3 %collective-permute-start.30 = (f32[32]{0:T(128)S(1)}, f32[32]{0:T(128)S(1)}, u32[]{:S(2)}, u32[]{:S(2)}) collective-permute-start(f32[32]{0:T(128)S(1)} %add.192), channel_id=1, source_target_pairs={{0,2},{1,3},{2,0},{3,1},{4,6},{5,7},{6,4},{7,5},{8,10},{9,11},{10,... | collective-permute-start | bytes 392 | tf_op jit(solution)/shard_map/ppermute | solution.py:374
  138.4 35.1 %collective-permute-start.27 = (bf16[2,128,512]{2,1,0:T(8,128)(2,1)S(1)}, bf16[2,128,512]{2,1,0:T(8,128)(2,1)S(1)}, u32[]{:S(2)}, u32[]{:S(2)}) collective-permute-start(bf16[2,128,512]{2,1,0:T(8,128)(2,1)S(1)} %get-tuple-element.85), channel_id=1, source_target_pairs={{6,0},{7,1},{8,2},{9,3},{10,4},{11,5},{12,6},{13,7},{14,8},{15,9},... | collective-permute-start | bytes 786440 | tf_op jit(solution)/shard_map/ppermute | solution.py:321
  142.5 3.3 %collective-permute-start.31 = (f32[32]{0:T(128)S(1)}, f32[32]{0:T(128)S(1)}, u32[]{:S(2)}, u32[]{:S(2)}) collective-permute-start(f32[32]{0:T(128)S(1)} %add.193), channel_id=1, source_target_pairs={{0,4},{1,5},{2,6},{3,7},{4,0},{5,1},{6,2},{7,3},{8,12},{9,13},{10,... | collective-permute-start | bytes 392 | tf_op jit(solution)/shard_map/ppermute | solution.py:374
  142.6 30.9 %collective-permute-start.28 = (bf16[2,128,512]{2,1,0:T(8,128)(2,1)S(1)}, bf16[2,128,512]{2,1,0:T(8,128)(2,1)S(1)}, u32[]{:S(2)}, u32[]{:S(2)}) collective-permute-start(bf16[2,128,512]{2,1,0:T(8,128)(2,1)S(1)} %get-tuple-element.86), channel_id=1, source_target_pairs={{8,0},{9,1},{10,2},{11,3},{12,4},{13,5},{14,6},{15,7},{24,16},{25,... | collective-permute-start | bytes 786440 | tf_op jit(solution)/shard_map/ppermute | solution.py:321
  145.9 27.1 %collective-permute-start.32 = (f32[32]{0:T(128)S(1)}, f32[32]{0:T(128)S(1)}, u32[]{:S(2)}, u32[]{:S(2)}) collective-permute-start(f32[32]{0:T(128)S(1)} %add.194), channel_id=1, source_target_pairs={{0,8},{1,9},{2,10},{3,11},{4,12},{5,13},{6,14},{7,15},{8,0},{9,1},... | collective-permute-start | bytes 392 | tf_op jit(solution)/shard_map/ppermute | solution.py:374
  (4 other events, 2.8 us)

commit v3 on v2

v3 whole, which is shorter than its diff:
```python
import functools
import math

import jax
import jax.numpy as jnp
from jax import lax
from jax.experimental import pallas as pl
from jax.experimental.pallas import tpu as pltpu
from jax.sharding import PartitionSpec as P

HEAD_WIDTH = 128
HQ = 32
KEY_HEADS = 4
QUERY_PER_KV = 8
TILE = 128
DOCS = 4
RELAY_COUNT = 2
LONGEST = 9
REACH = LONGEST // 2
ROWS = QUERY_PER_KV * TILE
SCALE = 1.0 / math.sqrt(HEAD_WIDTH)
LOG2E = 1.4426950408889634
HIDDEN = -1e30
VMEM_BYTES = 26 * 1024 * 1024
GROUP = 3
SLOTS = 2 * (REACH + 1)
HEADS = KEY_HEADS // 2
STEPS = 2 * HEADS
KEY_PART = HEADS * HEAD_WIDTH
WIDE = QUERY_PER_KV * HEAD_WIDTH
QUERY_PART = HEADS * WIDE


def dot(left, right, left_dim, right_dim):
    return lax.dot_general(
        left,
        right,
        (((left_dim,), (right_dim,)), ((), ())),
        preferred_element_type=jnp.float32,
    )


def attend_kernel(relay, refilled, meta, sink, q_own, g_own, q_got, g_got, *refs):
    pieces = refs[: REACH + 1]
    refs = refs[REACH + 1 + refilled :]
    o_ref, dq_ref, out_send = refs[:3]
    terms = refs[3 : REACH + 4]
    sink_part = refs[REACH + 4]
    q_in, g_in, o_out, dq_out, kv, grads, grads_low = refs[REACH + 5 : REACH + 12]
    q_turned, g_turned, q_rows, g_rows, scores, shares, out_sum, dq_sum = refs[
        REACH + 12 : REACH + 20
    ]
    q_sem, kv_sem, out_sem, grad_sem = refs[REACH + 20 :]
    step = pl.program_id(0)
    head = lax.div(step, 2)
    later = lax.rem(step, 2)
    core = meta[2]
    count = jnp.where(later == 1, meta[1], meta[0])
    groups = lax.div(count + GROUP - 1, GROUP)
    offset = 1 - later

    def wide_cols(j):
        return pl.ds(pl.multiple_of(j * WIDE, WIDE), WIDE)

    def fetch_rows(i, own):
        pairs = ((q_own, q_got, q_in), (g_own, g_got, g_in))
        return [
            pltpu.make_async_copy(
                mine.at[relay, 0, :, wide_cols(HEADS * core + i // 2)]
                if own
                else got.at[relay, :, pl.ds((i // 2) * WIDE, WIDE)],
                to.at[i],
                q_sem.at[k, i],
            )
            for k, (mine, got, to) in enumerate(pairs)
        ]

    def fetch_keys(j, distance):
        return pltpu.make_async_copy(
            pieces[distance].at[:, :, :, pl.ds(j * HEAD_WIDTH, HEAD_WIDTH)],
            kv.at[j, :, pl.ds(2 * distance, 2)],
            kv_sem.at[j, distance],
        )

    def give_rows(i, own):
        return [
            pltpu.make_async_copy(
                source.at[i],
                target.at[relay, 0, :, wide_cols(HEADS * core + i // 2)]
                if own
                else out_send.at[k, :, pl.ds((i // 2) * WIDE, WIDE)],
                out_sem.at[k, i],
            )
            for k, (source, target) in enumerate(((o_out, o_ref), (dq_out, dq_ref)))
        ]

    def give_grads(j, distance):
        return pltpu.make_async_copy(
            grads_low.at[j, :, pl.ds(2 * distance, 2)],
            terms[distance].at[:, :, :, pl.ds(j * HEAD_WIDTH, HEAD_WIDTH)],
            grad_sem.at[j, distance],
        )

    def start_all(copies):
        for copy in copies:
            copy.start()

    def wait_all(copies):
        for copy in copies:
            copy.wait()

    @pl.when(step == 0)
    def _():
        for i in range(STEPS):
            pl.when(core == i % 2)(lambda: start_all(fetch_rows(i, True)))
            pl.when(core != i % 2)(lambda: start_all(fetch_rows(i, False)))
            if i % 2 == 0:
                start_all(fetch_keys(i // 2, distance) for distance in range(REACH + 1))

    for i in range(STEPS):

        @pl.when(step == i)
        def _():
            wait_all(fetch_rows(i, False))
            if i % 2 == 0:
                wait_all(fetch_keys(i // 2, distance) for distance in range(REACH + 1))

    heads = [slice(i * HEAD_WIDTH, (i + 1) * HEAD_WIDTH) for i in range(QUERY_PER_KV)]
    for part in heads:
        q, g = q_in[step, :, part], g_in[step, :, part]
        q_rows[part, :] = q
        g_rows[part, :] = g
        q_turned[:, part] = q.T
        g_turned[:, part] = g.T

    def tiles_of(which, group):
        rows = kv[head, which, pl.ds(offset + group * GROUP, GROUP)]
        return rows.reshape(GROUP * TILE, HEAD_WIDTH)

    def block(group):
        return pl.ds(pl.multiple_of(group * GROUP * TILE, GROUP * TILE), GROUP * TILE)

    def scores_of(group):
        score = dot(tiles_of(0, group), q_turned[...], 1, 0)
        rows = [score[:TILE]]
        for i in range(1, GROUP):
            bias = jnp.where(GROUP * group + i < count, 0.0, HIDDEN).astype(jnp.float32)
            rows.append(score[i * TILE : (i + 1) * TILE] + bias)
        return rows

    def keep_scores(group, rows, top):
        score = jnp.concatenate(rows, axis=0)
        scores[block(group), :] = score
        most = jnp.max(score.reshape(-1, 8, ROWS), axis=0)
        return most if top is None else jnp.maximum(top, most)

    row = lax.broadcasted_iota(jnp.int32, (TILE, TILE), 0)
    column = lax.broadcasted_iota(jnp.int32, (TILE, TILE), 1)
    seen = jnp.concatenate([row <= column] * QUERY_PER_KV, axis=1)
    rows = scores_of(0)
    top = keep_scores(0, [jnp.where(seen, rows[0], HIDDEN)] + rows[1:], None)
    top = lax.fori_loop(
        1, groups, lambda group, top: keep_scores(group, scores_of(group), top), top
    )
    logit = jnp.concatenate(
        [
            jnp.full(
                (1, TILE), sink[(HEADS * core + head) * QUERY_PER_KV + i] * LOG2E, jnp.float32
            )
            for i in range(QUERY_PER_KV)
        ],
        axis=1,
    )
    top = jnp.maximum(jnp.max(top, axis=0, keepdims=True) * (SCALE * LOG2E), logit)

    out_sum[...] = jnp.zeros_like(out_sum)
    dq_sum[...] = jnp.zeros_like(dq_sum)
    ones = jnp.ones((16, GROUP * TILE), jnp.bfloat16)

    def share_step(group, carry):
        turned = jnp.concatenate([tiles_of(1, group).T, ones], axis=0)
        low = jnp.exp2(scores[block(group), :] * (SCALE * LOG2E) - top).astype(jnp.bfloat16)
        shares[block(group), :] = low
        out_sum[...] += dot(turned, low, 1, 0)
        return carry

    lax.fori_loop(0, groups, share_step, 0)
    sink_raised = jnp.exp2(logit - top)
    inverse = 1.0 / (out_sum[HEAD_WIDTH : HEAD_WIDTH + 1, :] + sink_raised)
    out = (out_sum[:HEAD_WIDTH, :] * inverse).astype(jnp.bfloat16)
    delta = jnp.sum(
        out.astype(jnp.float32) * g_turned[...].astype(jnp.float32), axis=0, keepdims=True
    )
    sink_rows = sink_raised * inverse * delta
    for i, part in enumerate(heads):
        o_out[step, :, part] = out[:, part].T
        sink_part[0, i : i + 1, :] = jnp.broadcast_to(
            -jnp.sum(sink_rows[:, part], axis=1, keepdims=True), (1, HEAD_WIDTH)
        )

    @pl.when(later == 0)
    def _():
        grads[...] = jnp.zeros_like(grads)

    def add_grads(which, group, term):
        rows = pl.ds(offset + group * GROUP, GROUP)
        grads[which, rows] += term.reshape(GROUP, TILE, HEAD_WIDTH)

    def grad_step(group, carry):
        share = shares[block(group), :].astype(jnp.float32) * inverse
        share_grad = dot(tiles_of(1, group), g_turned[...], 1, 0)
        score_grad = (share * (share_grad - delta)).astype(jnp.bfloat16)
        dq_sum[...] += dot(tiles_of(0, group).T, score_grad, 1, 0)
        add_grads(0, group, dot(score_grad, q_rows[...], 1, 0))
        add_grads(1, group, dot(share.astype(jnp.bfloat16), g_rows[...], 1, 0))
        return carry

    lax.fori_loop(0, groups, grad_step, 0)
    for part in heads:
        dq_out[step, :, part] = (dq_sum[:, part] * SCALE).astype(jnp.bfloat16).T

    @pl.when(later == 1)
    def _():
        grads_low[head, 0] = (grads[0] * SCALE).astype(jnp.bfloat16)
        grads_low[head, 1] = grads[1].astype(jnp.bfloat16)

    for i in range(STEPS):

        @pl.when(step == i)
        def _():
            pl.when(core == i % 2)(lambda: start_all(give_rows(i, True)))
            pl.when(core != i % 2)(lambda: start_all(give_rows(i, False)))
            if i % 2 == 1:
                start_all(give_grads(i // 2, distance) for distance in range(REACH + 1))

    @pl.when(step == STEPS - 1)
    def _():
        for i in range(STEPS):
            wait_all(give_rows(i, False))
            if i % 2 == 1:
                wait_all(give_grads(i // 2, distance) for distance in range(REACH + 1))


def attend(relay, meta, sink, queries, output_gradient, got, pieces, filled):
    smem = pl.BlockSpec(memory_space=pltpu.SMEM)
    whole = pl.BlockSpec(memory_space=pl.ANY)
    low = jnp.bfloat16
    inputs = [queries, output_gradient, *got, *pieces, *filled]
    first = 2 + len(inputs) - len(filled)
    rows = pltpu.VMEM((STEPS, TILE, WIDE), low)
    return pl.pallas_call(
        functools.partial(attend_kernel, relay, len(filled)),
        grid=(STEPS,),
        in_specs=[smem, smem] + [whole] * len(inputs),
        out_specs=[whole] * (REACH + 4)
        + [pl.BlockSpec((1, QUERY_PER_KV, HEAD_WIDTH), lambda i: (i, 0, 0))],
        out_shape=[
            jax.ShapeDtypeStruct(queries.shape, low),
            jax.ShapeDtypeStruct(queries.shape, low),
            jax.ShapeDtypeStruct((2, TILE, QUERY_PART), low),
        ]
        + [jax.ShapeDtypeStruct((2, 2, TILE, KEY_PART), low)] * (REACH + 1)
        + [jax.ShapeDtypeStruct((STEPS, QUERY_PER_KV, HEAD_WIDTH), jnp.float32)],
        scratch_shapes=[
            rows,
            rows,
            rows,
            rows,
            pltpu.VMEM((HEADS, 2, SLOTS, TILE, HEAD_WIDTH), low),
            pltpu.VMEM((2, SLOTS, TILE, HEAD_WIDTH), jnp.float32),
            pltpu.VMEM((HEADS, 2, SLOTS, TILE, HEAD_WIDTH), low),
            pltpu.VMEM((HEAD_WIDTH, ROWS), low),
            pltpu.VMEM((HEAD_WIDTH, ROWS), low),
            pltpu.VMEM((ROWS, HEAD_WIDTH), low),
            pltpu.VMEM((ROWS, HEAD_WIDTH), low),
            pltpu.VMEM((LONGEST * TILE, ROWS), jnp.float32),
            pltpu.VMEM((LONGEST * TILE, ROWS), low),
            pltpu.VMEM((HEAD_WIDTH + 16, ROWS), jnp.float32),
            pltpu.VMEM((HEAD_WIDTH, ROWS), jnp.float32),
            pltpu.SemaphoreType.DMA((2, STEPS)),
            pltpu.SemaphoreType.DMA((HEADS, REACH + 1)),
            pltpu.SemaphoreType.DMA((2, STEPS)),
            pltpu.SemaphoreType.DMA((HEADS, REACH + 1)),
        ],
        input_output_aliases={first + i: i for i in range(len(filled))},
        compiler_params=pltpu.CompilerParams(vmem_limit_bytes=VMEM_BYTES),
        cost_estimate=pl.CostEstimate(
            flops=12 * LONGEST * HQ * TILE * TILE * HEAD_WIDTH * 4,
            bytes_accessed=9 << 20,
            transcendentals=LONGEST * HQ * TILE * TILE,
        ),
        name=f"attend_{relay}",
    )(meta, sink, *inputs)


def shards(queries, keys, values, output_gradient, doc_tiles, sink_logits):
    ctx_count = lax.axis_size("ctx")
    ctx_pos = lax.axis_index("ctx")
    section_pos = lax.axis_index("section")
    section_count = lax.axis_size("section")
    core = lax.rem(ctx_pos, 2)
    first, second = 1, 0

    def shifted(pieces, amount):
        route = [
            (c, c + amount * 2 * (distance + 1))
            for distance in range(REACH)
            for c in range(ctx_count)
        ]
        routes = [route[d * ctx_count : (d + 1) * ctx_count] for d in range(REACH)]
        return [
            lax.ppermute(
                pieces[d + 1] if len(pieces) > 1 else pieces[0],
                "ctx",
                [(a, b) for a, b in routes[d] if 0 <= b < ctx_count],
            )
            for d in range(REACH)
        ]

    def swapped(array):
        return lax.ppermute(array, "ctx", [(c, c ^ 1) for c in range(ctx_count)])

    def half(array, which):
        width = array.shape[-1] // 2
        return lax.dynamic_slice_in_dim(array, which * width, width, array.ndim - 1)

    def in_order(own, got, later_first, axis):
        own_first = (core == 1) if later_first else (core == 0)
        return jnp.stack(
            [jnp.where(own_first, own, got), jnp.where(own_first, got, own)], axis=axis
        )

    def meta_of(relay):
        counts = []
        for position in (ctx_pos - core, ctx_pos - core + 1):
            end = start = jnp.zeros((), jnp.int32)
            for document in range(DOCS):
                end = end + doc_tiles[relay, 0, document]
                start = jnp.where(end <= position, end, start)
            counts.append(position - start + 1)
        return jnp.stack(counts + [core]).astype(jnp.int32)

    def sink_of(relay):
        layer = section_pos if relay == 0 else section_count - 1 - section_pos
        return lax.dynamic_index_in_dim(sink_logits, layer, 0, keepdims=False)

    def sink_terms(sink_part):
        mine = jnp.sum(sink_part[:, :, 0].reshape(HEADS, 2, QUERY_PER_KV), axis=1).reshape(-1)
        mine = jnp.concatenate([mine, mine])
        return jnp.where(jnp.arange(HQ) // (HQ // 2) == core, mine, 0.0)

    def summed(terms, sent):
        total = terms[0].astype(jnp.float32)
        for other in sent:
            total = total + other.astype(jnp.float32)
        return total.astype(jnp.bfloat16)

    both = jnp.stack([keys[:, 0], values[:, 0]], axis=1)
    own = half(both, core)
    piece = in_order(own, swapped(half(both, 1 - core)), True, 2)
    pieces = [piece[relay] for relay in range(RELAY_COUNT)]
    pieces[0], pieces[1], mate = lax.optimization_barrier((pieces[0], pieces[1], 1 - core))
    mine_first = [pieces[first]] + shifted([pieces[first]], 1)
    got = [swapped(half(array[:, 0], mate)) for array in (queries, output_gradient)]
    mine_second = [pieces[second]] + shifted([pieces[second]], 1)
    attention, query_grad, out_first, *terms_first, sink_part = attend(
        first, meta_of(first), sink_of(first), queries, output_gradient, got, mine_first, []
    )
    mine_second, sink_part = lax.optimization_barrier((mine_second, sink_part))
    sent_first = shifted(terms_first, -1)
    out_first = swapped(out_first)
    mirrored = lax.ppermute(
        sink_terms(sink_part),
        "section",
        [(s, section_count - 1 - s) for s in range(section_count)],
    )
    attention, query_grad, out_second, *terms_second, sink_part = attend(
        second,
        meta_of(second),
        sink_of(second),
        queries,
        output_gradient,
        got,
        mine_second,
        [attention, query_grad],
    )
    sent_first, out_first, mirrored, sink_part = lax.optimization_barrier(
        (sent_first, out_first, mirrored, sink_part)
    )
    sent_second = shifted(terms_second, -1)
    out_second = swapped(out_second)
    sink_grad = sink_terms(sink_part) + mirrored
    distance = 1
    while distance < ctx_count:
        sink_grad = sink_grad + lax.ppermute(
            sink_grad, "ctx", [(c, c ^ distance) for c in range(ctx_count)]
        )
        distance *= 2
    for relay, got in ((first, out_first), (second, out_second)):
        place = (relay, 0, 0, mate * QUERY_PART)
        attention = lax.dynamic_update_slice(attention, got[0][None, None], place)
        query_grad = lax.dynamic_update_slice(query_grad, got[1][None, None], place)
    first_sum = summed(terms_first, sent_first)
    sent_second, sink_grad, first_sum, attention, query_grad = lax.optimization_barrier(
        (sent_second, sink_grad, first_sum, attention, query_grad)
    )
    second_sum = summed(terms_second, sent_second)
    sums = jnp.stack([second_sum, first_sum])
    own = lax.dynamic_index_in_dim(sums, mate, 2, keepdims=False)
    got = swapped(lax.dynamic_index_in_dim(sums, core, 2, keepdims=False))
    grads = jnp.concatenate(
        [jnp.where(core == 0, own, got), jnp.where(core == 0, got, own)], axis=-1
    )
    return (attention, query_grad, grads[:, :1], grads[:, 1:], sink_grad[None])


def solution(mesh):
    placed = (
        P(None, "section", "ctx", None),
        P(None, "section", "ctx", None),
        P(None, "section", "ctx", None),
        P(None, "section", "ctx", None),
        P(None, "section", None),
        P(),
    )
    return jax.shard_map(
        shards,
        mesh=mesh,
        in_specs=placed,
        out_specs=(
            P(None, "section", "ctx", None),
            P(None, "section", "ctx", None),
            P(None, "section", "ctx", None),
            P(None, "section", "ctx", None),
            P("section", None),
        ),
        check_vma=False,
    )
```

time: 176 us -> 168 us (0.955)
  the two profiles are of different devices: /device:TPU:45 before, /device:TPU:1 now
where the time goes in v3:
time: 168 us; the launch traced here: 167 us
  starting transfers between devices  89.9 us (54%)
  Pallas kernels  25.1 us (15%)
  local copies, waits for them, and re-layouts  24.1 us (14%)
  waiting for transfers between devices  12.9 us (8%)
  between operations  11.3 us (7%)
  other arithmetic  3.48 us (2%)
    ppermute x4, starting transfers between devices, shards(): lax.ppermute(sink_grad, 'ctx', [(c, c ^ distance) for c in range(ctx_coun...  42.9 us
    ppermute x16, starting transfers between devices, shifted(): lax.ppermute(pieces[d + 1] if len(pieces) > 1 else pieces[0], 'ctx', [(a,...  37.7 us
    pallas_call x2, Pallas kernels, attend(): pl.pallas_call(functools.partial(attend_kernel, relay, len(filled)), grid...  25.1 us
    unnamed x39, local copies, waits for them, and re-layouts  15.9 us
    ppermute x16, waiting for transfers between devices, shifted(): lax.ppermute(pieces[d + 1] if len(pieces) > 1 else pieces[0], 'ctx', [(a,...  8.4 us
    ppermute x6, starting transfers between devices, swapped(): return lax.ppermute(array, 'ctx', [(c, c ^ 1) for c in range(ctx_count)])  5.56 us
    ppermute x1, starting transfers between devices, shards(): lax.ppermute(sink_terms(sink_part), 'section', [(s, section_count - 1 - s...  3.79 us
  transfers between devices with their start and end apart: 27, of which 6 were waited for; matrix products, arithmetic and copies ran while one was open for 5% of the time, Pallas kernels for 15%

profile of v3, /device:TPU:1, one launch (start us, length us, event | category | flops | bytes accessed | tf_op | source)
XLA Modules:
  0.0 166.7 jit_solution(2959014526181563239)
XLA Ops:
  0.6 1.1 constant_dynamic-update-slice_fusion.1
  1.8 1.0 constant_dynamic-update-slice_fusion
  2.8 1.5 collective-permute-start
  4.3 1.2 collective-permute-done
  5.4 0.1 select_bitcast_fusion
  5.7 1.1 dynamic-slice_bitcast_fusion.1
  6.8 0.4 collective-permute-start.1
  7.1 0.5 copy-done.1
  7.6 1.0 dynamic-slice_bitcast_fusion
  8.7 0.4 collective-permute-start.2
  9.0 4.9 %collective-permute-start.10 = (bf16[2,2,128,256]{3,2,1,0:T(8,128)(2,1)S(1)}, bf16[2,2,128,256]{3,2,1,0:T(8,128)(2,1)S(1)}, u32[]{:S(2)}, u32[]{:S(2)}) collective-permute-start(bf16[2,2,128,256]{3,2,1,0:T(8,128)(2,1)S(1)} %get-tuple-element.49.refs_0_), channel_id=1, source_target_pairs={{0,8},{1,9},{2,10},{3,11},{4,12},{5,13},{6,14},{7,15},{16,24},{17,... | collective-permute-start | bytes 786440 | tf_op jit(solution)/shard_map/ppermute | solution.py:312
  13.9 0.7 fusion.14
  19.7 4.7 %collective-permute-start.7 = (bf16[2,2,128,256]{3,2,1,0:T(8,128)(2,1)S(1)}, bf16[2,2,128,256]{3,2,1,0:T(8,128)(2,1)S(1)}, u32[]{:S(2)}, u32[]{:S(2)}) collective-permute-start(bf16[2,2,128,256]{3,2,1,0:T(8,128)(2,1)S(1)} %get-tuple-element.49.refs_0_), channel_id=1, source_target_pairs={{0,2},{1,3},{2,4},{3,5},{4,6},{5,7},{6,8},{7,9},{8,10},{9,11},{10,... | collective-permute-start | bytes 786440 | tf_op jit(solution)/shard_map/ppermute | solution.py:312
  24.4 2.3 %collective-permute-start.8 = (bf16[2,2,128,256]{3,2,1,0:T(8,128)(2,1)S(1)}, bf16[2,2,128,256]{3,2,1,0:T(8,128)(2,1)S(1)}, u32[]{:S(2)}, u32[]{:S(2)}) collective-permute-start(bf16[2,2,128,256]{3,2,1,0:T(8,128)(2,1)S(1)} %get-tuple-element.49.refs_0_), channel_id=1, source_target_pairs={{0,4},{1,5},{2,6},{3,7},{4,8},{5,9},{6,10},{7,11},{8,12},{9,13},{1... | collective-permute-start | bytes 786440 | tf_op jit(solution)/shard_map/ppermute | solution.py:312
  26.7 2.4 %collective-permute-start.9 = (bf16[2,2,128,256]{3,2,1,0:T(8,128)(2,1)S(1)}, bf16[2,2,128,256]{3,2,1,0:T(8,128)(2,1)}, u32[]{:S(2)}, u32[]{:S(2)}) collective-permute-start(bf16[2,2,128,256]{3,2,1,0:T(8,128)(2,1)S(1)} %get-tuple-element.49.refs_0_), channel_id=1, source_target_pairs={{0,6},{1,7},{2,8},{3,9},{4,10},{5,11},{6,12},{7,13},{8,14},{9,15},... | collective-permute-start | bytes 786440 | tf_op jit(solution)/shard_map/ppermute | solution.py:312
  34.4 0.8 fusion.13
  35.1 4.8 %collective-permute-start.3 = (bf16[2,2,128,256]{3,2,1,0:T(8,128)(2,1)S(1)}, bf16[2,2,128,256]{3,2,1,0:T(8,128)(2,1)S(1)}, u32[]{:S(2)}, u32[]{:S(2)}) collective-permute-start(bf16[2,2,128,256]{3,2,1,0:T(8,128)(2,1)S(1)} %get-tuple-element.51.refs_0_), channel_id=1, source_target_pairs={{0,2},{1,3},{2,4},{3,5},{4,6},{5,7},{6,8},{7,9},{8,10},{9,11},{10,... | collective-permute-start | bytes 786440 | tf_op jit(solution)/shard_map/ppermute | solution.py:312
  40.0 7.3 %collective-permute-done.8.refs_2_ = bf16[2,2,128,256]{3,2,1,0:T(8,128)(2,1)S(1)} collective-permute-done((bf16[2,2,128,256]{3,2,1,0:T(8,128)(2,1)S(1)}, bf16[2,2,128,256]{3,2,1,0:T(8,128)(2,1)S(1)}, u32[]{:S(2)}, u32[]{:S(2)}) %collective-permute-start.8) | collective-permute-done | bytes 262176 | tf_op jit(solution)/shard_map/ppermute | solution.py:312
  47.3 0.7 copy-done.4
  48.0 4.1 %collective-permute-start.4 = (bf16[2,2,128,256]{3,2,1,0:T(8,128)(2,1)S(1)}, bf16[2,2,128,256]{3,2,1,0:T(8,128)(2,1)S(1)}, u32[]{:S(2)}, u32[]{:S(2)}) collective-permute-start(bf16[2,2,128,256]{3,2,1,0:T(8,128)(2,1)S(1)} %get-tuple-element.51.refs_0_), channel_id=1, source_target_pairs={{0,4},{1,5},{2,6},{3,7},{4,8},{5,9},{6,10},{7,11},{8,12},{9,13},{1... | collective-permute-start | bytes 786440 | tf_op jit(solution)/shard_map/ppermute | solution.py:312
  52.1 1.3 collective-permute-start.5
  53.5 2.9 %collective-permute-start.6 = (bf16[2,2,128,256]{3,2,1,0:T(8,128)(2,1)S(1)}, bf16[2,2,128,256]{3,2,1,0:T(8,128)(2,1)S(1)}, u32[]{:S(2)}, u32[]{:S(2)}) collective-permute-start(bf16[2,2,128,256]{3,2,1,0:T(8,128)(2,1)S(1)} %get-tuple-element.51.refs_0_), channel_id=1, source_target_pairs={{0,8},{1,9},{2,10},{3,11},{4,12},{5,13},{6,14},{7,15},{16,24},{17,... | collective-permute-start | bytes 786440 | tf_op jit(solution)/shard_map/ppermute | solution.py:312
  56.4 1.6 copy-done.2
  58.0 0.9 copy-done.5
  59.0 12.6 %attend_1.1 = (bf16[2,1,128,4096]{3,2,1,0:T(8,128)(2,1)}, bf16[2,1,128,4096]{3,2,1,0:T(8,128)(2,1)}, bf16[2,128,2048]{2,1,0:T(8,128)(2,1)}, bf16[2,2,128,256]{3,...) custom-call(s32[3]{0:T(128)S(1)} %add_add_fusion.1.meta, ...), custom_call_target="tpu_custom_call" | custom-call | flops 28991029248 | bytes 9437184 | tf_op jit(solution)/shard_map/attend_1/pallas_call | solution.py:251
  71.6 0.7 copy-done.8
  72.3 0.7 copy-done.11
  73.0 0.7 copy-done.9
  73.7 0.7 copy-done.12
  74.4 0.7 copy-done.14
  75.1 0.7 copy-done.16
  75.8 0.8 collective-permute-start.19
  76.6 1.3 collective-permute-start.15
  77.9 1.3 collective-permute-start.16
  79.5 3.8 %collective-permute-start.20 = (f32[32]{0:T(128)S(1)}, f32[32]{0:T(128)S(1)}, u32[]{:S(2)}, u32[]{:S(2)}) collective-permute-start(f32[32]{0:T(128)S(1)} %compare_select_fusion.1), channel_id=1, source_target_pairs={{0,112},{16,96},{32,80},{48,64},{64,48},{80,32},{96,16},{112,0},{1... | collective-permute-start | bytes 392 | tf_op jit(solution)/shard_map/ppermute | solution.py:372
  83.3 1.3 collective-permute-start.17
  84.6 1.3 collective-permute-start.18
  85.9 1.6 copy-done.3
  87.5 0.9 copy-done.10
  88.4 0.9 copy-done.13
  89.4 0.9 copy-done.15
  90.3 0.9 copy-done.17
  91.3 12.5 %attend_0.1 = (bf16[2,1,128,4096]{3,2,1,0:T(8,128)(2,1)}, bf16[2,1,128,4096]{3,2,1,0:T(8,128)(2,1)}, bf16[2,128,2048]{2,1,0:T(8,128)(2,1)}, bf16[2,2,128,256]{3,...) custom-call(s32[3]{0:T(128)S(1)} %add_add_fusion.meta, ...), custom_call_target="tpu_custom_call", output_to_operand_aliasing={{0}: (11, {}), {1}: (12, {})} | custom-call | flops 28991029248 | bytes 9437184 | tf_op jit(solution)/shard_map/attend_0/pallas_call | solution.py:251
  103.8 0.7 copy-done.6
  104.5 0.7 copy-done.7
  105.2 1.3 collective-permute-start.11
  106.5 1.3 collective-permute-start.12
  107.8 1.0 collective-permute-done.18
  109.1 1.7 %collective-permute-start.21 = (f32[32]{0:T(128)S(1)}, f32[32]{0:T(128)S(1)}, u32[]{:S(2)}, u32[]{:S(2)}) collective-permute-start(f32[32]{0:T(128)S(1)} %fusion.11), channel_id=1, source_target_pairs={{0,1},{1,0},{2,3},{3,2},{4,5},{5,4},{6,7},{7,6},{8,9},{9,8},{10,11... | collective-permute-start | bytes 392 | tf_op jit(solution)/shard_map/ppermute | solution.py:395
  110.8 1.3 collective-permute-start.13
  112.1 9.5 %collective-permute-start.22 = (f32[32]{0:T(128)S(1)}, f32[32]{0:T(128)S(1)}, u32[]{:S(2)}, u32[]{:S(2)}) collective-permute-start(f32[32]{0:T(128)S(1)} %add.126), channel_id=1, source_target_pairs={{0,2},{1,3},{2,0},{3,1},{4,6},{5,7},{6,4},{7,5},{8,10},{9,11},{10,... | collective-permute-start | bytes 392 | tf_op jit(solution)/shard_map/ppermute | solution.py:395
  121.7 2.3 %bitcast_dynamic-update-slice_fusion = (bf16[2,1,128,4096]{3,2,1,0:T(8,128)(2,1)}, bf16[2,1,128,4096]{3,2,1,0:T(8,128)(2,1)}) fusion(bf16[2,1,128,4096]{3,2,1,0:T(8,128)(2,1)} %get-tuple-element.79, s32[]{:T(128)S(6)} %select_n.126, bf16[2,128,2048]{2,1,0:T(8,128)(2,1)} %collective-permute-done.19, bf16[2,1,128,4096]{3,2,1,0:T(8,128)(2,1)} %get-tuple-element.76), kind=kLoop, calls=%fused_computation.14 | loop fusion | bytes 2097156 | tf_op jit(solution)/shard_map/dynamic_update_slice | solution.py:402
  124.0 1.4 collective-permute-done.22
  125.4 1.3 collective-permute-start.14
  126.7 5.5 %collective-permute-start.23 = (f32[32]{0:T(128)S(1)}, f32[32]{0:T(128)S(1)}, u32[]{:S(2)}, u32[]{:S(2)}) collective-permute-start(f32[32]{0:T(128)S(1)} %add.127), channel_id=1, source_target_pairs={{0,4},{1,5},{2,6},{3,7},{4,0},{5,1},{6,2},{7,3},{8,12},{9,13},{10,... | collective-permute-start | bytes 392 | tf_op jit(solution)/shard_map/ppermute | solution.py:395
  132.2 1.1 fusion
  133.3 0.7 collective-permute-done.23
  133.9 26.1 %collective-permute-start.24 = (f32[32]{0:T(128)S(1)}, f32[32]{0:T(128)S(1)}, u32[]{:S(2)}, u32[]{:S(2)}) collective-permute-start(f32[32]{0:T(128)S(1)} %add.128), channel_id=1, source_target_pairs={{0,8},{1,9},{2,10},{3,11},{4,12},{5,13},{6,14},{7,15},{8,0},{9,1},... | collective-permute-start | bytes 392 | tf_op jit(solution)/shard_map/ppermute | solution.py:395
  160.0 1.4 add_convert_fusion.1
  161.4 0.5 add.129
  161.9 0.2 fusion.2
  162.2 2.5 %collective-permute-start.26 = (bf16[2,2,128,256]{3,2,1,0:T(8,128)(2,1)S(1)}, bf16[2,2,128,256]{3,2,1,0:T(8,128)(2,1)S(1)}, u32[]{:S(2)}, u32[]{:S(2)}) collective-permute-start(bf16[2,2,128,256]{3,2,1,0:T(8,128)(2,1)S(1)} %fusion.7), channel_id=1, source_target_pairs={{0,1},{1,0},{2,3},{3,2},{4,5},{5,4},{6,7},{7,6},{8,9},{9,8},{10,11... | collective-permute-start | bytes 786440 | tf_op jit(solution)/shard_map/ppermute | solution.py:321
  164.7 1.2 collective-permute-done.26
  165.9 0.8 pad_maximum_fusion
  (60 shorter events, 1.0 us)
Async XLA Ops:
  0.6 5.0 %copy-start = (bf16[2,1,128,4096]{3,2,1,0:T(8,128)(2,1)S(1)}, bf16[2,1,128,4096]{3,2,1,0:T(8,128)(2,1)}, u32[]{:S(2)}) copy-start(bf16[2,1,128,4096]{3,2,1,0:T(8,128)(2,1)} %q_own.3) | copy-start | bytes 6291460
  2.8 2.7 %collective-permute-start = (bf16[2,2,128,256]{3,2,1,0:T(8,128)(2,1)S(1)}, bf16[2,2,128,256]{3,2,1,0:T(8,128)(2,1)S(1)}, u32[]{:S(2)}, u32[]{:S(2)}) collective-permute-start(bf16[2,2,128,256]{3,2,1,0:T(8,128)(2,1)S(1)} %constant_dynamic-slice_fusion.1), channel_id=1, source_target_pairs={{0,1},{1,0},{2,3},{3,2},{4,5},{5,4},{6,7},{7,6},{8,9},{9,8},{10,11... | collective-permute-start | bytes 786440 | tf_op jit(solution)/shard_map/ppermute | solution.py:321
  5.6 2.0 %copy-start.1 = (bf16[2,1,128,4096]{3,2,1,0:T(8,128)(2,1)S(1)}, bf16[2,1,128,4096]{3,2,1,0:T(8,128)(2,1)}, u32[]{:S(2)}) copy-start(bf16[2,1,128,4096]{3,2,1,0:T(8,128)(2,1)} %g_own.3) | copy-start | bytes 6291460
  5.7 8.3 %copy-start.18 = (s32[2,1,4]{2,1,0:T(1,128)S(1)}, s32[2,1,4]{2,1,0:T(1,128)}, u32[]{:S(2)}) copy-start(s32[2,1,4]{2,1,0:T(1,128)} %param.10) | copy-start | bytes 100
  6.8 46.7 %collective-permute-start.1 = (bf16[2,128,2048]{2,1,0:T(8,128)(2,1)}, bf16[2,128,2048]{2,1,0:T(8,128)(2,1)}, u32[]{:S(2)}, u32[]{:S(2)}) collective-permute-start(bf16[2,128,2048]{2,1,0:T(8,128)(2,1)} %dynamic-slice_bitcast_fusion.1), channel_id=1, source_target_pairs={{0,1},{1,0},{2,3},{3,2},{4,5},{5,4},{6,7},{7,6},{8,9},{9,8},{10,11... | collective-permute-start | bytes 3145736 | tf_op jit(solution)/shard_map/ppermute | solution.py:321
  8.7 47.8 %collective-permute-start.2 = (bf16[2,128,2048]{2,1,0:T(8,128)(2,1)}, bf16[2,128,2048]{2,1,0:T(8,128)(2,1)}, u32[]{:S(2)}, u32[]{:S(2)}) collective-permute-start(bf16[2,128,2048]{2,1,0:T(8,128)(2,1)} %dynamic-slice_bitcast_fusion), channel_id=1, source_target_pairs={{0,1},{1,0},{2,3},{3,2},{4,5},{5,4},{6,7},{7,6},{8,9},{9,8},{10,11... | collective-permute-start | bytes 3145736 | tf_op jit(solution)/shard_map/ppermute | solution.py:321
  9.0 17.7 %collective-permute-start.10 = (bf16[2,2,128,256]{3,2,1,0:T(8,128)(2,1)S(1)}, bf16[2,2,128,256]{3,2,1,0:T(8,128)(2,1)S(1)}, u32[]{:S(2)}, u32[]{:S(2)}) collective-permute-start(bf16[2,2,128,256]{3,2,1,0:T(8,128)(2,1)S(1)} %get-tuple-element.49.refs_0_), channel_id=1, source_target_pairs={{0,8},{1,9},{2,10},{3,11},{4,12},{5,13},{6,14},{7,15},{16,24},{17,... | collective-permute-start | bytes 786440 | tf_op jit(solution)/shard_map/ppermute | solution.py:312
  19.7 15.4 %collective-permute-start.7 = (bf16[2,2,128,256]{3,2,1,0:T(8,128)(2,1)S(1)}, bf16[2,2,128,256]{3,2,1,0:T(8,128)(2,1)S(1)}, u32[]{:S(2)}, u32[]{:S(2)}) collective-permute-start(bf16[2,2,128,256]{3,2,1,0:T(8,128)(2,1)S(1)} %get-tuple-element.49.refs_0_), channel_id=1, source_target_pairs={{0,2},{1,3},{2,4},{3,5},{4,6},{5,7},{6,8},{7,9},{8,10},{9,11},{10,... | collective-permute-start | bytes 786440 | tf_op jit(solution)/shard_map/ppermute | solution.py:312
  24.4 22.9 %collective-permute-start.8 = (bf16[2,2,128,256]{3,2,1,0:T(8,128)(2,1)S(1)}, bf16[2,2,128,256]{3,2,1,0:T(8,128)(2,1)S(1)}, u32[]{:S(2)}, u32[]{:S(2)}) collective-permute-start(bf16[2,2,128,256]{3,2,1,0:T(8,128)(2,1)S(1)} %get-tuple-element.49.refs_0_), channel_id=1, source_target_pairs={{0,4},{1,5},{2,6},{3,7},{4,8},{5,9},{6,10},{7,11},{8,12},{9,13},{1... | collective-permute-start | bytes 786440 | tf_op jit(solution)/shard_map/ppermute | solution.py:312
  26.7 25.4 %collective-permute-start.9 = (bf16[2,2,128,256]{3,2,1,0:T(8,128)(2,1)S(1)}, bf16[2,2,128,256]{3,2,1,0:T(8,128)(2,1)}, u32[]{:S(2)}, u32[]{:S(2)}) collective-permute-start(bf16[2,2,128,256]{3,2,1,0:T(8,128)(2,1)S(1)} %get-tuple-element.49.refs_0_), channel_id=1, source_target_pairs={{0,6},{1,7},{2,8},{3,9},{4,10},{5,11},{6,12},{7,13},{8,14},{9,15},... | collective-permute-start | bytes 786440 | tf_op jit(solution)/shard_map/ppermute | solution.py:312
  35.1 37.9 %collective-permute-start.3 = (bf16[2,2,128,256]{3,2,1,0:T(8,128)(2,1)S(1)}, bf16[2,2,128,256]{3,2,1,0:T(8,128)(2,1)S(1)}, u32[]{:S(2)}, u32[]{:S(2)}) collective-permute-start(bf16[2,2,128,256]{3,2,1,0:T(8,128)(2,1)S(1)} %get-tuple-element.51.refs_0_), channel_id=1, source_target_pairs={{0,2},{1,3},{2,4},{3,5},{4,6},{5,7},{6,8},{7,9},{8,10},{9,11},{10,... | collective-permute-start | bytes 786440 | tf_op jit(solution)/shard_map/ppermute | solution.py:312
  47.3 0.7 copy-start.4
  48.0 25.7 %collective-permute-start.4 = (bf16[2,2,128,256]{3,2,1,0:T(8,128)(2,1)S(1)}, bf16[2,2,128,256]{3,2,1,0:T(8,128)(2,1)S(1)}, u32[]{:S(2)}, u32[]{:S(2)}) collective-permute-start(bf16[2,2,128,256]{3,2,1,0:T(8,128)(2,1)S(1)} %get-tuple-element.51.refs_0_), channel_id=1, source_target_pairs={{0,4},{1,5},{2,6},{3,7},{4,8},{5,9},{6,10},{7,11},{8,12},{9,13},{1... | collective-permute-start | bytes 786440 | tf_op jit(solution)/shard_map/ppermute | solution.py:312
  52.1 22.3 %collective-permute-start.5 = (bf16[2,2,128,256]{3,2,1,0:T(8,128)(2,1)S(1)}, bf16[2,2,128,256]{3,2,1,0:T(8,128)(2,1)S(1)}, u32[]{:S(2)}, u32[]{:S(2)}) collective-permute-start(bf16[2,2,128,256]{3,2,1,0:T(8,128)(2,1)S(1)} %get-tuple-element.51.refs_0_), channel_id=1, source_target_pairs={{0,6},{1,7},{2,8},{3,9},{4,10},{5,11},{6,12},{7,13},{8,14},{9,15},... | collective-permute-start | bytes 786440 | tf_op jit(solution)/shard_map/ppermute | solution.py:312
  53.5 21.7 %collective-permute-start.6 = (bf16[2,2,128,256]{3,2,1,0:T(8,128)(2,1)S(1)}, bf16[2,2,128,256]{3,2,1,0:T(8,128)(2,1)S(1)}, u32[]{:S(2)}, u32[]{:S(2)}) collective-permute-start(bf16[2,2,128,256]{3,2,1,0:T(8,128)(2,1)S(1)} %get-tuple-element.51.refs_0_), channel_id=1, source_target_pairs={{0,8},{1,9},{2,10},{3,11},{4,12},{5,13},{6,14},{7,15},{16,24},{17,... | collective-permute-start | bytes 786440 | tf_op jit(solution)/shard_map/ppermute | solution.py:312
  56.4 1.6 copy-start.2
  58.0 0.9 copy-start.5
  71.6 0.7 copy-start.8
  72.3 0.7 copy-start.11
  73.0 0.7 copy-start.9
  73.7 0.7 copy-start.12
  74.4 0.7 copy-start.14
  75.1 0.7 copy-start.16
  75.8 33.0 %collective-permute-start.19 = (bf16[2,128,2048]{2,1,0:T(8,128)(2,1)}, bf16[2,128,2048]{2,1,0:T(8,128)(2,1)}, u32[]{:S(2)}, u32[]{:S(2)}) collective-permute-start(bf16[2,128,2048]{2,1,0:T(8,128)(2,1)} %get-tuple-element.66), channel_id=1, source_target_pairs={{0,1},{1,0},{2,3},{3,2},{4,5},{5,4},{6,7},{7,6},{8,9},{9,8},{10,11... | collective-permute-start | bytes 3145736 | tf_op jit(solution)/shard_map/ppermute | solution.py:321
  76.6 28.6 %collective-permute-start.15 = (bf16[2,2,128,256]{3,2,1,0:T(8,128)(2,1)}, bf16[2,2,128,256]{3,2,1,0:T(8,128)(2,1)}, u32[]{:S(2)}, u32[]{:S(2)}) collective-permute-start(bf16[2,2,128,256]{3,2,1,0:T(8,128)(2,1)} %get-tuple-element.62), channel_id=1, source_target_pairs={{2,0},{3,1},{4,2},{5,3},{6,4},{7,5},{8,6},{9,7},{10,8},{11,9},{12,... | collective-permute-start | bytes 786440 | tf_op jit(solution)/shard_map/ppermute | solution.py:312
  77.9 27.3 %collective-permute-start.16 = (bf16[2,2,128,256]{3,2,1,0:T(8,128)(2,1)}, bf16[2,2,128,256]{3,2,1,0:T(8,128)(2,1)}, u32[]{:S(2)}, u32[]{:S(2)}) collective-permute-start(bf16[2,2,128,256]{3,2,1,0:T(8,128)(2,1)} %get-tuple-element.63), channel_id=1, source_target_pairs={{4,0},{5,1},{6,2},{7,3},{8,4},{9,5},{10,6},{11,7},{12,8},{13,9},{1... | collective-permute-start | bytes 786440 | tf_op jit(solution)/shard_map/ppermute | solution.py:312
  79.5 5.1 %collective-permute-start.20 = (f32[32]{0:T(128)S(1)}, f32[32]{0:T(128)S(1)}, u32[]{:S(2)}, u32[]{:S(2)}) collective-permute-start(f32[32]{0:T(128)S(1)} %compare_select_fusion.1), channel_id=1, source_target_pairs={{0,112},{16,96},{32,80},{48,64},{64,48},{80,32},{96,16},{112,0},{1... | collective-permute-start | bytes 392 | tf_op jit(solution)/shard_map/ppermute | solution.py:372
  83.3 23.2 %collective-permute-start.17 = (bf16[2,2,128,256]{3,2,1,0:T(8,128)(2,1)}, bf16[2,2,128,256]{3,2,1,0:T(8,128)(2,1)}, u32[]{:S(2)}, u32[]{:S(2)}) collective-permute-start(bf16[2,2,128,256]{3,2,1,0:T(8,128)(2,1)} %copy-done.11), channel_id=1, source_target_pairs={{6,0},{7,1},{8,2},{9,3},{10,4},{11,5},{12,6},{13,7},{14,8},{15,9},... | collective-permute-start | bytes 786440 | tf_op jit(solution)/shard_map/ppermute | solution.py:312
  84.6 24.3 %collective-permute-start.18 = (bf16[2,2,128,256]{3,2,1,0:T(8,128)(2,1)}, bf16[2,2,128,256]{3,2,1,0:T(8,128)(2,1)}, u32[]{:S(2)}, u32[]{:S(2)}) collective-permute-start(bf16[2,2,128,256]{3,2,1,0:T(8,128)(2,1)} %copy-done.8), channel_id=1, source_target_pairs={{8,0},{9,1},{10,2},{11,3},{12,4},{13,5},{14,6},{15,7},{24,16},{25,... | collective-permute-start | bytes 786440 | tf_op jit(solution)/shard_map/ppermute | solution.py:312
  85.9 1.6 copy-start.3
  87.5 0.9 copy-start.10
  88.4 0.9 copy-start.13
  89.4 0.9 copy-start.15
  90.3 0.9 copy-start.17
  103.8 0.7 copy-start.6
  104.5 0.7 copy-start.7
  105.2 21.5 %collective-permute-start.25 = (bf16[2,128,2048]{2,1,0:T(8,128)(2,1)}, bf16[2,128,2048]{2,1,0:T(8,128)(2,1)S(1)}, u32[]{:S(2)}, u32[]{:S(2)}) collective-permute-start(bf16[2,128,2048]{2,1,0:T(8,128)(2,1)} %get-tuple-element.78), channel_id=1, source_target_pairs={{0,1},{1,0},{2,3},{3,2},{4,5},{5,4},{6,7},{7,6},{8,9},{9,8},{10,11... | collective-permute-start | bytes 3145736 | tf_op jit(solution)/shard_map/ppermute | solution.py:321
  105.2 56.7 %collective-permute-start.11 = (bf16[2,2,128,256]{3,2,1,0:T(8,128)(2,1)}, bf16[2,2,128,256]{3,2,1,0:T(8,128)(2,1)S(1)}, u32[]{:S(2)}, u32[]{:S(2)}) collective-permute-start(bf16[2,2,128,256]{3,2,1,0:T(8,128)(2,1)} %copy-done.7), channel_id=1, source_target_pairs={{2,0},{3,1},{4,2},{5,3},{6,4},{7,5},{8,6},{9,7},{10,8},{11,9},{12,... | collective-permute-start | bytes 786440 | tf_op jit(solution)/shard_map/ppermute | solution.py:312
  106.5 55.4 %collective-permute-start.12 = (bf16[2,2,128,256]{3,2,1,0:T(8,128)(2,1)}, bf16[2,2,128,256]{3,2,1,0:T(8,128)(2,1)S(1)}, u32[]{:S(2)}, u32[]{:S(2)}) collective-permute-start(bf16[2,2,128,256]{3,2,1,0:T(8,128)(2,1)} %copy-done.6), channel_id=1, source_target_pairs={{4,0},{5,1},{6,2},{7,3},{8,4},{9,5},{10,6},{11,7},{12,8},{13,9},{1... | collective-permute-start | bytes 786440 | tf_op jit(solution)/shard_map/ppermute | solution.py:312
  109.1 3.0 %collective-permute-start.21 = (f32[32]{0:T(128)S(1)}, f32[32]{0:T(128)S(1)}, u32[]{:S(2)}, u32[]{:S(2)}) collective-permute-start(f32[32]{0:T(128)S(1)} %fusion.11), channel_id=1, source_target_pairs={{0,1},{1,0},{2,3},{3,2},{4,5},{5,4},{6,7},{7,6},{8,9},{9,8},{10,11... | collective-permute-start | bytes 392 | tf_op jit(solution)/shard_map/ppermute | solution.py:395
  110.8 51.1 %collective-permute-start.13 = (bf16[2,2,128,256]{3,2,1,0:T(8,128)(2,1)S(1)}, bf16[2,2,128,256]{3,2,1,0:T(8,128)(2,1)S(1)}, u32[]{:S(2)}, u32[]{:S(2)}) collective-permute-start(bf16[2,2,128,256]{3,2,1,0:T(8,128)(2,1)S(1)} %get-tuple-element.60), channel_id=1, source_target_pairs={{6,0},{7,1},{8,2},{9,3},{10,4},{11,5},{12,6},{13,7},{14,8},{15,9},... | collective-permute-start | bytes 786440 | tf_op jit(solution)/shard_map/ppermute | solution.py:312
  112.1 13.2 %collective-permute-start.22 = (f32[32]{0:T(128)S(1)}, f32[32]{0:T(128)S(1)}, u32[]{:S(2)}, u32[]{:S(2)}) collective-permute-start(f32[32]{0:T(128)S(1)} %add.126), channel_id=1, source_target_pairs={{0,2},{1,3},{2,0},{3,1},{4,6},{5,7},{6,4},{7,5},{8,10},{9,11},{10,... | collective-permute-start | bytes 392 | tf_op jit(solution)/shard_map/ppermute | solution.py:395
  125.4 36.6 %collective-permute-start.14 = (bf16[2,2,128,256]{3,2,1,0:T(8,128)(2,1)S(1)}, bf16[2,2,128,256]{3,2,1,0:T(8,128)(2,1)S(1)}, u32[]{:S(2)}, u32[]{:S(2)}) collective-permute-start(bf16[2,2,128,256]{3,2,1,0:T(8,128)(2,1)S(1)} %get-tuple-element.61), channel_id=1, source_target_pairs={{8,0},{9,1},{10,2},{11,3},{12,4},{13,5},{14,6},{15,7},{24,16},{25,... | collective-permute-start | bytes 786440 | tf_op jit(solution)/shard_map/ppermute | solution.py:312
  126.7 7.2 %collective-permute-start.23 = (f32[32]{0:T(128)S(1)}, f32[32]{0:T(128)S(1)}, u32[]{:S(2)}, u32[]{:S(2)}) collective-permute-start(f32[32]{0:T(128)S(1)} %add.127), channel_id=1, source_target_pairs={{0,4},{1,5},{2,6},{3,7},{4,0},{5,1},{6,2},{7,3},{8,12},{9,13},{10,... | collective-permute-start | bytes 392 | tf_op jit(solution)/shard_map/ppermute | solution.py:395
  133.9 27.5 %collective-permute-start.24 = (f32[32]{0:T(128)S(1)}, f32[32]{0:T(128)S(1)}, u32[]{:S(2)}, u32[]{:S(2)}) collective-permute-start(f32[32]{0:T(128)S(1)} %add.128), channel_id=1, source_target_pairs={{0,8},{1,9},{2,10},{3,11},{4,12},{5,13},{6,14},{7,15},{8,0},{9,1},... | collective-permute-start | bytes 392 | tf_op jit(solution)/shard_map/ppermute | solution.py:395
  162.2 3.7 %collective-permute-start.26 = (bf16[2,2,128,256]{3,2,1,0:T(8,128)(2,1)S(1)}, bf16[2,2,128,256]{3,2,1,0:T(8,128)(2,1)S(1)}, u32[]{:S(2)}, u32[]{:S(2)}) collective-permute-start(bf16[2,2,128,256]{3,2,1,0:T(8,128)(2,1)S(1)} %fusion.7), channel_id=1, source_target_pairs={{0,1},{1,0},{2,3},{3,2},{4,5},{5,4},{6,7},{7,6},{8,9},{9,8},{10,11... | collective-permute-start | bytes 786440 | tf_op jit(solution)/shard_map/ppermute | solution.py:321

commit v4 on v3

--- a/solution.py
+++ b/solution.py
@@ -21,7 +21,7 @@
 SCALE = 1.0 / math.sqrt(HEAD_WIDTH)
 LOG2E = 1.4426950408889634
 HIDDEN = -1e30
-VMEM_BYTES = 26 * 1024 * 1024
+VMEM_BYTES = 20 * 1024 * 1024
 GROUP = 3
 SLOTS = 2 * (REACH + 1)
 HEADS = KEY_HEADS // 2
@@ -40,7 +40,7 @@
     )
 
 
-def attend_kernel(relay, refilled, meta, sink, q_own, g_own, q_got, g_got, *refs):
+def attend_kernel(relay, refilled, doc_tiles, sink, q_own, g_own, q_got, g_got, *refs):
     pieces = refs[: REACH + 1]
     refs = refs[REACH + 1 + refilled :]
     o_ref, dq_ref, out_send = refs[:3]
@@ -54,8 +54,16 @@
     step = pl.program_id(0)
     head = lax.div(step, 2)
     later = lax.rem(step, 2)
-    core = meta[2]
-    count = jnp.where(later == 1, meta[1], meta[0])
+    ctx_pos = lax.axis_index("ctx")
+    section_pos = lax.axis_index("section")
+    core = lax.rem(ctx_pos, 2)
+    layer = section_pos if relay == 0 else lax.axis_size("section") - 1 - section_pos
+    position = ctx_pos - core + later
+    end = start = jnp.int32(0)
+    for document in range(DOCS):
+        end = end + doc_tiles[relay, 0, document]
+        start = jnp.where(end <= position, end, start)
+    count = position - start + 1
     groups = lax.div(count + GROUP - 1, GROUP)
     offset = 1 - later
 
@@ -165,7 +173,7 @@
     logit = jnp.concatenate(
         [
             jnp.full(
-                (1, TILE), sink[(HEADS * core + head) * QUERY_PER_KV + i] * LOG2E, jnp.float32
+                (1, TILE), sink[layer, (HEADS * core + head) * QUERY_PER_KV + i] * LOG2E, jnp.float32
             )
             for i in range(QUERY_PER_KV)
         ],
@@ -241,7 +249,7 @@
                 wait_all(give_grads(i // 2, distance) for distance in range(REACH + 1))
 
 
-def attend(relay, meta, sink, queries, output_gradient, got, pieces, filled):
+def attend(relay, doc_tiles, sink_logits, queries, output_gradient, got, pieces, filled):
     smem = pl.BlockSpec(memory_space=pltpu.SMEM)
     whole = pl.BlockSpec(memory_space=pl.ANY)
     low = jnp.bfloat16
@@ -290,7 +298,7 @@
             transcendentals=LONGEST * HQ * TILE * TILE,
         ),
         name=f"attend_{relay}",
-    )(meta, sink, *inputs)
+    )(doc_tiles, sink_logits, *inputs)
 
 
 def shards(queries, keys, values, output_gradient, doc_tiles, sink_logits):
@@ -330,20 +338,6 @@
             [jnp.where(own_first, own, got), jnp.where(own_first, got, own)], axis=axis
         )
 
-    def meta_of(relay):
-        counts = []
-        for position in (ctx_pos - core, ctx_pos - core + 1):
-            end = start = jnp.zeros((), jnp.int32)
-            for document in range(DOCS):
-                end = end + doc_tiles[relay, 0, document]
-                start = jnp.where(end <= position, end, start)
-            counts.append(position - start + 1)
-        return jnp.stack(counts + [core]).astype(jnp.int32)
-
-    def sink_of(relay):
-        layer = section_pos if relay == 0 else section_count - 1 - section_pos
-        return lax.dynamic_index_in_dim(sink_logits, layer, 0, keepdims=False)
-
     def sink_terms(sink_part):
         mine = jnp.sum(sink_part[:, :, 0].reshape(HEADS, 2, QUERY_PER_KV), axis=1).reshape(-1)
         mine = jnp.concatenate([mine, mine])
@@ -355,41 +349,45 @@
             total = total + other.astype(jnp.float32)
         return total.astype(jnp.bfloat16)
 
-    both = jnp.stack([keys[:, 0], values[:, 0]], axis=1)
-    own = half(both, core)
-    piece = in_order(own, swapped(half(both, 1 - core)), True, 2)
+    def halves(which):
+        return jnp.stack([half(keys[:, 0], which), half(values[:, 0], which)], axis=1)
+
+    piece = in_order(halves(core), swapped(halves(1 - core)), True, 2)
     pieces = [piece[relay] for relay in range(RELAY_COUNT)]
     pieces[0], pieces[1], mate = lax.optimization_barrier((pieces[0], pieces[1], 1 - core))
     mine_first = [pieces[first]] + shifted([pieces[first]], 1)
     got = [swapped(half(array[:, 0], mate)) for array in (queries, output_gradient)]
     mine_second = [pieces[second]] + shifted([pieces[second]], 1)
     attention, query_grad, out_first, *terms_first, sink_part = attend(
-        first, meta_of(first), sink_of(first), queries, output_gradient, got, mine_first, []
+        first, doc_tiles, sink_logits, queries, output_gradient, got, mine_first, []
     )
     mine_second, sink_part = lax.optimization_barrier((mine_second, sink_part))
     sent_first = shifted(terms_first, -1)
     out_first = swapped(out_first)
-    mirrored = lax.ppermute(
-        sink_terms(sink_part),
-        "section",
-        [(s, section_count - 1 - s) for s in range(section_count)],
-    )
+    sink_first = sink_terms(sink_part)
     attention, query_grad, out_second, *terms_second, sink_part = attend(
         second,
-        meta_of(second),
-        sink_of(second),
+        doc_tiles,
+        sink_logits,
         queries,
         output_gradient,
         got,
         mine_second,
         [attention, query_grad],
     )
-    sent_first, out_first, mirrored, sink_part = lax.optimization_barrier(
-        (sent_first, out_first, mirrored, sink_part)
+    sent_first, out_first, sink_first, sink_part, out_second, terms_second = (
+        lax.optimization_barrier(
+            (sent_first, out_first, sink_first, sink_part, out_second, terms_second)
+        )
     )
     sent_second = shifted(terms_second, -1)
     out_second = swapped(out_second)
-    sink_grad = sink_terms(sink_part) + mirrored
+    out_second, sink_first = lax.optimization_barrier((out_second, sink_first))
+    sink_grad = sink_terms(sink_part) + lax.ppermute(
+        sink_first,
+        "section",
+        [(s, section_count - 1 - s) for s in range(section_count)],
+    )
     distance = 1
     while distance < ctx_count:
         sink_grad = sink_grad + lax.ppermute(

time: 168 us -> 148 us (0.88); the launches traced: 167 us -> 149 us
  local copies, waits for them, and re-layouts: 24.1 us -> 8.53 us
  starting transfers between devices: 89.9 us -> 103 us
  between operations: 11.3 us -> 1.08 us
  waiting for transfers between devices: 12.9 us -> 9.18 us
    unnamed x39 -> x14, local copies, waits for them, and re-layouts: 15.9 us -> 3.42 us
    ppermute x1, starting transfers between devices: 3.79 us -> 12 us  [shards(): lax.ppermute(sink_first, 'section', [(s, section_count - 1 - s) for s in...]
    ppermute x6, starting transfers between devices: 5.56 us -> 11.3 us  [swapped(): return lax.ppermute(array, 'ctx', [(c, c ^ 1) for c in range(ctx_count)])]
    ppermute x4, starting transfers between devices: 42.9 us -> 39.2 us  [shards(): lax.ppermute(sink_grad, 'ctx', [(c, c ^ distance) for c in range(ctx_coun...]
    ppermute x16, starting transfers between devices: 37.7 us -> 40.4 us  [shifted(): lax.ppermute(pieces[d + 1] if len(pieces) > 1 else pieces[0], 'ctx', [(a,...]
    ppermute x16, waiting for transfers between devices: 8.4 us -> 6.01 us  [shifted(): lax.ppermute(pieces[d + 1] if len(pieces) > 1 else pieces[0], 'ctx', [(a,...]
    ppermute x4, waiting for transfers between devices: 2.09 us -> 0.01 us  [shards(): lax.ppermute(sink_grad, 'ctx', [(c, c ^ distance) for c in range(ctx_coun...]
  transfers between devices with their start and end apart: 27 -> 27, of which waited for: 6 -> 4; matrix products, arithmetic and copies ran while one was open for 5% -> 4% of each run, Pallas kernels for 15% -> 16%
where the time goes in v4:
time: 148 us; the launch traced here: 149 us
  starting transfers between devices  103 us (70%)
  Pallas kernels  24.2 us (16%)
  waiting for transfers between devices  9.18 us (6%)
  local copies, waits for them, and re-layouts  8.53 us (6%)
  other arithmetic  3.26 us (2%)
    ppermute x16, starting transfers between devices, shifted(): lax.ppermute(pieces[d + 1] if len(pieces) > 1 else pieces[0], 'ctx', [(a,...  40.4 us
    ppermute x4, starting transfers between devices, shards(): lax.ppermute(sink_grad, 'ctx', [(c, c ^ distance) for c in range(ctx_coun...  39.2 us
    pallas_call x2, Pallas kernels, attend(): pl.pallas_call(functools.partial(attend_kernel, relay, len(filled)), grid...  24.2 us
    ppermute x1, starting transfers between devices, shards(): lax.ppermute(sink_first, 'section', [(s, section_count - 1 - s) for s in...  12 us
    ppermute x6, starting transfers between devices, swapped(): return lax.ppermute(array, 'ctx', [(c, c ^ 1) for c in range(ctx_count)])  11.3 us
    ppermute x16, waiting for transfers between devices, shifted(): lax.ppermute(pieces[d + 1] if len(pieces) > 1 else pieces[0], 'ctx', [(a,...  6.01 us
    unnamed x14, local copies, waits for them, and re-layouts  3.42 us
    dynamic_update_slice x2, local copies, waits for them, and re-layouts, shards(): query_grad = lax.dynamic_update_slice(query_grad, got[1][None, None], place)  3.31 us
  transfers between devices with their start and end apart: 27, of which 4 were waited for; matrix products, arithmetic and copies ran while one was open for 4% of the time, Pallas kernels for 16%

profile of v4, /device:TPU:1, one launch (start us, length us, event | category | flops | bytes accessed | tf_op | source)
XLA Modules:
  0.0 149.2 jit_solution(6592653776004491882)
XLA Ops:
  0.7 1.3 constant_dynamic-slice_fusion.2
  2.0 1.5 %collective-permute-start = (bf16[2,2,128,256]{3,2,1,0:T(8,128)(2,1)S(1)}, bf16[2,2,128,256]{3,2,1,0:T(8,128)(2,1)S(1)}, u32[]{:S(2)}, u32[]{:S(2)}) collective-permute-start(bf16[2,2,128,256]{3,2,1,0:T(8,128)(2,1)S(1)} %pad_maximum_fusion.3), channel_id=1, source_target_pairs={{0,1},{1,0},{2,3},{3,2},{4,5},{5,4},{6,7},{7,6},{8,9},{9,8},{10,11... | collective-permute-start | bytes 786440 | tf_op jit(solution)/shard_map/ppermute | solution.py:329
  3.5 1.2 collective-permute-done
  4.7 0.0 copy-start.1
  4.8 0.0 copy-start.5
  4.8 0.0 copy-start.6
  4.8 0.1 dynamic-slice_bitcast_fusion.1
  4.9 0.5 collective-permute-start.1
  5.4 1.0 copy-done.1
  6.3 0.1 dynamic-slice_bitcast_fusion
  6.4 0.5 collective-permute-start.2
  6.9 4.7 %collective-permute-start.3 = (bf16[2,2,128,256]{3,2,1,0:T(8,128)(2,1)S(1)}, bf16[2,2,128,256]{3,2,1,0:T(8,128)(2,1)S(1)}, u32[]{:S(2)}, u32[]{:S(2)}) collective-permute-start(bf16[2,2,128,256]{3,2,1,0:T(8,128)(2,1)S(1)} %get-tuple-element.56.refs_0_), channel_id=1, source_target_pairs={{0,2},{1,3},{2,4},{3,5},{4,6},{5,7},{6,8},{7,9},{8,10},{9,11},{10,... | collective-permute-start | bytes 786440 | tf_op jit(solution)/shard_map/ppermute | solution.py:320
  11.6 3.2 %collective-permute-start.4 = (bf16[2,2,128,256]{3,2,1,0:T(8,128)(2,1)S(1)}, bf16[2,2,128,256]{3,2,1,0:T(8,128)(2,1)S(1)}, u32[]{:S(2)}, u32[]{:S(2)}) collective-permute-start(bf16[2,2,128,256]{3,2,1,0:T(8,128)(2,1)S(1)} %get-tuple-element.56.refs_0_), channel_id=1, source_target_pairs={{0,4},{1,5},{2,6},{3,7},{4,8},{5,9},{6,10},{7,11},{8,12},{9,13},{1... | collective-permute-start | bytes 786440 | tf_op jit(solution)/shard_map/ppermute | solution.py:320
  14.8 3.9 %collective-permute-start.5 = (bf16[2,2,128,256]{3,2,1,0:T(8,128)(2,1)S(1)}, bf16[2,2,128,256]{3,2,1,0:T(8,128)(2,1)S(1)}, u32[]{:S(2)}, u32[]{:S(2)}) collective-permute-start(bf16[2,2,128,256]{3,2,1,0:T(8,128)(2,1)S(1)} %get-tuple-element.56.refs_0_), channel_id=1, source_target_pairs={{0,6},{1,7},{2,8},{3,9},{4,10},{5,11},{6,12},{7,13},{8,14},{9,15},... | collective-permute-start | bytes 786440 | tf_op jit(solution)/shard_map/ppermute | solution.py:320
  18.7 0.0 collective-permute-done.3.refs_1_
  18.7 5.1 %collective-permute-start.6 = (bf16[2,2,128,256]{3,2,1,0:T(8,128)(2,1)S(1)}, bf16[2,2,128,256]{3,2,1,0:T(8,128)(2,1)S(1)}, u32[]{:S(2)}, u32[]{:S(2)}) collective-permute-start(bf16[2,2,128,256]{3,2,1,0:T(8,128)(2,1)S(1)} %get-tuple-element.56.refs_0_), channel_id=1, source_target_pairs={{0,8},{1,9},{2,10},{3,11},{4,12},{5,13},{6,14},{7,15},{16,24},{17,... | collective-permute-start | bytes 786440 | tf_op jit(solution)/shard_map/ppermute | solution.py:320
  23.8 6.0 %collective-permute-done.4.refs_2_ = bf16[2,2,128,256]{3,2,1,0:T(8,128)(2,1)S(1)} collective-permute-done((bf16[2,2,128,256]{3,2,1,0:T(8,128)(2,1)S(1)}, bf16[2,2,128,256]{3,2,1,0:T(8,128)(2,1)S(1)}, u32[]{:S(2)}, u32[]{:S(2)}) %collective-permute-start.4) | collective-permute-done | bytes 262176 | tf_op jit(solution)/shard_map/ppermute | solution.py:320
  29.8 1.3 collective-permute-start.12
  31.1 4.7 %collective-permute-start.13 = (bf16[2,2,128,256]{3,2,1,0:T(8,128)(2,1)S(1)}, bf16[2,2,128,256]{3,2,1,0:T(8,128)(2,1)S(1)}, u32[]{:S(2)}, u32[]{:S(2)}) collective-permute-start(bf16[2,2,128,256]{3,2,1,0:T(8,128)(2,1)S(1)} %get-tuple-element.65.refs_0_), channel_id=1, source_target_pairs={{0,4},{1,5},{2,6},{3,7},{4,8},{5,9},{6,10},{7,11},{8,12},{9,13},{1... | collective-permute-start | bytes 786440 | tf_op jit(solution)/shard_map/ppermute | solution.py:320
  35.9 0.0 collective-permute-done.6.refs_4_
  35.9 5.7 %collective-permute-start.14 = (bf16[2,2,128,256]{3,2,1,0:T(8,128)(2,1)S(1)}, bf16[2,2,128,256]{3,2,1,0:T(8,128)(2,1)S(1)}, u32[]{:S(2)}, u32[]{:S(2)}) collective-permute-start(bf16[2,2,128,256]{3,2,1,0:T(8,128)(2,1)S(1)} %get-tuple-element.65.refs_0_), channel_id=1, source_target_pairs={{0,6},{1,7},{2,8},{3,9},{4,10},{5,11},{6,12},{7,13},{8,14},{9,15},... | collective-permute-start | bytes 786440 | tf_op jit(solution)/shard_map/ppermute | solution.py:320
  41.6 1.4 collective-permute-start.15
  43.0 0.0 collective-permute-done.2.g_got
  43.1 12.1 %attend_1.1 = (bf16[2,1,128,4096]{3,2,1,0:T(8,128)(2,1)}, bf16[2,1,128,4096]{3,2,1,0:T(8,128)(2,1)}, bf16[2,128,2048]{2,1,0:T(8,128)(2,1)}, bf16[2,2,128,256]{3,...) custom-call(s32[2,1,4]{2,1,0:T(1,128)S(1)} %copy-done.6, ...), custom_call_target="tpu_custom_call" | custom-call | flops 28991029248 | bytes 9437184 | tf_op jit(solution)/shard_map/attend_1/pallas_call | solution.py:259
  55.2 1.3 collective-permute-start.7
  56.5 1.3 collective-permute-start.8
  57.8 0.0 collective-permute-done.13.refs_2_
  57.8 1.3 collective-permute-start.9
  59.1 0.0 collective-permute-done.14.refs_3_
  59.1 1.3 collective-permute-start.10
  60.4 6.5 %collective-permute-start.11 = (bf16[2,128,2048]{2,1,0:T(8,128)(2,1)}, bf16[2,128,2048]{2,1,0:T(8,128)(2,1)}, u32[]{:S(2)}, u32[]{:S(2)}) collective-permute-start(bf16[2,128,2048]{2,1,0:T(8,128)(2,1)} %get-tuple-element.61), channel_id=1, source_target_pairs={{0,1},{1,0},{2,3},{3,2},{4,5},{5,4},{6,7},{7,6},{8,9},{9,8},{10,11... | collective-permute-start | bytes 3145736 | tf_op jit(solution)/shard_map/ppermute | solution.py:329
  67.0 12.0 %attend_0.1 = (bf16[2,1,128,4096]{3,2,1,0:T(8,128)(2,1)}, bf16[2,1,128,4096]{3,2,1,0:T(8,128)(2,1)}, bf16[2,128,2048]{2,1,0:T(8,128)(2,1)S(1)}, bf16[2,2,128,256...) custom-call(s32[2,1,4]{2,1,0:T(1,128)S(1)} %copy-done.6, ...), custom_call_target="tpu_custom_call", output_to_operand_aliasing={{0}: (11, {}), {1}: (12, {})} | custom-call | flops 28991029248 | bytes 9437184 | tf_op jit(solution)/shard_map/attend_0/pallas_call | solution.py:259
  79.1 1.0 copy-done.2
  80.0 0.7 copy-done.3
  80.7 0.7 copy-done.4
  81.5 0.1 slice_reduce_fusion.1
  81.6 0.1 reshape.26
  81.7 0.1 compare_select_fusion.1
  81.7 0.0 collective-permute-done.7
  81.7 0.0 collective-permute-done.8
  81.7 0.0 collective-permute-done.9
  81.8 0.0 collective-permute-done.10
  81.8 0.1 collective-permute-start.20
  81.9 1.3 collective-permute-start.16
  83.2 1.3 collective-permute-start.17
  84.5 1.3 collective-permute-start.18
  85.8 0.1 slice_reduce_fusion
  85.9 12.0 %collective-permute-start.21 = (f32[32]{0:T(128)S(1)}, f32[32]{0:T(128)S(1)}, u32[]{:S(2)}, u32[]{:S(2)}) collective-permute-start(f32[32]{0:T(128)S(1)} %compare_select_fusion.1), channel_id=1, source_target_pairs={{0,112},{16,96},{32,80},{48,64},{64,48},{80,32},{96,16},{112,0},{1... | collective-permute-start | bytes 392 | tf_op jit(solution)/shard_map/ppermute | solution.py:386
  97.9 0.1 reshape.27
  98.0 0.8 collective-permute-done.21
  98.8 0.1 fusion.9
  98.9 0.9 collective-permute-start.22
  99.8 1.3 collective-permute-start.19
  101.1 7.4 %collective-permute-start.23 = (f32[32]{0:T(128)S(1)}, f32[32]{0:T(128)S(1)}, u32[]{:S(2)}, u32[]{:S(2)}) collective-permute-start(f32[32]{0:T(128)S(1)} %add.67), channel_id=1, source_target_pairs={{0,2},{1,3},{2,0},{3,1},{4,6},{5,7},{6,4},{7,5},{8,10},{9,11},{10,... | collective-permute-start | bytes 392 | tf_op jit(solution)/shard_map/ppermute | solution.py:393
  108.5 2.3 %bitcast_dynamic-update-slice_fusion.1 = (bf16[2,1,128,4096]{3,2,1,0:T(8,128)(2,1)}, bf16[2,1,128,4096]{3,2,1,0:T(8,128)(2,1)}) fusion(bf16[2,1,128,4096]{3,2,1,0:T(8,128)(2,1)} %get-tuple-element.95, s32[]{:T(128)S(6)} %select_n.63, bf16[2,128,2048]{2,1,0:T(8,128)(2,1)} %collective-permute-done.11, bf16[2,1,128,4096]{3,2,1,0:T(8,128)(2,1)} %get-tuple-element.92), kind=kLoop, calls=%fused_computation.11 | loop fusion | bytes 2097156 | tf_op jit(solution)/shard_map/dynamic_update_slice | solution.py:400
  110.8 17.7 %collective-permute-start.24 = (f32[32]{0:T(128)S(1)}, f32[32]{0:T(128)S(1)}, u32[]{:S(2)}, u32[]{:S(2)}) collective-permute-start(f32[32]{0:T(128)S(1)} %add.68), channel_id=1, source_target_pairs={{0,4},{1,5},{2,6},{3,7},{4,0},{5,1},{6,2},{7,3},{8,12},{9,13},{10,... | collective-permute-start | bytes 392 | tf_op jit(solution)/shard_map/ppermute | solution.py:393
  128.5 1.4 add_convert_fusion.1
  129.9 13.2 %collective-permute-start.25 = (f32[32]{0:T(128)S(1)}, f32[32]{0:T(128)S(1)}, u32[]{:S(2)}, u32[]{:S(2)}) collective-permute-start(f32[32]{0:T(128)S(1)} %add.69), channel_id=1, source_target_pairs={{0,8},{1,9},{2,10},{3,11},{4,12},{5,13},{6,14},{7,15},{8,0},{9,1},... | collective-permute-start | bytes 392 | tf_op jit(solution)/shard_map/ppermute | solution.py:393
  143.1 1.0 bitcast_dynamic-update-slice_fusion
  144.1 0.5 add.70
  144.7 0.2 fusion
  144.9 2.3 %collective-permute-start.26 = (bf16[2,2,128,256]{3,2,1,0:T(8,128)(2,1)S(1)}, bf16[2,2,128,256]{3,2,1,0:T(8,128)(2,1)S(1)}, u32[]{:S(2)}, u32[]{:S(2)}) collective-permute-start(bf16[2,2,128,256]{3,2,1,0:T(8,128)(2,1)S(1)} %fusion.5), channel_id=1, source_target_pairs={{0,1},{1,0},{2,3},{3,2},{4,5},{5,4},{6,7},{7,6},{8,9},{9,8},{10,11... | collective-permute-start | bytes 786440 | tf_op jit(solution)/shard_map/ppermute | solution.py:329
  147.2 1.2 collective-permute-done.26
  148.4 0.8 pad_maximum_fusion
  (31 shorter events, 0.3 us)
Async XLA Ops:
  0.6 4.1 %copy-start = (bf16[2,1,128,4096]{3,2,1,0:T(8,128)(2,1)S(1)}, bf16[2,1,128,4096]{3,2,1,0:T(8,128)(2,1)}, u32[]{:S(2)}) copy-start(bf16[2,1,128,4096]{3,2,1,0:T(8,128)(2,1)} %q_own.3) | copy-start | bytes 6291460
  2.0 2.7 %collective-permute-start = (bf16[2,2,128,256]{3,2,1,0:T(8,128)(2,1)S(1)}, bf16[2,2,128,256]{3,2,1,0:T(8,128)(2,1)S(1)}, u32[]{:S(2)}, u32[]{:S(2)}) collective-permute-start(bf16[2,2,128,256]{3,2,1,0:T(8,128)(2,1)S(1)} %pad_maximum_fusion.3), channel_id=1, source_target_pairs={{0,1},{1,0},{2,3},{3,2},{4,5},{5,4},{6,7},{7,6},{8,9},{9,8},{10,11... | collective-permute-start | bytes 786440 | tf_op jit(solution)/shard_map/ppermute | solution.py:329
  4.7 1.6 %copy-start.1 = (bf16[2,1,128,4096]{3,2,1,0:T(8,128)(2,1)S(1)}, bf16[2,1,128,4096]{3,2,1,0:T(8,128)(2,1)}, u32[]{:S(2)}) copy-start(bf16[2,1,128,4096]{3,2,1,0:T(8,128)(2,1)} %g_own.3) | copy-start | bytes 6291460
  4.8 38.3 %copy-start.5 = (f32[8,32]{1,0:T(8,128)S(1)}, f32[8,32]{1,0:T(8,128)}, u32[]{:S(2)}) copy-start(f32[8,32]{1,0:T(8,128)} %sink.3) | copy-start | bytes 3076
  4.8 38.3 %copy-start.6 = (s32[2,1,4]{2,1,0:T(1,128)S(1)}, s32[2,1,4]{2,1,0:T(1,128)}, u32[]{:S(2)}) copy-start(s32[2,1,4]{2,1,0:T(1,128)} %doc_tiles.3) | copy-start | bytes 100
  4.9 36.7 %collective-permute-start.1 = (bf16[2,128,2048]{2,1,0:T(8,128)(2,1)S(1)}, bf16[2,128,2048]{2,1,0:T(8,128)(2,1)S(1)}, u32[]{:S(2)}, u32[]{:S(2)}) collective-permute-start(bf16[2,128,2048]{2,1,0:T(8,128)(2,1)S(1)} %dynamic-slice_bitcast_fusion.1), channel_id=1, source_target_pairs={{0,1},{1,0},{2,3},{3,2},{4,5},{5,4},{6,7},{7,6},{8,9},{9,8},{10,11... | collective-permute-start | bytes 3145736 | tf_op jit(solution)/shard_map/ppermute | solution.py:329
  6.4 36.6 %collective-permute-start.2 = (bf16[2,128,2048]{2,1,0:T(8,128)(2,1)S(1)}, bf16[2,128,2048]{2,1,0:T(8,128)(2,1)S(1)}, u32[]{:S(2)}, u32[]{:S(2)}) collective-permute-start(bf16[2,128,2048]{2,1,0:T(8,128)(2,1)S(1)} %dynamic-slice_bitcast_fusion), channel_id=1, source_target_pairs={{0,1},{1,0},{2,3},{3,2},{4,5},{5,4},{6,7},{7,6},{8,9},{9,8},{10,11... | collective-permute-start | bytes 3145736 | tf_op jit(solution)/shard_map/ppermute | solution.py:329
  6.9 11.8 %collective-permute-start.3 = (bf16[2,2,128,256]{3,2,1,0:T(8,128)(2,1)S(1)}, bf16[2,2,128,256]{3,2,1,0:T(8,128)(2,1)S(1)}, u32[]{:S(2)}, u32[]{:S(2)}) collective-permute-start(bf16[2,2,128,256]{3,2,1,0:T(8,128)(2,1)S(1)} %get-tuple-element.56.refs_0_), channel_id=1, source_target_pairs={{0,2},{1,3},{2,4},{3,5},{4,6},{5,7},{6,8},{7,9},{8,10},{9,11},{10,... | collective-permute-start | bytes 786440 | tf_op jit(solution)/shard_map/ppermute | solution.py:320
  11.6 18.2 %collective-permute-start.4 = (bf16[2,2,128,256]{3,2,1,0:T(8,128)(2,1)S(1)}, bf16[2,2,128,256]{3,2,1,0:T(8,128)(2,1)S(1)}, u32[]{:S(2)}, u32[]{:S(2)}) collective-permute-start(bf16[2,2,128,256]{3,2,1,0:T(8,128)(2,1)S(1)} %get-tuple-element.56.refs_0_), channel_id=1, source_target_pairs={{0,4},{1,5},{2,6},{3,7},{4,8},{5,9},{6,10},{7,11},{8,12},{9,13},{1... | collective-permute-start | bytes 786440 | tf_op jit(solution)/shard_map/ppermute | solution.py:320
  14.8 16.3 %collective-permute-start.5 = (bf16[2,2,128,256]{3,2,1,0:T(8,128)(2,1)S(1)}, bf16[2,2,128,256]{3,2,1,0:T(8,128)(2,1)S(1)}, u32[]{:S(2)}, u32[]{:S(2)}) collective-permute-start(bf16[2,2,128,256]{3,2,1,0:T(8,128)(2,1)S(1)} %get-tuple-element.56.refs_0_), channel_id=1, source_target_pairs={{0,6},{1,7},{2,8},{3,9},{4,10},{5,11},{6,12},{7,13},{8,14},{9,15},... | collective-permute-start | bytes 786440 | tf_op jit(solution)/shard_map/ppermute | solution.py:320
  18.7 17.2 %collective-permute-start.6 = (bf16[2,2,128,256]{3,2,1,0:T(8,128)(2,1)S(1)}, bf16[2,2,128,256]{3,2,1,0:T(8,128)(2,1)S(1)}, u32[]{:S(2)}, u32[]{:S(2)}) collective-permute-start(bf16[2,2,128,256]{3,2,1,0:T(8,128)(2,1)S(1)} %get-tuple-element.56.refs_0_), channel_id=1, source_target_pairs={{0,8},{1,9},{2,10},{3,11},{4,12},{5,13},{6,14},{7,15},{16,24},{17,... | collective-permute-start | bytes 786440 | tf_op jit(solution)/shard_map/ppermute | solution.py:320
  29.8 26.7 %collective-permute-start.12 = (bf16[2,2,128,256]{3,2,1,0:T(8,128)(2,1)S(1)}, bf16[2,2,128,256]{3,2,1,0:T(8,128)(2,1)S(1)}, u32[]{:S(2)}, u32[]{:S(2)}) collective-permute-start(bf16[2,2,128,256]{3,2,1,0:T(8,128)(2,1)S(1)} %get-tuple-element.65.refs_0_), channel_id=1, source_target_pairs={{0,2},{1,3},{2,4},{3,5},{4,6},{5,7},{6,8},{7,9},{8,10},{9,11},{10,... | collective-permute-start | bytes 786440 | tf_op jit(solution)/shard_map/ppermute | solution.py:320
  31.1 26.7 %collective-permute-start.13 = (bf16[2,2,128,256]{3,2,1,0:T(8,128)(2,1)S(1)}, bf16[2,2,128,256]{3,2,1,0:T(8,128)(2,1)S(1)}, u32[]{:S(2)}, u32[]{:S(2)}) collective-permute-start(bf16[2,2,128,256]{3,2,1,0:T(8,128)(2,1)S(1)} %get-tuple-element.65.refs_0_), channel_id=1, source_target_pairs={{0,4},{1,5},{2,6},{3,7},{4,8},{5,9},{6,10},{7,11},{8,12},{9,13},{1... | collective-permute-start | bytes 786440 | tf_op jit(solution)/shard_map/ppermute | solution.py:320
  35.9 23.3 %collective-permute-start.14 = (bf16[2,2,128,256]{3,2,1,0:T(8,128)(2,1)S(1)}, bf16[2,2,128,256]{3,2,1,0:T(8,128)(2,1)S(1)}, u32[]{:S(2)}, u32[]{:S(2)}) collective-permute-start(bf16[2,2,128,256]{3,2,1,0:T(8,128)(2,1)S(1)} %get-tuple-element.65.refs_0_), channel_id=1, source_target_pairs={{0,6},{1,7},{2,8},{3,9},{4,10},{5,11},{6,12},{7,13},{8,14},{9,15},... | collective-permute-start | bytes 786440 | tf_op jit(solution)/shard_map/ppermute | solution.py:320
  41.6 18.8 %collective-permute-start.15 = (bf16[2,2,128,256]{3,2,1,0:T(8,128)(2,1)S(1)}, bf16[2,2,128,256]{3,2,1,0:T(8,128)(2,1)S(1)}, u32[]{:S(2)}, u32[]{:S(2)}) collective-permute-start(bf16[2,2,128,256]{3,2,1,0:T(8,128)(2,1)S(1)} %get-tuple-element.65.refs_0_), channel_id=1, source_target_pairs={{0,8},{1,9},{2,10},{3,11},{4,12},{5,13},{6,14},{7,15},{16,24},{17,... | collective-permute-start | bytes 786440 | tf_op jit(solution)/shard_map/ppermute | solution.py:320
  55.2 26.5 %collective-permute-start.7 = (bf16[2,2,128,256]{3,2,1,0:T(8,128)(2,1)}, bf16[2,2,128,256]{3,2,1,0:T(8,128)(2,1)}, u32[]{:S(2)}, u32[]{:S(2)}) collective-permute-start(bf16[2,2,128,256]{3,2,1,0:T(8,128)(2,1)} %get-tuple-element.57), channel_id=1, source_target_pairs={{2,0},{3,1},{4,2},{5,3},{6,4},{7,5},{8,6},{9,7},{10,8},{11,9},{12,... | collective-permute-start | bytes 786440 | tf_op jit(solution)/shard_map/ppermute | solution.py:320
  56.5 25.2 %collective-permute-start.8 = (bf16[2,2,128,256]{3,2,1,0:T(8,128)(2,1)}, bf16[2,2,128,256]{3,2,1,0:T(8,128)(2,1)}, u32[]{:S(2)}, u32[]{:S(2)}) collective-permute-start(bf16[2,2,128,256]{3,2,1,0:T(8,128)(2,1)} %get-tuple-element.58), channel_id=1, source_target_pairs={{4,0},{5,1},{6,2},{7,3},{8,4},{9,5},{10,6},{11,7},{12,8},{13,9},{1... | collective-permute-start | bytes 786440 | tf_op jit(solution)/shard_map/ppermute | solution.py:320
  57.8 23.9 %collective-permute-start.9 = (bf16[2,2,128,256]{3,2,1,0:T(8,128)(2,1)}, bf16[2,2,128,256]{3,2,1,0:T(8,128)(2,1)}, u32[]{:S(2)}, u32[]{:S(2)}) collective-permute-start(bf16[2,2,128,256]{3,2,1,0:T(8,128)(2,1)} %get-tuple-element.59), channel_id=1, source_target_pairs={{6,0},{7,1},{8,2},{9,3},{10,4},{11,5},{12,6},{13,7},{14,8},{15,9},... | collective-permute-start | bytes 786440 | tf_op jit(solution)/shard_map/ppermute | solution.py:320
  59.1 22.6 %collective-permute-start.10 = (bf16[2,2,128,256]{3,2,1,0:T(8,128)(2,1)}, bf16[2,2,128,256]{3,2,1,0:T(8,128)(2,1)}, u32[]{:S(2)}, u32[]{:S(2)}) collective-permute-start(bf16[2,2,128,256]{3,2,1,0:T(8,128)(2,1)} %get-tuple-element.60), channel_id=1, source_target_pairs={{8,0},{9,1},{10,2},{11,3},{12,4},{13,5},{14,6},{15,7},{24,16},{25,... | collective-permute-start | bytes 786440 | tf_op jit(solution)/shard_map/ppermute | solution.py:320
  60.4 21.3 %collective-permute-start.11 = (bf16[2,128,2048]{2,1,0:T(8,128)(2,1)}, bf16[2,128,2048]{2,1,0:T(8,128)(2,1)}, u32[]{:S(2)}, u32[]{:S(2)}) collective-permute-start(bf16[2,128,2048]{2,1,0:T(8,128)(2,1)} %get-tuple-element.61), channel_id=1, source_target_pairs={{0,1},{1,0},{2,3},{3,2},{4,5},{5,4},{6,7},{7,6},{8,9},{9,8},{10,11... | collective-permute-start | bytes 3145736 | tf_op jit(solution)/shard_map/ppermute | solution.py:329
  79.0 1.0 copy-start.2
  80.0 0.7 copy-start.3
  80.7 0.7 copy-start.4
  81.8 4.1 %collective-permute-start.20 = (bf16[2,128,2048]{2,1,0:T(8,128)(2,1)}, bf16[2,128,2048]{2,1,0:T(8,128)(2,1)S(1)}, u32[]{:S(2)}, u32[]{:S(2)}) collective-permute-start(bf16[2,128,2048]{2,1,0:T(8,128)(2,1)} %copy-done.2), channel_id=1, source_target_pairs={{0,1},{1,0},{2,3},{3,2},{4,5},{5,4},{6,7},{7,6},{8,9},{9,8},{10,11... | collective-permute-start | bytes 3145736 | tf_op jit(solution)/shard_map/ppermute | solution.py:329
  81.9 62.8 %collective-permute-start.16 = (bf16[2,2,128,256]{3,2,1,0:T(8,128)(2,1)}, bf16[2,2,128,256]{3,2,1,0:T(8,128)(2,1)S(1)}, u32[]{:S(2)}, u32[]{:S(2)}) collective-permute-start(bf16[2,2,128,256]{3,2,1,0:T(8,128)(2,1)} %copy-done.4), channel_id=1, source_target_pairs={{2,0},{3,1},{4,2},{5,3},{6,4},{7,5},{8,6},{9,7},{10,8},{11,9},{12,... | collective-permute-start | bytes 786440 | tf_op jit(solution)/shard_map/ppermute | solution.py:320
  83.2 61.5 %collective-permute-start.17 = (bf16[2,2,128,256]{3,2,1,0:T(8,128)(2,1)}, bf16[2,2,128,256]{3,2,1,0:T(8,128)(2,1)S(1)}, u32[]{:S(2)}, u32[]{:S(2)}) collective-permute-start(bf16[2,2,128,256]{3,2,1,0:T(8,128)(2,1)} %copy-done.3), channel_id=1, source_target_pairs={{4,0},{5,1},{6,2},{7,3},{8,4},{9,5},{10,6},{11,7},{12,8},{13,9},{1... | collective-permute-start | bytes 786440 | tf_op jit(solution)/shard_map/ppermute | solution.py:320
  84.5 60.2 %collective-permute-start.18 = (bf16[2,2,128,256]{3,2,1,0:T(8,128)(2,1)S(1)}, bf16[2,2,128,256]{3,2,1,0:T(8,128)(2,1)S(1)}, u32[]{:S(2)}, u32[]{:S(2)}) collective-permute-start(bf16[2,2,128,256]{3,2,1,0:T(8,128)(2,1)S(1)} %get-tuple-element.81), channel_id=1, source_target_pairs={{6,0},{7,1},{8,2},{9,3},{10,4},{11,5},{12,6},{13,7},{14,8},{15,9},... | collective-permute-start | bytes 786440 | tf_op jit(solution)/shard_map/ppermute | solution.py:320
  85.9 13.0 %collective-permute-start.21 = (f32[32]{0:T(128)S(1)}, f32[32]{0:T(128)S(1)}, u32[]{:S(2)}, u32[]{:S(2)}) collective-permute-start(f32[32]{0:T(128)S(1)} %compare_select_fusion.1), channel_id=1, source_target_pairs={{0,112},{16,96},{32,80},{48,64},{64,48},{80,32},{96,16},{112,0},{1... | collective-permute-start | bytes 392 | tf_op jit(solution)/shard_map/ppermute | solution.py:386
  98.9 2.2 %collective-permute-start.22 = (f32[32]{0:T(128)S(1)}, f32[32]{0:T(128)S(1)}, u32[]{:S(2)}, u32[]{:S(2)}) collective-permute-start(f32[32]{0:T(128)S(1)} %fusion.9), channel_id=1, source_target_pairs={{0,1},{1,0},{2,3},{3,2},{4,5},{5,4},{6,7},{7,6},{8,9},{9,8},{10,11... | collective-permute-start | bytes 392 | tf_op jit(solution)/shard_map/ppermute | solution.py:393
  99.8 44.9 %collective-permute-start.19 = (bf16[2,2,128,256]{3,2,1,0:T(8,128)(2,1)S(1)}, bf16[2,2,128,256]{3,2,1,0:T(8,128)(2,1)S(1)}, u32[]{:S(2)}, u32[]{:S(2)}) collective-permute-start(bf16[2,2,128,256]{3,2,1,0:T(8,128)(2,1)S(1)} %get-tuple-element.82), channel_id=1, source_target_pairs={{8,0},{9,1},{10,2},{11,3},{12,4},{13,5},{14,6},{15,7},{24,16},{25,... | collective-permute-start | bytes 786440 | tf_op jit(solution)/shard_map/ppermute | solution.py:320
  101.1 9.7 %collective-permute-start.23 = (f32[32]{0:T(128)S(1)}, f32[32]{0:T(128)S(1)}, u32[]{:S(2)}, u32[]{:S(2)}) collective-permute-start(f32[32]{0:T(128)S(1)} %add.67), channel_id=1, source_target_pairs={{0,2},{1,3},{2,0},{3,1},{4,6},{5,7},{6,4},{7,5},{8,10},{9,11},{10,... | collective-permute-start | bytes 392 | tf_op jit(solution)/shard_map/ppermute | solution.py:393
  110.8 19.1 %collective-permute-start.24 = (f32[32]{0:T(128)S(1)}, f32[32]{0:T(128)S(1)}, u32[]{:S(2)}, u32[]{:S(2)}) collective-permute-start(f32[32]{0:T(128)S(1)} %add.68), channel_id=1, source_target_pairs={{0,4},{1,5},{2,6},{3,7},{4,0},{5,1},{6,2},{7,3},{8,12},{9,13},{10,... | collective-permute-start | bytes 392 | tf_op jit(solution)/shard_map/ppermute | solution.py:393
  129.9 14.3 %collective-permute-start.25 = (f32[32]{0:T(128)S(1)}, f32[32]{0:T(128)S(1)}, u32[]{:S(2)}, u32[]{:S(2)}) collective-permute-start(f32[32]{0:T(128)S(1)} %add.69), channel_id=1, source_target_pairs={{0,8},{1,9},{2,10},{3,11},{4,12},{5,13},{6,14},{7,15},{8,0},{9,1},... | collective-permute-start | bytes 392 | tf_op jit(solution)/shard_map/ppermute | solution.py:393
  144.9 3.5 %collective-permute-start.26 = (bf16[2,2,128,256]{3,2,1,0:T(8,128)(2,1)S(1)}, bf16[2,2,128,256]{3,2,1,0:T(8,128)(2,1)S(1)}, u32[]{:S(2)}, u32[]{:S(2)}) collective-permute-start(bf16[2,2,128,256]{3,2,1,0:T(8,128)(2,1)S(1)} %fusion.5), channel_id=1, source_target_pairs={{0,1},{1,0},{2,3},{3,2},{4,5},{5,4},{6,7},{7,6},{8,9},{9,8},{10,11... | collective-permute-start | bytes 786440 | tf_op jit(solution)/shard_map/ppermute | solution.py:329

commit v5 on v4

--- a/solution.py
+++ b/solution.py
@@ -40,7 +40,7 @@
     )
 
 
-def attend_kernel(relay, refilled, doc_tiles, sink, q_own, g_own, q_got, g_got, *refs):
+def attend_kernel(relay, refilled, doc_tiles, sink, q_own, g_own, got, *refs):
     pieces = refs[: REACH + 1]
     refs = refs[REACH + 1 + refilled :]
     o_ref, dq_ref, out_send = refs[:3]
@@ -71,16 +71,16 @@
         return pl.ds(pl.multiple_of(j * WIDE, WIDE), WIDE)
 
     def fetch_rows(i, own):
-        pairs = ((q_own, q_got, q_in), (g_own, g_got, g_in))
+        pairs = ((q_own, q_in), (g_own, g_in))
         return [
             pltpu.make_async_copy(
                 mine.at[relay, 0, :, wide_cols(HEADS * core + i // 2)]
                 if own
-                else got.at[relay, :, pl.ds((i // 2) * WIDE, WIDE)],
+                else got.at[k, relay, :, pl.ds((i // 2) * WIDE, WIDE)],
                 to.at[i],
                 q_sem.at[k, i],
             )
-            for k, (mine, got, to) in enumerate(pairs)
+            for k, (mine, to) in enumerate(pairs)
         ]
 
     def fetch_keys(j, distance):
@@ -96,7 +96,7 @@
                 source.at[i],
                 target.at[relay, 0, :, wide_cols(HEADS * core + i // 2)]
                 if own
-                else out_send.at[k, :, pl.ds((i // 2) * WIDE, WIDE)],
+                else out_send.at[relay, k, :, pl.ds((i // 2) * WIDE, WIDE)],
                 out_sem.at[k, i],
             )
             for k, (source, target) in enumerate(((o_out, o_ref), (dq_out, dq_ref)))
@@ -253,7 +253,7 @@
     smem = pl.BlockSpec(memory_space=pltpu.SMEM)
     whole = pl.BlockSpec(memory_space=pl.ANY)
     low = jnp.bfloat16
-    inputs = [queries, output_gradient, *got, *pieces, *filled]
+    inputs = [queries, output_gradient, got, *pieces, *filled]
     first = 2 + len(inputs) - len(filled)
     rows = pltpu.VMEM((STEPS, TILE, WIDE), low)
     return pl.pallas_call(
@@ -265,7 +265,7 @@
         out_shape=[
             jax.ShapeDtypeStruct(queries.shape, low),
             jax.ShapeDtypeStruct(queries.shape, low),
-            jax.ShapeDtypeStruct((2, TILE, QUERY_PART), low),
+            jax.ShapeDtypeStruct((RELAY_COUNT, 2, TILE, QUERY_PART), low),
         ]
         + [jax.ShapeDtypeStruct((2, 2, TILE, KEY_PART), low)] * (REACH + 1)
         + [jax.ShapeDtypeStruct((STEPS, QUERY_PER_KV, HEAD_WIDTH), jnp.float32)],
@@ -356,16 +356,16 @@
     pieces = [piece[relay] for relay in range(RELAY_COUNT)]
     pieces[0], pieces[1], mate = lax.optimization_barrier((pieces[0], pieces[1], 1 - core))
     mine_first = [pieces[first]] + shifted([pieces[first]], 1)
-    got = [swapped(half(array[:, 0], mate)) for array in (queries, output_gradient)]
+    got = swapped(
+        jnp.stack([half(queries[:, 0], mate), half(output_gradient[:, 0], mate)])
+    )
     mine_second = [pieces[second]] + shifted([pieces[second]], 1)
-    attention, query_grad, out_first, *terms_first, sink_part = attend(
+    attention, query_grad, out_send, *terms_first, sink_part = attend(
         first, doc_tiles, sink_logits, queries, output_gradient, got, mine_first, []
     )
-    mine_second, sink_part = lax.optimization_barrier((mine_second, sink_part))
+    mine_second, sink_first = lax.optimization_barrier((mine_second, sink_part))
     sent_first = shifted(terms_first, -1)
-    out_first = swapped(out_first)
-    sink_first = sink_terms(sink_part)
-    attention, query_grad, out_second, *terms_second, sink_part = attend(
+    attention, query_grad, out_send, *terms_second, sink_part = attend(
         second,
         doc_tiles,
         sink_logits,
@@ -373,34 +373,31 @@
         output_gradient,
         got,
         mine_second,
-        [attention, query_grad],
-    )
-    sent_first, out_first, sink_first, sink_part, out_second, terms_second = (
-        lax.optimization_barrier(
-            (sent_first, out_first, sink_first, sink_part, out_second, terms_second)
-        )
+        [attention, query_grad, out_send],
+    )
+    sent_first, sink_first, sink_part, out_send, terms_second = lax.optimization_barrier(
+        (sent_first, sink_first, sink_part, out_send, terms_second)
     )
     sent_second = shifted(terms_second, -1)
-    out_second = swapped(out_second)
-    out_second, sink_first = lax.optimization_barrier((out_second, sink_first))
+    out_got = swapped(out_send)
+    out_got, sink_first = lax.optimization_barrier((out_got, sink_first))
     sink_grad = sink_terms(sink_part) + lax.ppermute(
-        sink_first,
+        sink_terms(sink_first),
         "section",
         [(s, section_count - 1 - s) for s in range(section_count)],
     )
-    distance = 1
-    while distance < ctx_count:
+    for turn, distance in enumerate((8, 4, 2, 1)):
+        if turn == 2:
+            sent_second, sink_grad = lax.optimization_barrier((sent_second, sink_grad))
         sink_grad = sink_grad + lax.ppermute(
             sink_grad, "ctx", [(c, c ^ distance) for c in range(ctx_count)]
         )
-        distance *= 2
-    for relay, got in ((first, out_first), (second, out_second)):
-        place = (relay, 0, 0, mate * QUERY_PART)
-        attention = lax.dynamic_update_slice(attention, got[0][None, None], place)
-        query_grad = lax.dynamic_update_slice(query_grad, got[1][None, None], place)
+    place = (0, 0, 0, mate * QUERY_PART)
+    attention = lax.dynamic_update_slice(attention, out_got[:, :1], place)
+    query_grad = lax.dynamic_update_slice(query_grad, out_got[:, 1:], place)
     first_sum = summed(terms_first, sent_first)
-    sent_second, sink_grad, first_sum, attention, query_grad = lax.optimization_barrier(
-        (sent_second, sink_grad, first_sum, attention, query_grad)
+    sent_second, first_sum, attention, query_grad = lax.optimization_barrier(
+        (sent_second, first_sum, attention, query_grad)
     )
     second_sum = summed(terms_second, sent_second)
     sums = jnp.stack([second_sum, first_sum])

time: 148 us -> 149 us (level)
  the two profiles are of different devices: /device:TPU:1 before, /device:TPU:15 now
where the time goes in v5:
time: 149 us; the launch traced here: 147 us
  starting transfers between devices  70.4 us (47%)
  Pallas kernels  37.8 us (25%)
  waiting for transfers between devices  26.2 us (18%)
  local copies, waits for them, and re-layouts  6.94 us (5%)
  other arithmetic  4.64 us (3%)
    ppermute x16, starting transfers between devices, shifted(): lax.ppermute(pieces[d + 1] if len(pieces) > 1 else pieces[0], 'ctx', [(a,...  48.1 us
    pallas_call x2, Pallas kernels, attend(): pl.pallas_call(functools.partial(attend_kernel, relay, len(filled)), grid...  37.8 us
    ppermute x4, waiting for transfers between devices, shards(): lax.ppermute(sink_grad, 'ctx', [(c, c ^ distance) for c in range(ctx_coun...  12.8 us
    ppermute x1, starting transfers between devices, shards(): lax.ppermute(sink_terms(sink_first), 'section', [(s, section_count - 1 -...  9.33 us
    ppermute x4, starting transfers between devices, swapped(): return lax.ppermute(array, 'ctx', [(c, c ^ 1) for c in range(ctx_count)])  7.72 us
    ppermute x1, waiting for transfers between devices, shards(): lax.ppermute(sink_terms(sink_first), 'section', [(s, section_count - 1 -...  6.93 us
    ppermute x16, waiting for transfers between devices, shifted(): lax.ppermute(pieces[d + 1] if len(pieces) > 1 else pieces[0], 'ctx', [(a,...  5.37 us
    ppermute x4, starting transfers between devices, shards(): lax.ppermute(sink_grad, 'ctx', [(c, c ^ distance) for c in range(ctx_coun...  5.19 us
  transfers between devices with their start and end apart: 25, of which 9 were waited for; matrix products, arithmetic and copies ran while one was open for 3% of the time, Pallas kernels for 26%

profile of v5, /device:TPU:15, one launch (start us, length us, event | category | flops | bytes accessed | tf_op | source)
XLA Modules:
  0.0 147.0 jit_solution(1124638993357844624)
XLA Ops:
  0.6 1.1 constant_dynamic-slice_fusion.2
  1.8 0.8 collective-permute-start
  2.6 1.2 collective-permute-done
  3.8 1.4 dynamic-slice_bitcast_fusion
  5.3 0.4 copy-done
  5.6 0.1 dynamic-slice_bitcast_fusion.1
  5.7 0.0 copy-start.1
  5.8 0.0 copy-start.4
  5.8 0.0 copy-start.5
  5.8 0.2 pad_maximum_fusion
  6.0 0.5 collective-permute-start.1
  6.4 4.0 %collective-permute-start.2 = (bf16[2,2,128,256]{3,2,1,0:T(8,128)(2,1)S(1)}, bf16[2,2,128,256]{3,2,1,0:T(8,128)(2,1)S(1)}, u32[]{:S(2)}, u32[]{:S(2)}) collective-permute-start(bf16[2,2,128,256]{3,2,1,0:T(8,128)(2,1)S(1)} %get-tuple-element.59.refs_0_), channel_id=1, source_target_pairs={{0,2},{1,3},{2,4},{3,5},{4,6},{5,7},{6,8},{7,9},{8,10},{9,11},{10,... | collective-permute-start | bytes 786440 | tf_op jit(solution)/shard_map/ppermute | solution.py:320
  10.5 2.9 %collective-permute-start.3 = (bf16[2,2,128,256]{3,2,1,0:T(8,128)(2,1)S(1)}, bf16[2,2,128,256]{3,2,1,0:T(8,128)(2,1)S(1)}, u32[]{:S(2)}, u32[]{:S(2)}) collective-permute-start(bf16[2,2,128,256]{3,2,1,0:T(8,128)(2,1)S(1)} %get-tuple-element.59.refs_0_), channel_id=1, source_target_pairs={{0,4},{1,5},{2,6},{3,7},{4,8},{5,9},{6,10},{7,11},{8,12},{9,13},{1... | collective-permute-start | bytes 786440 | tf_op jit(solution)/shard_map/ppermute | solution.py:320
  13.4 2.9 %collective-permute-start.4 = (bf16[2,2,128,256]{3,2,1,0:T(8,128)(2,1)S(1)}, bf16[2,2,128,256]{3,2,1,0:T(8,128)(2,1)S(1)}, u32[]{:S(2)}, u32[]{:S(2)}) collective-permute-start(bf16[2,2,128,256]{3,2,1,0:T(8,128)(2,1)S(1)} %get-tuple-element.59.refs_0_), channel_id=1, source_target_pairs={{0,6},{1,7},{2,8},{3,9},{4,10},{5,11},{6,12},{7,13},{8,14},{9,15},... | collective-permute-start | bytes 786440 | tf_op jit(solution)/shard_map/ppermute | solution.py:320
  16.3 1.3 collective-permute-start.5
  17.6 4.8 %collective-permute-start.10 = (bf16[2,2,128,256]{3,2,1,0:T(8,128)(2,1)S(1)}, bf16[2,2,128,256]{3,2,1,0:T(8,128)(2,1)S(1)}, u32[]{:S(2)}, u32[]{:S(2)}) collective-permute-start(bf16[2,2,128,256]{3,2,1,0:T(8,128)(2,1)S(1)} %get-tuple-element.67.refs_0_), channel_id=1, source_target_pairs={{0,2},{1,3},{2,4},{3,5},{4,6},{5,7},{6,8},{7,9},{8,10},{9,11},{10,... | collective-permute-start | bytes 786440 | tf_op jit(solution)/shard_map/ppermute | solution.py:320
  22.4 0.0 collective-permute-done.3.refs_2_
  22.4 5.0 %collective-permute-start.11 = (bf16[2,2,128,256]{3,2,1,0:T(8,128)(2,1)S(1)}, bf16[2,2,128,256]{3,2,1,0:T(8,128)(2,1)S(1)}, u32[]{:S(2)}, u32[]{:S(2)}) collective-permute-start(bf16[2,2,128,256]{3,2,1,0:T(8,128)(2,1)S(1)} %get-tuple-element.67.refs_0_), channel_id=1, source_target_pairs={{0,4},{1,5},{2,6},{3,7},{4,8},{5,9},{6,10},{7,11},{8,12},{9,13},{1... | collective-permute-start | bytes 786440 | tf_op jit(solution)/shard_map/ppermute | solution.py:320
  27.4 0.0 collective-permute-done.4.refs_3_
  27.5 3.2 %collective-permute-start.12 = (bf16[2,2,128,256]{3,2,1,0:T(8,128)(2,1)S(1)}, bf16[2,2,128,256]{3,2,1,0:T(8,128)(2,1)S(1)}, u32[]{:S(2)}, u32[]{:S(2)}) collective-permute-start(bf16[2,2,128,256]{3,2,1,0:T(8,128)(2,1)S(1)} %get-tuple-element.67.refs_0_), channel_id=1, source_target_pairs={{0,6},{1,7},{2,8},{3,9},{4,10},{5,11},{6,12},{7,13},{8,14},{9,15},... | collective-permute-start | bytes 786440 | tf_op jit(solution)/shard_map/ppermute | solution.py:320
  30.7 1.3 collective-permute-start.13
  32.0 0.0 collective-permute-done.1.got
  32.0 18.9 %attend_1.1 = (bf16[2,1,128,4096]{3,2,1,0:T(8,128)(2,1)}, bf16[2,1,128,4096]{3,2,1,0:T(8,128)(2,1)}, bf16[2,2,128,2048]{3,2,1,0:T(8,128)(2,1)}, bf16[2,2,128,256...) custom-call(s32[2,1,4]{2,1,0:T(1,128)S(1)} %copy-done.5, ...), custom_call_target="tpu_custom_call" | custom-call | flops 28991029248 | bytes 9437184 | tf_op jit(solution)/shard_map/attend_1/pallas_call | solution.py:259
  50.9 9.4 %collective-permute-start.6 = (bf16[2,2,128,256]{3,2,1,0:T(8,128)(2,1)S(1)}, bf16[2,2,128,256]{3,2,1,0:T(8,128)(2,1)S(1)}, u32[]{:S(2)}, u32[]{:S(2)}) collective-permute-start(bf16[2,2,128,256]{3,2,1,0:T(8,128)(2,1)S(1)} %get-tuple-element.60), channel_id=1, source_target_pairs={{2,0},{3,1},{4,2},{5,3},{6,4},{7,5},{8,6},{9,7},{10,8},{11,9},{12,... | collective-permute-start | bytes 786440 | tf_op jit(solution)/shard_map/ppermute | solution.py:320
  60.3 0.0 collective-permute-done.10.refs_1_
  60.3 3.1 %collective-permute-start.7 = (bf16[2,2,128,256]{3,2,1,0:T(8,128)(2,1)S(1)}, bf16[2,2,128,256]{3,2,1,0:T(8,128)(2,1)S(1)}, u32[]{:S(2)}, u32[]{:S(2)}) collective-permute-start(bf16[2,2,128,256]{3,2,1,0:T(8,128)(2,1)S(1)} %get-tuple-element.61), channel_id=1, source_target_pairs={{4,0},{5,1},{6,2},{7,3},{8,4},{9,5},{10,6},{11,7},{12,8},{13,9},{1... | collective-permute-start | bytes 786440 | tf_op jit(solution)/shard_map/ppermute | solution.py:320
  63.4 0.0 collective-permute-done.11.refs_2_
  63.4 1.9 %collective-permute-start.8 = (bf16[2,2,128,256]{3,2,1,0:T(8,128)(2,1)S(1)}, bf16[2,2,128,256]{3,2,1,0:T(8,128)(2,1)S(1)}, u32[]{:S(2)}, u32[]{:S(2)}) collective-permute-start(bf16[2,2,128,256]{3,2,1,0:T(8,128)(2,1)S(1)} %get-tuple-element.62), channel_id=1, source_target_pairs={{6,0},{7,1},{8,2},{9,3},{10,4},{11,5},{12,6},{13,7},{14,8},{15,9},... | collective-permute-start | bytes 786440 | tf_op jit(solution)/shard_map/ppermute | solution.py:320
  65.3 1.3 collective-permute-start.9
  66.6 18.9 %attend_0.1 = (bf16[2,1,128,4096]{3,2,1,0:T(8,128)(2,1)}, bf16[2,1,128,4096]{3,2,1,0:T(8,128)(2,1)}, bf16[2,2,128,2048]{3,2,1,0:T(8,128)(2,1)}, bf16[2,2,128,256...) custom-call(s32[2,1,4]{2,1,0:T(1,128)S(1)} %copy-done.5, ...), custom_call_target="tpu_custom_call", output_to_operand_aliasing={{0}: (10, {}), {1}: (11, {}), {2}: (12, {})} | custom-call | flops 28991029248 | bytes 9437184 | tf_op jit(solution)/shard_map/attend_0/pallas_call | solution.py:259
  85.5 0.0 copy-start.2
  85.6 0.7 copy-done.2
  86.3 0.7 copy-done.3
  87.0 0.0 collective-permute-done.6
  87.0 4.0 %collective-permute-done.7 = bf16[2,2,128,256]{3,2,1,0:T(8,128)(2,1)S(1)} collective-permute-done((bf16[2,2,128,256]{3,2,1,0:T(8,128)(2,1)S(1)}, bf16[2,2,128,256]{3,2,1,0:T(8,128)(2,1)S(1)}, u32[]{:S(2)}, u32[]{:S(2)}) %collective-permute-start.7) | collective-permute-done | bytes 262176 | tf_op jit(solution)/shard_map/ppermute | solution.py:320
  91.0 1.3 collective-permute-done.9
  92.3 0.7 copy-done.9
  92.9 4.6 %collective-permute-start.18 = (bf16[2,2,128,2048]{3,2,1,0:T(8,128)(2,1)}, bf16[2,2,128,2048]{3,2,1,0:T(8,128)(2,1)S(1)}, u32[]{:S(2)}, u32[]{:S(2)}) collective-permute-start(bf16[2,2,128,2048]{3,2,1,0:T(8,128)(2,1)} %get-tuple-element.87), channel_id=1, source_target_pairs={{0,1},{1,0},{2,3},{3,2},{4,5},{5,4},{6,7},{7,6},{8,9},{9,8},{10,11... | collective-permute-start | bytes 6291464 | tf_op jit(solution)/shard_map/ppermute | solution.py:329
  97.5 1.9 %collective-permute-start.14 = (bf16[2,2,128,256]{3,2,1,0:T(8,128)(2,1)}, bf16[2,2,128,256]{3,2,1,0:T(8,128)(2,1)}, u32[]{:S(2)}, u32[]{:S(2)}) collective-permute-start(bf16[2,2,128,256]{3,2,1,0:T(8,128)(2,1)} %copy-done.3), channel_id=1, source_target_pairs={{2,0},{3,1},{4,2},{5,3},{6,4},{7,5},{8,6},{9,7},{10,8},{11,9},{12,... | collective-permute-start | bytes 786440 | tf_op jit(solution)/shard_map/ppermute | solution.py:320
  99.4 1.9 %collective-permute-start.15 = (bf16[2,2,128,256]{3,2,1,0:T(8,128)(2,1)}, bf16[2,2,128,256]{3,2,1,0:T(8,128)(2,1)}, u32[]{:S(2)}, u32[]{:S(2)}) collective-permute-start(bf16[2,2,128,256]{3,2,1,0:T(8,128)(2,1)} %copy-done.2), channel_id=1, source_target_pairs={{4,0},{5,1},{6,2},{7,3},{8,4},{9,5},{10,6},{11,7},{12,8},{13,9},{1... | collective-permute-start | bytes 786440 | tf_op jit(solution)/shard_map/ppermute | solution.py:320
  101.4 1.9 %collective-permute-start.16 = (bf16[2,2,128,256]{3,2,1,0:T(8,128)(2,1)S(1)}, bf16[2,2,128,256]{3,2,1,0:T(8,128)(2,1)}, u32[]{:S(2)}, u32[]{:S(2)}) collective-permute-start(bf16[2,2,128,256]{3,2,1,0:T(8,128)(2,1)S(1)} %get-tuple-element.84), channel_id=1, source_target_pairs={{6,0},{7,1},{8,2},{9,3},{10,4},{11,5},{12,6},{13,7},{14,8},{15,9},... | collective-permute-start | bytes 786440 | tf_op jit(solution)/shard_map/ppermute | solution.py:320
  103.3 1.3 collective-permute-start.17
  104.6 0.1 slice_reduce_fusion.1
  104.7 0.1 slice_reduce_fusion
  104.8 0.1 reshape.29
  104.9 0.1 compare_select_fusion
  104.9 9.3 %collective-permute-start.19 = (f32[32]{0:T(128)S(1)}, f32[32]{0:T(128)S(1)}, u32[]{:S(2)}, u32[]{:S(2)}) collective-permute-start(f32[32]{0:T(128)S(1)} %compare_select_fusion), channel_id=1, source_target_pairs={{0,112},{16,96},{32,80},{48,64},{64,48},{80,32},{96,16},{112,0},{1... | collective-permute-start | bytes 392 | tf_op jit(solution)/shard_map/ppermute | solution.py:384
  114.3 0.1 reshape.28
  114.4 6.9 %collective-permute-done.19 = f32[32]{0:T(128)S(1)} collective-permute-done((f32[32]{0:T(128)S(1)}, f32[32]{0:T(128)S(1)}, u32[]{:S(2)}, u32[]{:S(2)}) %collective-permute-start.19) | collective-permute-done | bytes 160 | tf_op jit(solution)/shard_map/ppermute | solution.py:384
  121.3 0.1 fusion.9
  121.4 4.0 %collective-permute-start.20 = (f32[32]{0:T(128)S(1)}, f32[32]{0:T(128)S(1)}, u32[]{:S(2)}, u32[]{:S(2)}) collective-permute-start(f32[32]{0:T(128)S(1)} %fusion.9), channel_id=1, source_target_pairs={{0,8},{1,9},{2,10},{3,11},{4,12},{5,13},{6,14},{7,15},{8,0},{9,1},... | collective-permute-start | bytes 392 | tf_op jit(solution)/shard_map/ppermute | solution.py:392
  125.3 1.4 add_convert_fusion.1
  126.7 6.7 %collective-permute-done.20 = f32[32]{0:T(128)S(1)} collective-permute-done((f32[32]{0:T(128)S(1)}, f32[32]{0:T(128)S(1)}, u32[]{:S(2)}, u32[]{:S(2)}) %collective-permute-start.20) | collective-permute-done | bytes 160 | tf_op jit(solution)/shard_map/ppermute | solution.py:392
  133.4 0.0 collective-permute-start.21
  133.4 1.5 slice_dynamic-update-slice_fusion
  134.9 1.3 collective-permute-done.21
  136.2 0.1 collective-permute-done.15
  136.3 1.4 fusion
  137.7 1.9 %collective-permute-start.22 = (bf16[2,2,128,256]{3,2,1,0:T(8,128)(2,1)S(1)}, bf16[2,2,128,256]{3,2,1,0:T(8,128)(2,1)S(1)}, u32[]{:S(2)}, u32[]{:S(2)}) collective-permute-start(bf16[2,2,128,256]{3,2,1,0:T(8,128)(2,1)S(1)} %fusion.5), channel_id=1, source_target_pairs={{0,1},{1,0},{2,3},{3,2},{4,5},{5,4},{6,7},{7,6},{8,9},{9,8},{10,11... | collective-permute-start | bytes 786440 | tf_op jit(solution)/shard_map/ppermute | solution.py:329
  139.6 3.9 %collective-permute-done.23 = f32[32]{0:T(128)S(1)} collective-permute-done((f32[32]{0:T(128)S(1)}, f32[32]{0:T(128)S(1)}, u32[]{:S(2)}, u32[]{:S(2)}) %collective-permute-start.23) | collective-permute-done | bytes 160 | tf_op jit(solution)/shard_map/ppermute | solution.py:392
  143.5 1.2 collective-permute-start.24
  144.8 0.8 collective-permute-done.24
  145.6 0.5 add_bitcast_fusion
  146.1 0.8 pad_maximum_fusion.1
  (33 shorter events, 0.3 us)
Async XLA Ops:
  1.8 1.9 %collective-permute-start = (bf16[2,2,128,256]{3,2,1,0:T(8,128)(2,1)S(1)}, bf16[2,2,128,256]{3,2,1,0:T(8,128)(2,1)S(1)}, u32[]{:S(2)}, u32[]{:S(2)}) collective-permute-start(bf16[2,2,128,256]{3,2,1,0:T(8,128)(2,1)S(1)} %pad_maximum_fusion.4), channel_id=1, source_target_pairs={{0,1},{1,0},{2,3},{3,2},{4,5},{5,4},{6,7},{7,6},{8,9},{9,8},{10,11... | collective-permute-start | bytes 786440 | tf_op jit(solution)/shard_map/ppermute | solution.py:329
  3.7 1.9 %copy-start = (bf16[2,1,128,4096]{3,2,1,0:T(8,128)(2,1)S(1)}, bf16[2,1,128,4096]{3,2,1,0:T(8,128)(2,1)}, u32[]{:S(2)}) copy-start(bf16[2,1,128,4096]{3,2,1,0:T(8,128)(2,1)} %q_own.3) | copy-start | bytes 6291460
  5.7 26.2 %copy-start.1 = (bf16[2,1,128,4096]{3,2,1,0:T(8,128)(2,1)S(1)}, bf16[2,1,128,4096]{3,2,1,0:T(8,128)(2,1)}, u32[]{:S(2)}) copy-start(bf16[2,1,128,4096]{3,2,1,0:T(8,128)(2,1)} %g_own.3) | copy-start | bytes 6291460
  5.8 26.2 %copy-start.4 = (f32[8,32]{1,0:T(8,128)S(1)}, f32[8,32]{1,0:T(8,128)}, u32[]{:S(2)}) copy-start(f32[8,32]{1,0:T(8,128)} %sink.3) | copy-start | bytes 3076
  5.8 26.2 %copy-start.5 = (s32[2,1,4]{2,1,0:T(1,128)S(1)}, s32[2,1,4]{2,1,0:T(1,128)}, u32[]{:S(2)}) copy-start(s32[2,1,4]{2,1,0:T(1,128)} %doc_tiles.3) | copy-start | bytes 100
  6.0 26.0 %collective-permute-start.1 = (bf16[2,2,128,2048]{3,2,1,0:T(8,128)(2,1)S(1)}, bf16[2,2,128,2048]{3,2,1,0:T(8,128)(2,1)S(1)}, u32[]{:S(2)}, u32[]{:S(2)}) collective-permute-start(bf16[2,2,128,2048]{3,2,1,0:T(8,128)(2,1)S(1)} %pad_maximum_fusion), channel_id=1, source_target_pairs={{0,1},{1,0},{2,3},{3,2},{4,5},{5,4},{6,7},{7,6},{8,9},{9,8},{10,11... | collective-permute-start | bytes 6291464 | tf_op jit(solution)/shard_map/ppermute | solution.py:329
  6.4 11.1 %collective-permute-start.2 = (bf16[2,2,128,256]{3,2,1,0:T(8,128)(2,1)S(1)}, bf16[2,2,128,256]{3,2,1,0:T(8,128)(2,1)S(1)}, u32[]{:S(2)}, u32[]{:S(2)}) collective-permute-start(bf16[2,2,128,256]{3,2,1,0:T(8,128)(2,1)S(1)} %get-tuple-element.59.refs_0_), channel_id=1, source_target_pairs={{0,2},{1,3},{2,4},{3,5},{4,6},{5,7},{6,8},{7,9},{8,10},{9,11},{10,... | collective-permute-start | bytes 786440 | tf_op jit(solution)/shard_map/ppermute | solution.py:320
  10.5 11.9 %collective-permute-start.3 = (bf16[2,2,128,256]{3,2,1,0:T(8,128)(2,1)S(1)}, bf16[2,2,128,256]{3,2,1,0:T(8,128)(2,1)S(1)}, u32[]{:S(2)}, u32[]{:S(2)}) collective-permute-start(bf16[2,2,128,256]{3,2,1,0:T(8,128)(2,1)S(1)} %get-tuple-element.59.refs_0_), channel_id=1, source_target_pairs={{0,4},{1,5},{2,6},{3,7},{4,8},{5,9},{6,10},{7,11},{8,12},{9,13},{1... | collective-permute-start | bytes 786440 | tf_op jit(solution)/shard_map/ppermute | solution.py:320
  13.4 14.0 %collective-permute-start.4 = (bf16[2,2,128,256]{3,2,1,0:T(8,128)(2,1)S(1)}, bf16[2,2,128,256]{3,2,1,0:T(8,128)(2,1)S(1)}, u32[]{:S(2)}, u32[]{:S(2)}) collective-permute-start(bf16[2,2,128,256]{3,2,1,0:T(8,128)(2,1)S(1)} %get-tuple-element.59.refs_0_), channel_id=1, source_target_pairs={{0,6},{1,7},{2,8},{3,9},{4,10},{5,11},{6,12},{7,13},{8,14},{9,15},... | collective-permute-start | bytes 786440 | tf_op jit(solution)/shard_map/ppermute | solution.py:320
  16.3 14.4 %collective-permute-start.5 = (bf16[2,2,128,256]{3,2,1,0:T(8,128)(2,1)S(1)}, bf16[2,2,128,256]{3,2,1,0:T(8,128)(2,1)S(1)}, u32[]{:S(2)}, u32[]{:S(2)}) collective-permute-start(bf16[2,2,128,256]{3,2,1,0:T(8,128)(2,1)S(1)} %get-tuple-element.59.refs_0_), channel_id=1, source_target_pairs={{0,8},{1,9},{2,10},{3,11},{4,12},{5,13},{6,14},{7,15},{16,24},{17,... | collective-permute-start | bytes 786440 | tf_op jit(solution)/shard_map/ppermute | solution.py:320
  17.6 42.7 %collective-permute-start.10 = (bf16[2,2,128,256]{3,2,1,0:T(8,128)(2,1)S(1)}, bf16[2,2,128,256]{3,2,1,0:T(8,128)(2,1)S(1)}, u32[]{:S(2)}, u32[]{:S(2)}) collective-permute-start(bf16[2,2,128,256]{3,2,1,0:T(8,128)(2,1)S(1)} %get-tuple-element.67.refs_0_), channel_id=1, source_target_pairs={{0,2},{1,3},{2,4},{3,5},{4,6},{5,7},{6,8},{7,9},{8,10},{9,11},{10,... | collective-permute-start | bytes 786440 | tf_op jit(solution)/shard_map/ppermute | solution.py:320
  22.4 41.0 %collective-permute-start.11 = (bf16[2,2,128,256]{3,2,1,0:T(8,128)(2,1)S(1)}, bf16[2,2,128,256]{3,2,1,0:T(8,128)(2,1)S(1)}, u32[]{:S(2)}, u32[]{:S(2)}) collective-permute-start(bf16[2,2,128,256]{3,2,1,0:T(8,128)(2,1)S(1)} %get-tuple-element.67.refs_0_), channel_id=1, source_target_pairs={{0,4},{1,5},{2,6},{3,7},{4,8},{5,9},{6,10},{7,11},{8,12},{9,13},{1... | collective-permute-start | bytes 786440 | tf_op jit(solution)/shard_map/ppermute | solution.py:320
  27.5 37.9 %collective-permute-start.12 = (bf16[2,2,128,256]{3,2,1,0:T(8,128)(2,1)S(1)}, bf16[2,2,128,256]{3,2,1,0:T(8,128)(2,1)S(1)}, u32[]{:S(2)}, u32[]{:S(2)}) collective-permute-start(bf16[2,2,128,256]{3,2,1,0:T(8,128)(2,1)S(1)} %get-tuple-element.67.refs_0_), channel_id=1, source_target_pairs={{0,6},{1,7},{2,8},{3,9},{4,10},{5,11},{6,12},{7,13},{8,14},{9,15},... | collective-permute-start | bytes 786440 | tf_op jit(solution)/shard_map/ppermute | solution.py:320
  30.7 36.0 %collective-permute-start.13 = (bf16[2,2,128,256]{3,2,1,0:T(8,128)(2,1)S(1)}, bf16[2,2,128,256]{3,2,1,0:T(8,128)(2,1)S(1)}, u32[]{:S(2)}, u32[]{:S(2)}) collective-permute-start(bf16[2,2,128,256]{3,2,1,0:T(8,128)(2,1)S(1)} %get-tuple-element.67.refs_0_), channel_id=1, source_target_pairs={{0,8},{1,9},{2,10},{3,11},{4,12},{5,13},{6,14},{7,15},{16,24},{17,... | collective-permute-start | bytes 786440 | tf_op jit(solution)/shard_map/ppermute | solution.py:320
  50.9 36.0 %collective-permute-start.6 = (bf16[2,2,128,256]{3,2,1,0:T(8,128)(2,1)S(1)}, bf16[2,2,128,256]{3,2,1,0:T(8,128)(2,1)S(1)}, u32[]{:S(2)}, u32[]{:S(2)}) collective-permute-start(bf16[2,2,128,256]{3,2,1,0:T(8,128)(2,1)S(1)} %get-tuple-element.60), channel_id=1, source_target_pairs={{2,0},{3,1},{4,2},{5,3},{6,4},{7,5},{8,6},{9,7},{10,8},{11,9},{12,... | collective-permute-start | bytes 786440 | tf_op jit(solution)/shard_map/ppermute | solution.py:320
  60.3 30.6 %collective-permute-start.7 = (bf16[2,2,128,256]{3,2,1,0:T(8,128)(2,1)S(1)}, bf16[2,2,128,256]{3,2,1,0:T(8,128)(2,1)S(1)}, u32[]{:S(2)}, u32[]{:S(2)}) collective-permute-start(bf16[2,2,128,256]{3,2,1,0:T(8,128)(2,1)S(1)} %get-tuple-element.61), channel_id=1, source_target_pairs={{4,0},{5,1},{6,2},{7,3},{8,4},{9,5},{10,6},{11,7},{12,8},{13,9},{1... | collective-permute-start | bytes 786440 | tf_op jit(solution)/shard_map/ppermute | solution.py:320
  63.4 27.6 %collective-permute-start.8 = (bf16[2,2,128,256]{3,2,1,0:T(8,128)(2,1)S(1)}, bf16[2,2,128,256]{3,2,1,0:T(8,128)(2,1)S(1)}, u32[]{:S(2)}, u32[]{:S(2)}) collective-permute-start(bf16[2,2,128,256]{3,2,1,0:T(8,128)(2,1)S(1)} %get-tuple-element.62), channel_id=1, source_target_pairs={{6,0},{7,1},{8,2},{9,3},{10,4},{11,5},{12,6},{13,7},{14,8},{15,9},... | collective-permute-start | bytes 786440 | tf_op jit(solution)/shard_map/ppermute | solution.py:320
  65.3 26.9 %collective-permute-start.9 = (bf16[2,2,128,256]{3,2,1,0:T(8,128)(2,1)S(1)}, bf16[2,2,128,256]{3,2,1,0:T(8,128)(2,1)S(1)}, u32[]{:S(2)}, u32[]{:S(2)}) collective-permute-start(bf16[2,2,128,256]{3,2,1,0:T(8,128)(2,1)S(1)} %get-tuple-element.63), channel_id=1, source_target_pairs={{8,0},{9,1},{10,2},{11,3},{12,4},{13,5},{14,6},{15,7},{24,16},{25,... | collective-permute-start | bytes 786440 | tf_op jit(solution)/shard_map/ppermute | solution.py:320
  85.5 0.7 copy-start.2
  86.3 0.7 copy-start.3
  87.0 5.3 %copy-start.6 = (bf16[2,2,128,256]{3,2,1,0:T(8,128)(2,1)}, bf16[2,2,128,256]{3,2,1,0:T(8,128)(2,1)S(1)}, u32[]{:S(2)}) copy-start(bf16[2,2,128,256]{3,2,1,0:T(8,128)(2,1)S(1)} %collective-permute-done.6) | copy-start | bytes 786436
  91.0 1.3 copy-start.7
  91.0 1.3 copy-start.8
  92.2 0.7 copy-start.9
  92.9 11.7 %collective-permute-start.18 = (bf16[2,2,128,2048]{3,2,1,0:T(8,128)(2,1)}, bf16[2,2,128,2048]{3,2,1,0:T(8,128)(2,1)S(1)}, u32[]{:S(2)}, u32[]{:S(2)}) collective-permute-start(bf16[2,2,128,2048]{3,2,1,0:T(8,128)(2,1)} %get-tuple-element.87), channel_id=1, source_target_pairs={{0,1},{1,0},{2,3},{3,2},{4,5},{5,4},{6,7},{7,6},{8,9},{9,8},{10,11... | collective-permute-start | bytes 6291464 | tf_op jit(solution)/shard_map/ppermute | solution.py:329
  97.5 38.7 %collective-permute-start.14 = (bf16[2,2,128,256]{3,2,1,0:T(8,128)(2,1)}, bf16[2,2,128,256]{3,2,1,0:T(8,128)(2,1)}, u32[]{:S(2)}, u32[]{:S(2)}) collective-permute-start(bf16[2,2,128,256]{3,2,1,0:T(8,128)(2,1)} %copy-done.3), channel_id=1, source_target_pairs={{2,0},{3,1},{4,2},{5,3},{6,4},{7,5},{8,6},{9,7},{10,8},{11,9},{12,... | collective-permute-start | bytes 786440 | tf_op jit(solution)/shard_map/ppermute | solution.py:320
  99.4 36.8 %collective-permute-start.15 = (bf16[2,2,128,256]{3,2,1,0:T(8,128)(2,1)}, bf16[2,2,128,256]{3,2,1,0:T(8,128)(2,1)}, u32[]{:S(2)}, u32[]{:S(2)}) collective-permute-start(bf16[2,2,128,256]{3,2,1,0:T(8,128)(2,1)} %copy-done.2), channel_id=1, source_target_pairs={{4,0},{5,1},{6,2},{7,3},{8,4},{9,5},{10,6},{11,7},{12,8},{13,9},{1... | collective-permute-start | bytes 786440 | tf_op jit(solution)/shard_map/ppermute | solution.py:320
  101.4 34.9 %collective-permute-start.16 = (bf16[2,2,128,256]{3,2,1,0:T(8,128)(2,1)S(1)}, bf16[2,2,128,256]{3,2,1,0:T(8,128)(2,1)}, u32[]{:S(2)}, u32[]{:S(2)}) collective-permute-start(bf16[2,2,128,256]{3,2,1,0:T(8,128)(2,1)S(1)} %get-tuple-element.84), channel_id=1, source_target_pairs={{6,0},{7,1},{8,2},{9,3},{10,4},{11,5},{12,6},{13,7},{14,8},{15,9},... | collective-permute-start | bytes 786440 | tf_op jit(solution)/shard_map/ppermute | solution.py:320
  103.3 33.0 %collective-permute-start.17 = (bf16[2,2,128,256]{3,2,1,0:T(8,128)(2,1)S(1)}, bf16[2,2,128,256]{3,2,1,0:T(8,128)(2,1)}, u32[]{:S(2)}, u32[]{:S(2)}) collective-permute-start(bf16[2,2,128,256]{3,2,1,0:T(8,128)(2,1)S(1)} %get-tuple-element.85), channel_id=1, source_target_pairs={{8,0},{9,1},{10,2},{11,3},{12,4},{13,5},{14,6},{15,7},{24,16},{25,... | collective-permute-start | bytes 786440 | tf_op jit(solution)/shard_map/ppermute | solution.py:320
  104.9 16.4 %collective-permute-start.19 = (f32[32]{0:T(128)S(1)}, f32[32]{0:T(128)S(1)}, u32[]{:S(2)}, u32[]{:S(2)}) collective-permute-start(f32[32]{0:T(128)S(1)} %compare_select_fusion), channel_id=1, source_target_pairs={{0,112},{16,96},{32,80},{48,64},{64,48},{80,32},{96,16},{112,0},{1... | collective-permute-start | bytes 392 | tf_op jit(solution)/shard_map/ppermute | solution.py:384
  121.4 12.0 %collective-permute-start.20 = (f32[32]{0:T(128)S(1)}, f32[32]{0:T(128)S(1)}, u32[]{:S(2)}, u32[]{:S(2)}) collective-permute-start(f32[32]{0:T(128)S(1)} %fusion.9), channel_id=1, source_target_pairs={{0,8},{1,9},{2,10},{3,11},{4,12},{5,13},{6,14},{7,15},{8,0},{9,1},... | collective-permute-start | bytes 392 | tf_op jit(solution)/shard_map/ppermute | solution.py:392
  133.4 2.8 %collective-permute-start.21 = (f32[32]{0:T(128)S(1)}, f32[32]{0:T(128)S(1)}, u32[]{:S(2)}, u32[]{:S(2)}) collective-permute-start(f32[32]{0:T(128)S(1)} %add.65), channel_id=1, source_target_pairs={{0,4},{1,5},{2,6},{3,7},{4,0},{5,1},{6,2},{7,3},{8,12},{9,13},{10,... | collective-permute-start | bytes 392 | tf_op jit(solution)/shard_map/ppermute | solution.py:392
  137.7 8.4 %collective-permute-start.22 = (bf16[2,2,128,256]{3,2,1,0:T(8,128)(2,1)S(1)}, bf16[2,2,128,256]{3,2,1,0:T(8,128)(2,1)S(1)}, u32[]{:S(2)}, u32[]{:S(2)}) collective-permute-start(bf16[2,2,128,256]{3,2,1,0:T(8,128)(2,1)S(1)} %fusion.5), channel_id=1, source_target_pairs={{0,1},{1,0},{2,3},{3,2},{4,5},{5,4},{6,7},{7,6},{8,9},{9,8},{10,11... | collective-permute-start | bytes 786440 | tf_op jit(solution)/shard_map/ppermute | solution.py:329
  139.6 3.9 %collective-permute-start.23 = (f32[32]{0:T(128)S(1)}, f32[32]{0:T(128)S(1)}, u32[]{:S(2)}, u32[]{:S(2)}) collective-permute-start(f32[32]{0:T(128)S(1)} %add.66), channel_id=1, source_target_pairs={{0,2},{1,3},{2,0},{3,1},{4,6},{5,7},{6,4},{7,5},{8,10},{9,11},{10,... | collective-permute-start | bytes 392 | tf_op jit(solution)/shard_map/ppermute | solution.py:392
  143.5 2.0 %collective-permute-start.24 = (f32[32]{0:T(128)S(1)}, f32[32]{0:T(128)S(1)}, u32[]{:S(2)}, u32[]{:S(2)}) collective-permute-start(f32[32]{0:T(128)S(1)} %add.77), channel_id=1, source_target_pairs={{0,1},{1,0},{2,3},{3,2},{4,5},{5,4},{6,7},{7,6},{8,9},{9,8},{10,11... | collective-permute-start | bytes 392 | tf_op jit(solution)/shard_map/ppermute | solution.py:392

commit v6 on v5

--- a/solution.py
+++ b/solution.py
@@ -47,10 +47,8 @@
     terms = refs[3 : REACH + 4]
     sink_part = refs[REACH + 4]
     q_in, g_in, o_out, dq_out, kv, grads, grads_low = refs[REACH + 5 : REACH + 12]
-    q_turned, g_turned, q_rows, g_rows, scores, shares, out_sum, dq_sum = refs[
-        REACH + 12 : REACH + 20
-    ]
-    q_sem, kv_sem, out_sem, grad_sem = refs[REACH + 20 :]
+    g_turned, q_rows, g_rows, scores, shares, out_sum, dq_sum = refs[REACH + 12 : REACH + 19]
+    q_sem, kv_sem, out_sem, grad_sem = refs[REACH + 19 :]
     step = pl.program_id(0)
     head = lax.div(step, 2)
     later = lax.rem(step, 2)
@@ -138,7 +136,6 @@
         q, g = q_in[step, :, part], g_in[step, :, part]
         q_rows[part, :] = q
         g_rows[part, :] = g
-        q_turned[:, part] = q.T
         g_turned[:, part] = g.T
 
     def tiles_of(which, group):
@@ -149,7 +146,7 @@
         return pl.ds(pl.multiple_of(group * GROUP * TILE, GROUP * TILE), GROUP * TILE)
 
     def scores_of(group):
-        score = dot(tiles_of(0, group), q_turned[...], 1, 0)
+        score = dot(tiles_of(0, group), q_rows[...], 1, 1)
         rows = [score[:TILE]]
         for i in range(1, GROUP):
             bias = jnp.where(GROUP * group + i < count, 0.0, HIDDEN).astype(jnp.float32)
@@ -278,7 +275,6 @@
             pltpu.VMEM((2, SLOTS, TILE, HEAD_WIDTH), jnp.float32),
             pltpu.VMEM((HEADS, 2, SLOTS, TILE, HEAD_WIDTH), low),
             pltpu.VMEM((HEAD_WIDTH, ROWS), low),
-            pltpu.VMEM((HEAD_WIDTH, ROWS), low),
             pltpu.VMEM((ROWS, HEAD_WIDTH), low),
             pltpu.VMEM((ROWS, HEAD_WIDTH), low),
             pltpu.VMEM((LONGEST * TILE, ROWS), jnp.float32),
@@ -386,18 +382,18 @@
         "section",
         [(s, section_count - 1 - s) for s in range(section_count)],
     )
-    for turn, distance in enumerate((8, 4, 2, 1)):
-        if turn == 2:
-            sent_second, sink_grad = lax.optimization_barrier((sent_second, sink_grad))
+    distance = 1
+    while distance < ctx_count:
         sink_grad = sink_grad + lax.ppermute(
             sink_grad, "ctx", [(c, c ^ distance) for c in range(ctx_count)]
         )
+        distance *= 2
     place = (0, 0, 0, mate * QUERY_PART)
     attention = lax.dynamic_update_slice(attention, out_got[:, :1], place)
     query_grad = lax.dynamic_update_slice(query_grad, out_got[:, 1:], place)
     first_sum = summed(terms_first, sent_first)
-    sent_second, first_sum, attention, query_grad = lax.optimization_barrier(
-        (sent_second, first_sum, attention, query_grad)
+    sent_second, sink_grad, first_sum, attention, query_grad = lax.optimization_barrier(
+        (sent_second, sink_grad, first_sum, attention, query_grad)
     )
     second_sum = summed(terms_second, sent_second)
     sums = jnp.stack([second_sum, first_sum])

time: 149 us -> 146 us (0.980)
  the two profiles are of different devices: /device:TPU:15 before, /device:TPU:1 now
where the time goes in v6:
time: 146 us; the launch traced here: 144 us
  starting transfers between devices  92.7 us (63%)
  Pallas kernels  23.5 us (16%)
  waiting for transfers between devices  14.9 us (10%)
  local copies, waits for them, and re-layouts  7.16 us (5%)
  other arithmetic  4.5 us (3%)
    ppermute x16, starting transfers between devices, shifted(): lax.ppermute(pieces[d + 1] if len(pieces) > 1 else pieces[0], 'ctx', [(a,...  39.7 us
    ppermute x4, starting transfers between devices, shards(): lax.ppermute(sink_grad, 'ctx', [(c, c ^ distance) for c in range(ctx_coun...  34.4 us
    pallas_call x2, Pallas kernels, attend(): pl.pallas_call(functools.partial(attend_kernel, relay, len(filled)), grid...  23.5 us
    ppermute x16, waiting for transfers between devices, shifted(): lax.ppermute(pieces[d + 1] if len(pieces) > 1 else pieces[0], 'ctx', [(a,...  10.4 us
    ppermute x4, starting transfers between devices, swapped(): return lax.ppermute(array, 'ctx', [(c, c ^ 1) for c in range(ctx_count)])  9.98 us
    ppermute x1, starting transfers between devices, shards(): lax.ppermute(sink_terms(sink_first), 'section', [(s, section_count - 1 -...  8.64 us
    ppermute x4, waiting for transfers between devices, swapped(): return lax.ppermute(array, 'ctx', [(c, c ^ 1) for c in range(ctx_count)])  3.65 us
  transfers between devices with their start and end apart: 25, of which 6 were waited for; matrix products, arithmetic and copies ran while one was open for 3% of the time, Pallas kernels for 16%

profile of v6, /device:TPU:1, one launch (start us, length us, event | category | flops | bytes accessed | tf_op | source)
XLA Modules:
  0.0 143.8 jit_solution(2763224148399474297)
XLA Ops:
  0.6 1.1 constant_dynamic-slice_fusion.2
  1.8 1.5 %collective-permute-start = (bf16[2,2,128,256]{3,2,1,0:T(8,128)(2,1)S(1)}, bf16[2,2,128,256]{3,2,1,0:T(8,128)(2,1)S(1)}, u32[]{:S(2)}, u32[]{:S(2)}) collective-permute-start(bf16[2,2,128,256]{3,2,1,0:T(8,128)(2,1)S(1)} %pad_maximum_fusion.4), channel_id=1, source_target_pairs={{0,1},{1,0},{2,3},{3,2},{4,5},{5,4},{6,7},{7,6},{8,9},{9,8},{10,11... | collective-permute-start | bytes 786440 | tf_op jit(solution)/shard_map/ppermute | solution.py:325
  3.3 1.2 collective-permute-done
  4.6 1.4 dynamic-slice_bitcast_fusion
  6.0 0.4 copy-done
  6.4 0.1 dynamic-slice_bitcast_fusion.1
  6.5 0.0 copy-start.1
  6.5 0.0 copy-start.4
  6.5 0.0 copy-start.5
  6.5 0.2 pad_maximum_fusion
  6.7 0.5 collective-permute-start.1
  7.2 4.7 %collective-permute-start.2 = (bf16[2,2,128,256]{3,2,1,0:T(8,128)(2,1)S(1)}, bf16[2,2,128,256]{3,2,1,0:T(8,128)(2,1)S(1)}, u32[]{:S(2)}, u32[]{:S(2)}) collective-permute-start(bf16[2,2,128,256]{3,2,1,0:T(8,128)(2,1)S(1)} %get-tuple-element.55.refs_0_), channel_id=1, source_target_pairs={{0,2},{1,3},{2,4},{3,5},{4,6},{5,7},{6,8},{7,9},{8,10},{9,11},{10,... | collective-permute-start | bytes 786440 | tf_op jit(solution)/shard_map/ppermute | solution.py:316
  11.9 3.2 %collective-permute-start.3 = (bf16[2,2,128,256]{3,2,1,0:T(8,128)(2,1)S(1)}, bf16[2,2,128,256]{3,2,1,0:T(8,128)(2,1)S(1)}, u32[]{:S(2)}, u32[]{:S(2)}) collective-permute-start(bf16[2,2,128,256]{3,2,1,0:T(8,128)(2,1)S(1)} %get-tuple-element.55.refs_0_), channel_id=1, source_target_pairs={{0,4},{1,5},{2,6},{3,7},{4,8},{5,9},{6,10},{7,11},{8,12},{9,13},{1... | collective-permute-start | bytes 786440 | tf_op jit(solution)/shard_map/ppermute | solution.py:316
  15.1 3.9 %collective-permute-start.4 = (bf16[2,2,128,256]{3,2,1,0:T(8,128)(2,1)S(1)}, bf16[2,2,128,256]{3,2,1,0:T(8,128)(2,1)S(1)}, u32[]{:S(2)}, u32[]{:S(2)}) collective-permute-start(bf16[2,2,128,256]{3,2,1,0:T(8,128)(2,1)S(1)} %get-tuple-element.55.refs_0_), channel_id=1, source_target_pairs={{0,6},{1,7},{2,8},{3,9},{4,10},{5,11},{6,12},{7,13},{8,14},{9,15},... | collective-permute-start | bytes 786440 | tf_op jit(solution)/shard_map/ppermute | solution.py:316
  19.0 2.6 %collective-permute-start.5 = (bf16[2,2,128,256]{3,2,1,0:T(8,128)(2,1)S(1)}, bf16[2,2,128,256]{3,2,1,0:T(8,128)(2,1)S(1)}, u32[]{:S(2)}, u32[]{:S(2)}) collective-permute-start(bf16[2,2,128,256]{3,2,1,0:T(8,128)(2,1)S(1)} %get-tuple-element.55.refs_0_), channel_id=1, source_target_pairs={{0,8},{1,9},{2,10},{3,11},{4,12},{5,13},{6,14},{7,15},{16,24},{17,... | collective-permute-start | bytes 786440 | tf_op jit(solution)/shard_map/ppermute | solution.py:316
  21.6 0.0 collective-permute-done.2.refs_1_
  21.6 4.0 %collective-permute-start.10 = (bf16[2,2,128,256]{3,2,1,0:T(8,128)(2,1)S(1)}, bf16[2,2,128,256]{3,2,1,0:T(8,128)(2,1)S(1)}, u32[]{:S(2)}, u32[]{:S(2)}) collective-permute-start(bf16[2,2,128,256]{3,2,1,0:T(8,128)(2,1)S(1)} %get-tuple-element.63.refs_0_), channel_id=1, source_target_pairs={{0,2},{1,3},{2,4},{3,5},{4,6},{5,7},{6,8},{7,9},{8,10},{9,11},{10,... | collective-permute-start | bytes 786440 | tf_op jit(solution)/shard_map/ppermute | solution.py:316
  25.6 10.1 %collective-permute-done.3.refs_2_ = bf16[2,2,128,256]{3,2,1,0:T(8,128)(2,1)S(1)} collective-permute-done((bf16[2,2,128,256]{3,2,1,0:T(8,128)(2,1)S(1)}, bf16[2,2,128,256]{3,2,1,0:T(8,128)(2,1)S(1)}, u32[]{:S(2)}, u32[]{:S(2)}) %collective-permute-start.3) | collective-permute-done | bytes 262176 | tf_op jit(solution)/shard_map/ppermute | solution.py:316
  35.7 4.1 %collective-permute-start.11 = (bf16[2,2,128,256]{3,2,1,0:T(8,128)(2,1)S(1)}, bf16[2,2,128,256]{3,2,1,0:T(8,128)(2,1)S(1)}, u32[]{:S(2)}, u32[]{:S(2)}) collective-permute-start(bf16[2,2,128,256]{3,2,1,0:T(8,128)(2,1)S(1)} %get-tuple-element.63.refs_0_), channel_id=1, source_target_pairs={{0,4},{1,5},{2,6},{3,7},{4,8},{5,9},{6,10},{7,11},{8,12},{9,13},{1... | collective-permute-start | bytes 786440 | tf_op jit(solution)/shard_map/ppermute | solution.py:316
  39.9 1.3 collective-permute-start.12
  41.2 0.2 collective-permute-done.5.refs_4_
  41.4 5.6 %collective-permute-start.13 = (bf16[2,2,128,256]{3,2,1,0:T(8,128)(2,1)S(1)}, bf16[2,2,128,256]{3,2,1,0:T(8,128)(2,1)S(1)}, u32[]{:S(2)}, u32[]{:S(2)}) collective-permute-start(bf16[2,2,128,256]{3,2,1,0:T(8,128)(2,1)S(1)} %get-tuple-element.63.refs_0_), channel_id=1, source_target_pairs={{0,8},{1,9},{2,10},{3,11},{4,12},{5,13},{6,14},{7,15},{16,24},{17,... | collective-permute-start | bytes 786440 | tf_op jit(solution)/shard_map/ppermute | solution.py:316
  47.0 0.0 collective-permute-done.1.got
  47.1 11.7 %attend_1.1 = (bf16[2,1,128,4096]{3,2,1,0:T(8,128)(2,1)}, bf16[2,1,128,4096]{3,2,1,0:T(8,128)(2,1)}, bf16[2,2,128,2048]{3,2,1,0:T(8,128)(2,1)}, bf16[2,2,128,256...) custom-call(s32[2,1,4]{2,1,0:T(1,128)S(1)} %copy-done.5, ...), custom_call_target="tpu_custom_call" | custom-call | flops 28991029248 | bytes 9437184 | tf_op jit(solution)/shard_map/attend_1/pallas_call | solution.py:256
  58.8 1.3 collective-permute-start.6
  60.1 1.3 collective-permute-start.7
  61.4 0.0 collective-permute-done.11.refs_2_
  61.4 1.3 collective-permute-start.8
  62.7 0.0 collective-permute-done.12.refs_3_
  62.7 1.3 collective-permute-start.9
  64.1 11.7 %attend_0.1 = (bf16[2,1,128,4096]{3,2,1,0:T(8,128)(2,1)}, bf16[2,1,128,4096]{3,2,1,0:T(8,128)(2,1)}, bf16[2,2,128,2048]{3,2,1,0:T(8,128)(2,1)}, bf16[2,2,128,256...) custom-call(s32[2,1,4]{2,1,0:T(1,128)S(1)} %copy-done.5, ...), custom_call_target="tpu_custom_call", output_to_operand_aliasing={{0}: (10, {}), {1}: (11, {}), {2}: (12, {})} | custom-call | flops 28991029248 | bytes 9437184 | tf_op jit(solution)/shard_map/attend_0/pallas_call | solution.py:256
  75.8 0.0 copy-start.2
  75.8 0.7 copy-done.2
  76.5 0.7 copy-done.3
  77.2 0.0 collective-permute-done.6
  77.3 0.7 copy-done.6
  77.9 0.1 copy-done.7
  78.0 0.1 copy-done.8
  78.1 0.1 copy-done.9
  78.2 6.8 %collective-permute-start.18 = (bf16[2,2,128,2048]{3,2,1,0:T(8,128)(2,1)}, bf16[2,2,128,2048]{3,2,1,0:T(8,128)(2,1)S(1)}, u32[]{:S(2)}, u32[]{:S(2)}) collective-permute-start(bf16[2,2,128,2048]{3,2,1,0:T(8,128)(2,1)} %get-tuple-element.83), channel_id=1, source_target_pairs={{0,1},{1,0},{2,3},{3,2},{4,5},{5,4},{6,7},{7,6},{8,9},{9,8},{10,11... | collective-permute-start | bytes 6291464 | tf_op jit(solution)/shard_map/ppermute | solution.py:325
  85.0 1.3 collective-permute-start.14
  86.3 1.3 collective-permute-start.15
  87.6 0.1 slice_reduce_fusion.1
  87.7 1.3 collective-permute-done.18
  89.0 0.1 slice_reduce_fusion
  89.1 0.1 reshape.29
  89.2 0.1 compare_select_fusion
  89.3 8.6 %collective-permute-start.19 = (f32[32]{0:T(128)S(1)}, f32[32]{0:T(128)S(1)}, u32[]{:S(2)}, u32[]{:S(2)}) collective-permute-start(f32[32]{0:T(128)S(1)} %compare_select_fusion), channel_id=1, source_target_pairs={{0,112},{16,96},{32,80},{48,64},{64,48},{80,32},{96,16},{112,0},{1... | collective-permute-start | bytes 392 | tf_op jit(solution)/shard_map/ppermute | solution.py:380
  98.0 0.1 reshape.28
  98.0 0.8 collective-permute-done.19
  98.9 0.1 fusion.9
  98.9 1.3 collective-permute-start.20
  100.2 1.3 collective-permute-start.16
  101.5 8.9 %collective-permute-start.21 = (f32[32]{0:T(128)S(1)}, f32[32]{0:T(128)S(1)}, u32[]{:S(2)}, u32[]{:S(2)}) collective-permute-start(f32[32]{0:T(128)S(1)} %add.65), channel_id=1, source_target_pairs={{0,2},{1,3},{2,0},{3,1},{4,6},{5,7},{6,4},{7,5},{8,10},{9,11},{10,... | collective-permute-start | bytes 392 | tf_op jit(solution)/shard_map/ppermute | solution.py:387
  110.4 1.3 collective-permute-start.17
  111.7 15.4 %collective-permute-start.22 = (f32[32]{0:T(128)S(1)}, f32[32]{0:T(128)S(1)}, u32[]{:S(2)}, u32[]{:S(2)}) collective-permute-start(f32[32]{0:T(128)S(1)} %add.66), channel_id=1, source_target_pairs={{0,4},{1,5},{2,6},{3,7},{4,0},{5,1},{6,2},{7,3},{8,12},{9,13},{10,... | collective-permute-start | bytes 392 | tf_op jit(solution)/shard_map/ppermute | solution.py:387
  127.1 1.4 add_convert_fusion.1
  128.5 8.8 %collective-permute-start.23 = (f32[32]{0:T(128)S(1)}, f32[32]{0:T(128)S(1)}, u32[]{:S(2)}, u32[]{:S(2)}) collective-permute-start(f32[32]{0:T(128)S(1)} %add.67), channel_id=1, source_target_pairs={{0,8},{1,9},{2,10},{3,11},{4,12},{5,13},{6,14},{7,15},{8,0},{9,1},... | collective-permute-start | bytes 392 | tf_op jit(solution)/shard_map/ppermute | solution.py:387
  137.3 1.4 %slice_dynamic-update-slice_fusion = (bf16[2,1,128,4096]{3,2,1,0:T(8,128)(2,1)}, bf16[2,1,128,4096]{3,2,1,0:T(8,128)(2,1)}) fusion(bf16[2,1,128,4096]{3,2,1,0:T(8,128)(2,1)} %get-tuple-element.93, s32[]{:T(128)S(6)} %select_n.61, bf16[2,2,128,2048]{3,2,1,0:T(8,128)(2,1)S(1)} %collective-permute-done.18, bf16[2,1,128,4096]{3,2,1,0:T(8,128)(2,1)} %get-tuple-element.91), kind=kLoop, calls=%fused_computation.1 | loop fusion | bytes 4194308 | tf_op jit(solution)/shard_map/dynamic_update_slice | solution.py:393
  138.8 0.5 add.68
  139.3 1.2 fusion
  140.6 1.2 collective-permute-start.24
  141.8 1.2 collective-permute-done.24
  143.0 0.8 pad_maximum_fusion.1
  (33 shorter events, 0.3 us)
Async XLA Ops:
  1.8 2.7 %collective-permute-start = (bf16[2,2,128,256]{3,2,1,0:T(8,128)(2,1)S(1)}, bf16[2,2,128,256]{3,2,1,0:T(8,128)(2,1)S(1)}, u32[]{:S(2)}, u32[]{:S(2)}) collective-permute-start(bf16[2,2,128,256]{3,2,1,0:T(8,128)(2,1)S(1)} %pad_maximum_fusion.4), channel_id=1, source_target_pairs={{0,1},{1,0},{2,3},{3,2},{4,5},{5,4},{6,7},{7,6},{8,9},{9,8},{10,11... | collective-permute-start | bytes 786440 | tf_op jit(solution)/shard_map/ppermute | solution.py:325
  4.5 1.9 %copy-start = (bf16[2,1,128,4096]{3,2,1,0:T(8,128)(2,1)S(1)}, bf16[2,1,128,4096]{3,2,1,0:T(8,128)(2,1)}, u32[]{:S(2)}) copy-start(bf16[2,1,128,4096]{3,2,1,0:T(8,128)(2,1)} %q_own.3) | copy-start | bytes 6291460
  6.5 40.5 %copy-start.1 = (bf16[2,1,128,4096]{3,2,1,0:T(8,128)(2,1)S(1)}, bf16[2,1,128,4096]{3,2,1,0:T(8,128)(2,1)}, u32[]{:S(2)}) copy-start(bf16[2,1,128,4096]{3,2,1,0:T(8,128)(2,1)} %g_own.3) | copy-start | bytes 6291460
  6.5 40.5 %copy-start.4 = (f32[8,32]{1,0:T(8,128)S(1)}, f32[8,32]{1,0:T(8,128)}, u32[]{:S(2)}) copy-start(f32[8,32]{1,0:T(8,128)} %sink.3) | copy-start | bytes 3076
  6.5 40.5 %copy-start.5 = (s32[2,1,4]{2,1,0:T(1,128)S(1)}, s32[2,1,4]{2,1,0:T(1,128)}, u32[]{:S(2)}) copy-start(s32[2,1,4]{2,1,0:T(1,128)} %doc_tiles.3) | copy-start | bytes 100
  6.7 40.3 %collective-permute-start.1 = (bf16[2,2,128,2048]{3,2,1,0:T(8,128)(2,1)S(1)}, bf16[2,2,128,2048]{3,2,1,0:T(8,128)(2,1)S(1)}, u32[]{:S(2)}, u32[]{:S(2)}) collective-permute-start(bf16[2,2,128,2048]{3,2,1,0:T(8,128)(2,1)S(1)} %pad_maximum_fusion), channel_id=1, source_target_pairs={{0,1},{1,0},{2,3},{3,2},{4,5},{5,4},{6,7},{7,6},{8,9},{9,8},{10,11... | collective-permute-start | bytes 6291464 | tf_op jit(solution)/shard_map/ppermute | solution.py:325
  7.2 14.4 %collective-permute-start.2 = (bf16[2,2,128,256]{3,2,1,0:T(8,128)(2,1)S(1)}, bf16[2,2,128,256]{3,2,1,0:T(8,128)(2,1)S(1)}, u32[]{:S(2)}, u32[]{:S(2)}) collective-permute-start(bf16[2,2,128,256]{3,2,1,0:T(8,128)(2,1)S(1)} %get-tuple-element.55.refs_0_), channel_id=1, source_target_pairs={{0,2},{1,3},{2,4},{3,5},{4,6},{5,7},{6,8},{7,9},{8,10},{9,11},{10,... | collective-permute-start | bytes 786440 | tf_op jit(solution)/shard_map/ppermute | solution.py:316
  11.9 23.8 %collective-permute-start.3 = (bf16[2,2,128,256]{3,2,1,0:T(8,128)(2,1)S(1)}, bf16[2,2,128,256]{3,2,1,0:T(8,128)(2,1)S(1)}, u32[]{:S(2)}, u32[]{:S(2)}) collective-permute-start(bf16[2,2,128,256]{3,2,1,0:T(8,128)(2,1)S(1)} %get-tuple-element.55.refs_0_), channel_id=1, source_target_pairs={{0,4},{1,5},{2,6},{3,7},{4,8},{5,9},{6,10},{7,11},{8,12},{9,13},{1... | collective-permute-start | bytes 786440 | tf_op jit(solution)/shard_map/ppermute | solution.py:316
  15.1 24.7 %collective-permute-start.4 = (bf16[2,2,128,256]{3,2,1,0:T(8,128)(2,1)S(1)}, bf16[2,2,128,256]{3,2,1,0:T(8,128)(2,1)S(1)}, u32[]{:S(2)}, u32[]{:S(2)}) collective-permute-start(bf16[2,2,128,256]{3,2,1,0:T(8,128)(2,1)S(1)} %get-tuple-element.55.refs_0_), channel_id=1, source_target_pairs={{0,6},{1,7},{2,8},{3,9},{4,10},{5,11},{6,12},{7,13},{8,14},{9,15},... | collective-permute-start | bytes 786440 | tf_op jit(solution)/shard_map/ppermute | solution.py:316
  19.0 22.4 %collective-permute-start.5 = (bf16[2,2,128,256]{3,2,1,0:T(8,128)(2,1)S(1)}, bf16[2,2,128,256]{3,2,1,0:T(8,128)(2,1)S(1)}, u32[]{:S(2)}, u32[]{:S(2)}) collective-permute-start(bf16[2,2,128,256]{3,2,1,0:T(8,128)(2,1)S(1)} %get-tuple-element.55.refs_0_), channel_id=1, source_target_pairs={{0,8},{1,9},{2,10},{3,11},{4,12},{5,13},{6,14},{7,15},{16,24},{17,... | collective-permute-start | bytes 786440 | tf_op jit(solution)/shard_map/ppermute | solution.py:316
  21.6 38.5 %collective-permute-start.10 = (bf16[2,2,128,256]{3,2,1,0:T(8,128)(2,1)S(1)}, bf16[2,2,128,256]{3,2,1,0:T(8,128)(2,1)S(1)}, u32[]{:S(2)}, u32[]{:S(2)}) collective-permute-start(bf16[2,2,128,256]{3,2,1,0:T(8,128)(2,1)S(1)} %get-tuple-element.63.refs_0_), channel_id=1, source_target_pairs={{0,2},{1,3},{2,4},{3,5},{4,6},{5,7},{6,8},{7,9},{8,10},{9,11},{10,... | collective-permute-start | bytes 786440 | tf_op jit(solution)/shard_map/ppermute | solution.py:316
  35.7 25.7 %collective-permute-start.11 = (bf16[2,2,128,256]{3,2,1,0:T(8,128)(2,1)S(1)}, bf16[2,2,128,256]{3,2,1,0:T(8,128)(2,1)S(1)}, u32[]{:S(2)}, u32[]{:S(2)}) collective-permute-start(bf16[2,2,128,256]{3,2,1,0:T(8,128)(2,1)S(1)} %get-tuple-element.63.refs_0_), channel_id=1, source_target_pairs={{0,4},{1,5},{2,6},{3,7},{4,8},{5,9},{6,10},{7,11},{8,12},{9,13},{1... | collective-permute-start | bytes 786440 | tf_op jit(solution)/shard_map/ppermute | solution.py:316
  39.9 22.9 %collective-permute-start.12 = (bf16[2,2,128,256]{3,2,1,0:T(8,128)(2,1)S(1)}, bf16[2,2,128,256]{3,2,1,0:T(8,128)(2,1)S(1)}, u32[]{:S(2)}, u32[]{:S(2)}) collective-permute-start(bf16[2,2,128,256]{3,2,1,0:T(8,128)(2,1)S(1)} %get-tuple-element.63.refs_0_), channel_id=1, source_target_pairs={{0,6},{1,7},{2,8},{3,9},{4,10},{5,11},{6,12},{7,13},{8,14},{9,15},... | collective-permute-start | bytes 786440 | tf_op jit(solution)/shard_map/ppermute | solution.py:316
  41.4 22.7 %collective-permute-start.13 = (bf16[2,2,128,256]{3,2,1,0:T(8,128)(2,1)S(1)}, bf16[2,2,128,256]{3,2,1,0:T(8,128)(2,1)S(1)}, u32[]{:S(2)}, u32[]{:S(2)}) collective-permute-start(bf16[2,2,128,256]{3,2,1,0:T(8,128)(2,1)S(1)} %get-tuple-element.63.refs_0_), channel_id=1, source_target_pairs={{0,8},{1,9},{2,10},{3,11},{4,12},{5,13},{6,14},{7,15},{16,24},{17,... | collective-permute-start | bytes 786440 | tf_op jit(solution)/shard_map/ppermute | solution.py:316
  58.8 18.4 %collective-permute-start.6 = (bf16[2,2,128,256]{3,2,1,0:T(8,128)(2,1)S(1)}, bf16[2,2,128,256]{3,2,1,0:T(8,128)(2,1)S(1)}, u32[]{:S(2)}, u32[]{:S(2)}) collective-permute-start(bf16[2,2,128,256]{3,2,1,0:T(8,128)(2,1)S(1)} %get-tuple-element.56), channel_id=1, source_target_pairs={{2,0},{3,1},{4,2},{5,3},{6,4},{7,5},{8,6},{9,7},{10,8},{11,9},{12,... | collective-permute-start | bytes 786440 | tf_op jit(solution)/shard_map/ppermute | solution.py:316
  60.1 17.1 %collective-permute-start.7 = (bf16[2,2,128,256]{3,2,1,0:T(8,128)(2,1)S(1)}, bf16[2,2,128,256]{3,2,1,0:T(8,128)(2,1)S(1)}, u32[]{:S(2)}, u32[]{:S(2)}) collective-permute-start(bf16[2,2,128,256]{3,2,1,0:T(8,128)(2,1)S(1)} %get-tuple-element.57), channel_id=1, source_target_pairs={{4,0},{5,1},{6,2},{7,3},{8,4},{9,5},{10,6},{11,7},{12,8},{13,9},{1... | collective-permute-start | bytes 786440 | tf_op jit(solution)/shard_map/ppermute | solution.py:316
  61.4 15.8 %collective-permute-start.8 = (bf16[2,2,128,256]{3,2,1,0:T(8,128)(2,1)S(1)}, bf16[2,2,128,256]{3,2,1,0:T(8,128)(2,1)S(1)}, u32[]{:S(2)}, u32[]{:S(2)}) collective-permute-start(bf16[2,2,128,256]{3,2,1,0:T(8,128)(2,1)S(1)} %get-tuple-element.58), channel_id=1, source_target_pairs={{6,0},{7,1},{8,2},{9,3},{10,4},{11,5},{12,6},{13,7},{14,8},{15,9},... | collective-permute-start | bytes 786440 | tf_op jit(solution)/shard_map/ppermute | solution.py:316
  62.7 14.5 %collective-permute-start.9 = (bf16[2,2,128,256]{3,2,1,0:T(8,128)(2,1)S(1)}, bf16[2,2,128,256]{3,2,1,0:T(8,128)(2,1)S(1)}, u32[]{:S(2)}, u32[]{:S(2)}) collective-permute-start(bf16[2,2,128,256]{3,2,1,0:T(8,128)(2,1)S(1)} %get-tuple-element.59), channel_id=1, source_target_pairs={{8,0},{9,1},{10,2},{11,3},{12,4},{13,5},{14,6},{15,7},{24,16},{25,... | collective-permute-start | bytes 786440 | tf_op jit(solution)/shard_map/ppermute | solution.py:316
  75.8 0.7 copy-start.2
  76.5 0.7 copy-start.3
  77.2 0.7 copy-start.6
  77.2 0.8 copy-start.7
  77.2 0.9 copy-start.8
  77.3 0.9 copy-start.9
  78.2 10.8 %collective-permute-start.18 = (bf16[2,2,128,2048]{3,2,1,0:T(8,128)(2,1)}, bf16[2,2,128,2048]{3,2,1,0:T(8,128)(2,1)S(1)}, u32[]{:S(2)}, u32[]{:S(2)}) collective-permute-start(bf16[2,2,128,2048]{3,2,1,0:T(8,128)(2,1)} %get-tuple-element.83), channel_id=1, source_target_pairs={{0,1},{1,0},{2,3},{3,2},{4,5},{5,4},{6,7},{7,6},{8,9},{9,8},{10,11... | collective-permute-start | bytes 6291464 | tf_op jit(solution)/shard_map/ppermute | solution.py:325
  85.0 54.3 %collective-permute-start.14 = (bf16[2,2,128,256]{3,2,1,0:T(8,128)(2,1)}, bf16[2,2,128,256]{3,2,1,0:T(8,128)(2,1)}, u32[]{:S(2)}, u32[]{:S(2)}) collective-permute-start(bf16[2,2,128,256]{3,2,1,0:T(8,128)(2,1)} %copy-done.3), channel_id=1, source_target_pairs={{2,0},{3,1},{4,2},{5,3},{6,4},{7,5},{8,6},{9,7},{10,8},{11,9},{12,... | collective-permute-start | bytes 786440 | tf_op jit(solution)/shard_map/ppermute | solution.py:316
  86.3 53.0 %collective-permute-start.15 = (bf16[2,2,128,256]{3,2,1,0:T(8,128)(2,1)}, bf16[2,2,128,256]{3,2,1,0:T(8,128)(2,1)}, u32[]{:S(2)}, u32[]{:S(2)}) collective-permute-start(bf16[2,2,128,256]{3,2,1,0:T(8,128)(2,1)} %copy-done.2), channel_id=1, source_target_pairs={{4,0},{5,1},{6,2},{7,3},{8,4},{9,5},{10,6},{11,7},{12,8},{13,9},{1... | collective-permute-start | bytes 786440 | tf_op jit(solution)/shard_map/ppermute | solution.py:316
  89.3 9.6 %collective-permute-start.19 = (f32[32]{0:T(128)S(1)}, f32[32]{0:T(128)S(1)}, u32[]{:S(2)}, u32[]{:S(2)}) collective-permute-start(f32[32]{0:T(128)S(1)} %compare_select_fusion), channel_id=1, source_target_pairs={{0,112},{16,96},{32,80},{48,64},{64,48},{80,32},{96,16},{112,0},{1... | collective-permute-start | bytes 392 | tf_op jit(solution)/shard_map/ppermute | solution.py:380
  98.9 2.5 %collective-permute-start.20 = (f32[32]{0:T(128)S(1)}, f32[32]{0:T(128)S(1)}, u32[]{:S(2)}, u32[]{:S(2)}) collective-permute-start(f32[32]{0:T(128)S(1)} %fusion.9), channel_id=1, source_target_pairs={{0,1},{1,0},{2,3},{3,2},{4,5},{5,4},{6,7},{7,6},{8,9},{9,8},{10,11... | collective-permute-start | bytes 392 | tf_op jit(solution)/shard_map/ppermute | solution.py:387
  100.2 39.1 %collective-permute-start.16 = (bf16[2,2,128,256]{3,2,1,0:T(8,128)(2,1)S(1)}, bf16[2,2,128,256]{3,2,1,0:T(8,128)(2,1)S(1)}, u32[]{:S(2)}, u32[]{:S(2)}) collective-permute-start(bf16[2,2,128,256]{3,2,1,0:T(8,128)(2,1)S(1)} %get-tuple-element.80), channel_id=1, source_target_pairs={{6,0},{7,1},{8,2},{9,3},{10,4},{11,5},{12,6},{13,7},{14,8},{15,9},... | collective-permute-start | bytes 786440 | tf_op jit(solution)/shard_map/ppermute | solution.py:316
  101.5 10.2 %collective-permute-start.21 = (f32[32]{0:T(128)S(1)}, f32[32]{0:T(128)S(1)}, u32[]{:S(2)}, u32[]{:S(2)}) collective-permute-start(f32[32]{0:T(128)S(1)} %add.65), channel_id=1, source_target_pairs={{0,2},{1,3},{2,0},{3,1},{4,6},{5,7},{6,4},{7,5},{8,10},{9,11},{10,... | collective-permute-start | bytes 392 | tf_op jit(solution)/shard_map/ppermute | solution.py:387
  110.4 28.9 %collective-permute-start.17 = (bf16[2,2,128,256]{3,2,1,0:T(8,128)(2,1)S(1)}, bf16[2,2,128,256]{3,2,1,0:T(8,128)(2,1)S(1)}, u32[]{:S(2)}, u32[]{:S(2)}) collective-permute-start(bf16[2,2,128,256]{3,2,1,0:T(8,128)(2,1)S(1)} %get-tuple-element.81), channel_id=1, source_target_pairs={{8,0},{9,1},{10,2},{11,3},{12,4},{13,5},{14,6},{15,7},{24,16},{25,... | collective-permute-start | bytes 786440 | tf_op jit(solution)/shard_map/ppermute | solution.py:316
  111.7 16.8 %collective-permute-start.22 = (f32[32]{0:T(128)S(1)}, f32[32]{0:T(128)S(1)}, u32[]{:S(2)}, u32[]{:S(2)}) collective-permute-start(f32[32]{0:T(128)S(1)} %add.66), channel_id=1, source_target_pairs={{0,4},{1,5},{2,6},{3,7},{4,0},{5,1},{6,2},{7,3},{8,12},{9,13},{10,... | collective-permute-start | bytes 392 | tf_op jit(solution)/shard_map/ppermute | solution.py:387
  128.5 10.3 %collective-permute-start.23 = (f32[32]{0:T(128)S(1)}, f32[32]{0:T(128)S(1)}, u32[]{:S(2)}, u32[]{:S(2)}) collective-permute-start(f32[32]{0:T(128)S(1)} %add.67), channel_id=1, source_target_pairs={{0,8},{1,9},{2,10},{3,11},{4,12},{5,13},{6,14},{7,15},{8,0},{9,1},... | collective-permute-start | bytes 392 | tf_op jit(solution)/shard_map/ppermute | solution.py:387
  140.6 2.3 %collective-permute-start.24 = (bf16[2,2,128,256]{3,2,1,0:T(8,128)(2,1)S(1)}, bf16[2,2,128,256]{3,2,1,0:T(8,128)(2,1)S(1)}, u32[]{:S(2)}, u32[]{:S(2)}) collective-permute-start(bf16[2,2,128,256]{3,2,1,0:T(8,128)(2,1)S(1)} %fusion.5), channel_id=1, source_target_pairs={{0,1},{1,0},{2,3},{3,2},{4,5},{5,4},{6,7},{7,6},{8,9},{9,8},{10,11... | collective-permute-start | bytes 786440 | tf_op jit(solution)/shard_map/ppermute | solution.py:325
